TPU v7x, 32 devices: a whole 2x2x4 slice. The times are simulated.
32 devices in a mesh: win: 8 (over z, core), seq: 4 (over y, x).
Axes of the slice: x: 2, y: 2, z: 4, core: 2. Of those that a mesh axis runs over, the one named last changes fastest.
Arguments:
- inputs: bfloat16 [8, 1536, 1536], P('win', 'seq'), may hold values from -6 to 6
- cotangent: bfloat16 [8, 1536, 1536], P('win', 'seq'), may hold values from -6 to 6
- ln1_scale: bfloat16 [1536], P(('win', 'seq')), may hold values from 0.5 to 1.5
- ln1_offset: bfloat16 [1536], P(('win', 'seq')), may hold values from -4 to 4
- w_query: bfloat16 [1536, 512], P(('win', 'seq')), may hold values from -0.15625 to 0.15625
- w_key: bfloat16 [1536, 512], P(('win', 'seq')), may hold values from -0.15625 to 0.15625
- w_value: bfloat16 [1536, 1536], P(('win', 'seq')), may hold values from -0.15625 to 0.15625
- w_rel: bfloat16 [192, 512], P(None, ('win', 'seq')), may hold values from -0.4375 to 0.4375
- content_bias: bfloat16 [512], P(('win', 'seq')), may hold values from -0.875 to 0.875
- position_bias: bfloat16 [512], P(('win', 'seq')), may hold values from -0.875 to 0.875
- w_out: bfloat16 [1536, 1536], P(('win', 'seq')), may hold values from -1.75 to 1.75
- b_out: bfloat16 [1536], P(('win', 'seq')), may hold values from -4 to 4
- ln2_scale: bfloat16 [1536], P(('win', 'seq')), may hold values from 0.5 to 1.5
- ln2_offset: bfloat16 [1536], P(('win', 'seq')), may hold values from -4 to 4
- w_in: bfloat16 [1536, 3072], P(('win', 'seq')), may hold values from -0.15625 to 0.15625
- b_in: bfloat16 [3072], P(('win', 'seq')), may hold values from -4 to 4
- w_mlp_out: bfloat16 [3072, 1536], P(('win', 'seq')), may hold values from -0.109375 to 0.109375
- b_mlp_out: bfloat16 [1536], P(('win', 'seq')), may hold values from -4 to 4
Outputs:
- layer_out: bfloat16 [8, 1536, 1536], P('win', 'seq')
- grad_inputs: float32 [8, 1536, 1536], P('win', 'seq')
- grad_ln1_scale: float32 [1536], P(('win', 'seq'))
- grad_ln1_offset: float32 [1536], P(('win', 'seq'))
- grad_w_query: float32 [1536, 512], P(('win', 'seq'))
- grad_w_key: float32 [1536, 512], P(('win', 'seq'))
- grad_w_value: float32 [1536, 1536], P(('win', 'seq'))
- grad_w_rel: float32 [192, 512], P(None, ('win', 'seq'))
- grad_content_bias: float32 [512], P(('win', 'seq'))
- grad_position_bias: float32 [512], P(('win', 'seq'))
- grad_w_out: float32 [1536, 1536], P(('win', 'seq'))
- grad_b_out: float32 [1536], P(('win', 'seq'))
- grad_ln2_scale: float32 [1536], P(('win', 'seq'))
- grad_ln2_offset: float32 [1536], P(('win', 'seq'))
- grad_w_in: float32 [1536, 3072], P(('win', 'seq'))
- grad_b_in: float32 [3072], P(('win', 'seq'))
- grad_w_mlp_out: float32 [3072, 1536], P(('win', 'seq'))
- grad_b_mlp_out: float32 [1536], P(('win', 'seq'))
All inputs are finite; a program needn't handle non-finite values.
Results may differ from a plain program's by a relative error of at most 0.03.
Values may be sent and summed in bfloat16 or wider, within the bound.
A program may use at most 256 MiB of HBM per device.

v0:
```python
import math

import jax
import jax.numpy as jnp
from jax import lax
from jax.sharding import PartitionSpec as P

HEADS = 8
KD = 64
F = 192
WLEN = 1536


def shifted(block, axis, distance):
    devices = range(lax.axis_size(axis))
    route = [((i - distance) % len(devices), i) for i in devices]
    return lax.ppermute(block, axis, route)


def rel_features(length, feature_count):
    per_basis = feature_count // 6
    offsets = jnp.arange(-length + 1, length).astype(jnp.float32)
    magnitude = jnp.abs(offsets)[:, None]
    half_life = 2.0 ** jnp.linspace(3.0, math.log2(length), per_basis)
    decaying = jnp.exp(-math.log(2.0) / half_life * magnitude)
    widths = 2.0 ** jnp.arange(1, per_basis + 1).astype(jnp.float32) - 1.0
    central = (widths > magnitude).astype(jnp.float32)
    stddev = length / (2.0 * per_basis)
    centers = jnp.linspace(length / per_basis, float(length), per_basis)
    shape_param = (centers / stddev) ** 2
    inverse_scale = centers / stddev**2
    peak_at = (shape_param - 1.0) / inverse_scale
    log_prob = (shape_param - 1.0) * (
        jnp.log(jnp.maximum(magnitude, 0.5)) - jnp.log(peak_at)
    ) - inverse_scale * (magnitude - peak_at)
    density = jnp.exp(log_prob) + 1e-08
    gamma_pdf = density / jnp.max(density, axis=0, keepdims=True)
    basis_set = jnp.concatenate([decaying, central, gamma_pdf], axis=1)
    return jnp.concatenate([basis_set, jnp.sign(offsets)[:, None] * basis_set], axis=1)


def layer_norm(values, norm_gain, norm_shift):
    centered = values - jnp.mean(values, axis=-1, keepdims=True)
    variance = jnp.mean(centered * centered, axis=-1, keepdims=True)
    return centered * lax.rsqrt(variance + 1e-05) * norm_gain + norm_shift


def shift_rows(relative, row_count, col_count):
    row_width = row_count + col_count - 1
    leading = relative.shape[:-2]
    flattened = relative.reshape(leading + (row_count * row_width,))
    trimmed = flattened[..., row_count - 1 : row_count - 1 + row_count * (row_width - 1)]
    return trimmed.reshape(leading + (row_count, row_width - 1))[..., :col_count]


def unshift_rows(gradient, row_count, col_count):
    row_width = row_count + col_count - 1
    leading = gradient.shape[:-2]
    padded = jnp.pad(gradient, [(0, 0)] * len(leading) + [(0, 0), (0, row_width - 1 - col_count)])
    flattened = padded.reshape(leading + (row_count * (row_width - 1),))
    flattened = jnp.pad(flattened, [(0, 0)] * len(leading) + [(row_count - 1, 1)])
    return flattened.reshape(leading + (row_count, row_width))


def shards(
    inputs,
    cotangent,
    ln1_scale,
    ln1_offset,
    w_query,
    w_key,
    w_value,
    w_rel,
    content_bias,
    position_bias,
    w_out,
    b_out,
    ln2_scale,
    ln2_offset,
    w_in,
    b_in,
    w_mlp_out,
    b_mlp_out,
):
    gathered = (
        lax.all_gather(ln1_scale, ("win", "seq"), axis=0, tiled=True),
        lax.all_gather(ln1_offset, ("win", "seq"), axis=0, tiled=True),
        lax.all_gather(w_query, ("win", "seq"), axis=0, tiled=True),
        lax.all_gather(w_key, ("win", "seq"), axis=0, tiled=True),
        lax.all_gather(w_value, ("win", "seq"), axis=0, tiled=True),
        lax.all_gather(w_rel, ("win", "seq"), axis=1, tiled=True),
        lax.all_gather(content_bias, ("win", "seq"), axis=0, tiled=True),
        lax.all_gather(position_bias, ("win", "seq"), axis=0, tiled=True),
        lax.all_gather(w_out, ("win", "seq"), axis=0, tiled=True),
        lax.all_gather(b_out, ("win", "seq"), axis=0, tiled=True),
        lax.all_gather(ln2_scale, ("win", "seq"), axis=0, tiled=True),
        lax.all_gather(ln2_offset, ("win", "seq"), axis=0, tiled=True),
        lax.all_gather(w_in, ("win", "seq"), axis=0, tiled=True),
        lax.all_gather(b_in, ("win", "seq"), axis=0, tiled=True),
        lax.all_gather(w_mlp_out, ("win", "seq"), axis=0, tiled=True),
        lax.all_gather(b_mlp_out, ("win", "seq"), axis=0, tiled=True),
    )
    (
        whole_ln1_scale,
        whole_ln1_offset,
        whole_w_query,
        whole_w_key,
        whole_w_value,
        whole_w_rel,
        whole_content_bias,
        whole_position_bias,
        whole_w_out,
        whole_b_out,
        whole_ln2_scale,
        whole_ln2_offset,
        whole_w_in,
        whole_b_in,
        whole_w_mlp_out,
        whole_b_mlp_out,
    ) = gathered
    window_count, row_count, model_width = inputs.shape
    key_width = HEADS * KD
    value_size = model_width // HEADS
    token_count = window_count * row_count
    scale_factor = KD ** (-0.5)
    query_start = lax.axis_index("seq") * row_count
    bfloat = jnp.bfloat16
    single = jnp.float32
    source = inputs.reshape(token_count, model_width).astype(single)
    normed_one_f, norm_one_back = jax.vjp(
        layer_norm, source, whole_ln1_scale.astype(single), whole_ln1_offset.astype(single)
    )
    normed_one = normed_one_f.astype(bfloat)
    features = rel_features(WLEN, F).astype(bfloat)
    table = (
        jnp.dot(features, whole_w_rel, preferred_element_type=single)
        .astype(bfloat)
        .reshape(2 * WLEN - 1, HEADS, KD)
    )
    query = jnp.dot(normed_one, whole_w_query, preferred_element_type=single) * scale_factor
    query_content = (
        (query + whole_content_bias.astype(single))
        .astype(bfloat)
        .reshape(window_count, row_count, HEADS, KD)
    )
    query_position = (
        (query + whole_position_bias.astype(single))
        .astype(bfloat)
        .reshape(window_count, row_count, HEADS, KD)
    )
    key_value_proj = jnp.dot(
        normed_one,
        jnp.concatenate([whole_w_key, whole_w_value], axis=1),
        preferred_element_type=single,
    ).astype(bfloat)
    keys = key_value_proj[:, :key_width].reshape(window_count, row_count, key_width)
    values_proj = key_value_proj[:, key_width:].reshape(window_count, row_count, model_width)

    def block_scores(key_piece, first_row):
        col_count = key_piece.shape[1]
        key_heads = key_piece.reshape(window_count, col_count, HEADS, KD)
        content = jnp.einsum(
            "wihk,wjhk->whij", query_content, key_heads, preferred_element_type=single
        )
        offset = first_row - query_start + (WLEN - row_count)
        span_rows = row_count + col_count - 1
        rel_rows = lax.dynamic_slice_in_dim(table, offset, span_rows, 0)
        relative = jnp.einsum(
            "wihk,chk->whic", query_position, rel_rows, preferred_element_type=single
        )
        return (content + shift_rows(relative, row_count, col_count), rel_rows, offset)

    running_max = jnp.full((window_count, HEADS, row_count), -1e30, single)
    scores = block_scores(lax.all_gather(keys, "seq", axis=1, tiled=True), jnp.int32(0))[0]
    new_max = jnp.maximum(running_max, jnp.max(scores, axis=-1))
    running_sum = jnp.sum(jnp.exp(scores - new_max[..., None]), axis=-1)
    running_max, running_sum = (new_max, running_sum)
    log_total = running_max + jnp.log(running_sum)
    key_piece = lax.all_gather(keys, "seq", axis=1, tiled=True)
    value_piece = lax.all_gather(values_proj, "seq", axis=1, tiled=True)
    col_count = key_piece.shape[1]
    scores = block_scores(key_piece, jnp.int32(0))[0]
    attention = jnp.exp(scores - log_total[..., None]).astype(bfloat)
    value_heads = value_piece.reshape(window_count, col_count, HEADS, value_size)
    mixed = jnp.einsum("whij,wjhd->wihd", attention, value_heads, preferred_element_type=single)
    attended = mixed.reshape(token_count, model_width).astype(bfloat)
    hidden_in = (
        source
        + jnp.dot(attended, whole_w_out, preferred_element_type=single)
        + whole_b_out.astype(single)
    )
    normed_two_f, norm_two_back = jax.vjp(
        layer_norm, hidden_in, whole_ln2_scale.astype(single), whole_ln2_offset.astype(single)
    )
    normed_two = normed_two_f.astype(bfloat)
    pre_act = jnp.dot(normed_two, whole_w_in, preferred_element_type=single) + whole_b_in.astype(
        single
    )
    gelu_out, gelu_back = jax.vjp(jax.nn.gelu, pre_act)
    activation = gelu_out.astype(bfloat)
    result = (
        hidden_in
        + jnp.dot(activation, whole_w_mlp_out, preferred_element_type=single)
        + whole_b_mlp_out.astype(single)
    )
    layer_out = result.astype(bfloat).reshape(window_count, row_count, model_width)
    cot_rows = cotangent.reshape(token_count, model_width)
    grad_w_mlp_out = jnp.einsum("tf,td->fd", activation, cot_rows, preferred_element_type=single)
    grad_b_mlp_out = jnp.sum(cot_rows.astype(single), axis=0)
    grad_act = jnp.einsum("td,fd->tf", cot_rows, whole_w_mlp_out, preferred_element_type=single)
    grad_pre = gelu_back(grad_act)[0].astype(bfloat)
    grad_w_in = jnp.einsum("td,tf->df", normed_two, grad_pre, preferred_element_type=single)
    grad_b_in = jnp.sum(grad_pre.astype(single), axis=0)
    grad_normed_two = jnp.einsum("tf,df->td", grad_pre, whole_w_in, preferred_element_type=single)
    hidden_term, grad_ln2_scale, grad_ln2_offset = norm_two_back(grad_normed_two)
    grad_hidden = cot_rows.astype(single) + hidden_term
    grad_branch = grad_hidden.astype(bfloat)
    grad_w_out = jnp.einsum("td,te->de", attended, grad_branch, preferred_element_type=single)
    grad_b_out = jnp.sum(grad_branch.astype(single), axis=0)
    grad_mixed = (
        jnp.einsum("te,de->td", grad_branch, whole_w_out, preferred_element_type=single)
        .astype(bfloat)
        .reshape(window_count, row_count, HEADS, value_size)
    )
    delta = jnp.transpose(jnp.sum(grad_mixed.astype(single) * mixed, axis=-1), (0, 2, 1))

    def pair_grads(key_piece, value_piece, first_row):
        col_count = key_piece.shape[1]
        span_rows = row_count + col_count - 1
        scores, rel_rows, offset = block_scores(key_piece, first_row)
        softmax_weights = jnp.exp(scores - log_total[..., None])
        value_heads = value_piece.reshape(window_count, col_count, HEADS, value_size)
        grad_weights = jnp.einsum(
            "wihd,wjhd->whij", grad_mixed, value_heads, preferred_element_type=single
        )
        grad_scores = (softmax_weights * (grad_weights - delta[..., None])).astype(bfloat)
        grad_vals = jnp.einsum(
            "whij,wihd->wjhd",
            softmax_weights.astype(bfloat),
            grad_mixed,
            preferred_element_type=single,
        ).reshape(window_count, col_count, model_width)
        key_heads = key_piece.reshape(window_count, col_count, HEADS, KD)
        grad_content = jnp.einsum(
            "whij,wjhk->wihk", grad_scores, key_heads, preferred_element_type=single
        )
        grad_keys = jnp.einsum(
            "whij,wihk->wjhk", grad_scores, query_content, preferred_element_type=single
        ).reshape(window_count, col_count, key_width)
        grad_relative = unshift_rows(grad_scores, row_count, col_count)
        grad_position = jnp.einsum(
            "whic,chk->wihk", grad_relative, rel_rows, preferred_element_type=single
        )
        grad_table = jnp.einsum(
            "whic,wihk->chk", grad_relative, query_position, preferred_element_type=single
        ).reshape(span_rows, key_width)
        feature_rows = lax.dynamic_slice_in_dim(features, offset, span_rows, 0).astype(single)
        grad_rel = jnp.dot(feature_rows.T, grad_table, precision=lax.Precision.HIGHEST)
        return (
            grad_content,
            grad_position,
            grad_rel,
            jnp.concatenate([grad_keys, grad_vals], axis=2),
        )

    key_pairs = jnp.concatenate([keys, values_proj], axis=2)
    zero_content = jnp.zeros((window_count, row_count, HEADS, KD), single)
    zero_rel = jnp.zeros((F, key_width), single)
    cycle_size = lax.axis_size("seq")

    def cycle_turn(cycle_step, carried):
        moving, moving_grads, grad_content, grad_position, grad_rel = carried
        owner = (lax.axis_index("seq") - cycle_step) % cycle_size
        pair_terms = pair_grads(moving[..., :key_width], moving[..., key_width:], owner * row_count)
        moving_grads = moving_grads + pair_terms[3]
        moving = shifted(moving, "seq", 1)
        moving_grads = shifted(moving_grads.astype(jnp.bfloat16), "seq", 1).astype(
            moving_grads.dtype
        )
        return (
            moving,
            moving_grads,
            grad_content + pair_terms[0],
            grad_position + pair_terms[1],
            grad_rel + pair_terms[2],
        )

    initial_cycle = (
        key_pairs,
        jnp.zeros(key_pairs.shape, single),
        zero_content,
        zero_content,
        zero_rel,
    )
    finished = lax.fori_loop(0, cycle_size, cycle_turn, initial_cycle)
    pair_grad_home, grad_content, grad_position, grad_rel_local = (
        finished[1],
        finished[2],
        finished[3],
        finished[4],
    )
    grad_content_bias = jnp.sum(grad_content, axis=(0, 1)).reshape(key_width)
    grad_position_bias = jnp.sum(grad_position, axis=(0, 1)).reshape(key_width)
    grad_query = (
        ((grad_content + grad_position) * scale_factor)
        .reshape(token_count, key_width)
        .astype(bfloat)
    )
    grad_keys_low = pair_grad_home[..., :key_width].reshape(token_count, key_width).astype(bfloat)
    grad_values_low = (
        pair_grad_home[..., key_width:].reshape(token_count, model_width).astype(bfloat)
    )
    grad_w_query = jnp.einsum("td,tk->dk", normed_one, grad_query, preferred_element_type=single)
    grad_w_key = jnp.einsum("td,tk->dk", normed_one, grad_keys_low, preferred_element_type=single)
    grad_w_value = jnp.einsum(
        "td,tk->dk", normed_one, grad_values_low, preferred_element_type=single
    )
    grad_normed_one = jnp.einsum(
        "tk,dk->td", grad_query, whole_w_query, preferred_element_type=single
    )
    grad_normed_one = grad_normed_one + jnp.einsum(
        "tk,dk->td", grad_keys_low, whole_w_key, preferred_element_type=single
    )
    grad_normed_one = grad_normed_one + jnp.einsum(
        "tk,dk->td", grad_values_low, whole_w_value, preferred_element_type=single
    )
    source_term, grad_ln1_scale, grad_ln1_offset = norm_one_back(grad_normed_one)
    grad_inputs = (grad_hidden + source_term).reshape(window_count, row_count, model_width)
    reduced = (
        lax.psum_scatter(grad_ln1_scale, ("win", "seq"), scatter_dimension=0, tiled=True),
        lax.psum_scatter(grad_ln1_offset, ("win", "seq"), scatter_dimension=0, tiled=True),
        lax.psum_scatter(grad_w_query, ("win", "seq"), scatter_dimension=0, tiled=True),
        lax.psum_scatter(grad_w_key, ("win", "seq"), scatter_dimension=0, tiled=True),
        lax.psum_scatter(grad_w_value, ("win", "seq"), scatter_dimension=0, tiled=True),
        lax.psum_scatter(grad_rel_local, ("win", "seq"), scatter_dimension=1, tiled=True),
        lax.psum_scatter(grad_content_bias, ("win", "seq"), scatter_dimension=0, tiled=True),
        lax.psum_scatter(grad_position_bias, ("win", "seq"), scatter_dimension=0, tiled=True),
        lax.psum_scatter(grad_w_out, ("win", "seq"), scatter_dimension=0, tiled=True),
        lax.psum_scatter(grad_b_out, ("win", "seq"), scatter_dimension=0, tiled=True),
        lax.psum_scatter(grad_ln2_scale, ("win", "seq"), scatter_dimension=0, tiled=True),
        lax.psum_scatter(grad_ln2_offset, ("win", "seq"), scatter_dimension=0, tiled=True),
        lax.psum_scatter(grad_w_in, ("win", "seq"), scatter_dimension=0, tiled=True),
        lax.psum_scatter(grad_b_in, ("win", "seq"), scatter_dimension=0, tiled=True),
        lax.psum_scatter(grad_w_mlp_out, ("win", "seq"), scatter_dimension=0, tiled=True),
        lax.psum_scatter(grad_b_mlp_out, ("win", "seq"), scatter_dimension=0, tiled=True),
    )
    return (layer_out, grad_inputs) + tuple(reduced)


def solution(mesh):
    in_specs = (
        P("win", "seq", None),
        P("win", "seq", None),
        P(("win", "seq")),
        P(("win", "seq")),
        P(("win", "seq"), None),
        P(("win", "seq"), None),
        P(("win", "seq"), None),
        P(None, ("win", "seq")),
        P(("win", "seq")),
        P(("win", "seq")),
        P(("win", "seq"), None),
        P(("win", "seq")),
        P(("win", "seq")),
        P(("win", "seq")),
        P(("win", "seq"), None),
        P(("win", "seq")),
        P(("win", "seq"), None),
        P(("win", "seq")),
    )
    out_specs = (
        P("win", "seq", None),
        P("win", "seq", None),
        P(("win", "seq")),
        P(("win", "seq")),
        P(("win", "seq"), None),
        P(("win", "seq"), None),
        P(("win", "seq"), None),
        P(None, ("win", "seq")),
        P(("win", "seq")),
        P(("win", "seq")),
        P(("win", "seq"), None),
        P(("win", "seq")),
        P(("win", "seq")),
        P(("win", "seq")),
        P(("win", "seq"), None),
        P(("win", "seq")),
        P(("win", "seq"), None),
        P(("win", "seq")),
    )
    return jax.shard_map(shards, mesh=mesh, in_specs=in_specs, out_specs=out_specs, check_vma=False)
```

profile of v0, /device:TPU:0, one launch (start us, length us, event | category | flops | bytes accessed | tf_op | source)
XLA Modules:
  0.0 2257.6 jit_solution(11208972238277447009)
XLA Ops:
  17.1 42.9 %all-reduce.21 = (bf16[1536]{0:T(1024)(128)(2,1)S(1)}, bf16[1536]{0:T(1024)(128)(2,1)S(1)}, bf16[512]{0:T(512)(128)(2,1)S(1)}, bf16[512]{0:T(512)(128)(2,1)S(1)}...) all-reduce(bf16[1536]{0:T(1024)(128)(2,1)S(1)} %dynamic-update-slic, ...), channel_id=1, replica_groups=mesh['win'=8,'seq'=4] {'win','seq'}, use_global_device_ids=true, to_apply=%add.3 | all-reduce | flops 13312 | bytes 53248
  69.0 65.0 %all-gather.13.cloned.1.call-done = bf16[1536,1536]{1,0:T(8,128)(2,1)} async-done(((bf16[48,1536]{1,0:T(8,128)(2,1)}), bf16[1536,1536]{1,0:T(8,128)(2,1)}) %all-gather.13.cloned.1.call-update) | async-done | bytes 4718608 | tf_op jit(solution)/shard_map/all_gather | solution.py:90
  148.8 68.5 %all_gather.63 = bf16[192,512]{0,1:T(8,128)(2,1)S(1)} all-gather(bf16[192,16]{0,1:T(8,128)(2,1)S(1)} %copy-done.60), channel_id=1, replica_groups=mesh['win'=8,'seq'=4] {'win','seq'}, dimensions={1}, use_global_device_ids=true | all-gather | bytes 202752 | tf_op jit(solution)/shard_map/all_gather | solution.py:91
  224.5 15.6 convolution_bitcast_fusion.2
  240.1 24.9 %copy.72 = f32[1,8,384,1919]{3,2,1,0:T(8,128)} copy(f32[1,8,384,1919]{2,3,1,0:T(8,128)} %convolution_bitcast_fusion.2) | data formatting | bytes 47161344 | tf_op jit(solution)/shard_map/wihk,chk->whic/transpose | solution.py:168
  265.0 35.5 %reshape.637 = f32[5895168]{0:T(1024)} reshape(f32[1,8,384,1919]{3,2,1,0:T(8,128)} %copy.72) | data formatting | bytes 47161344
  300.5 22.3 reshape.580
  322.8 18.8 slice.74
  341.6 17.6 reshape.639
  359.2 26.3 %reshape.581 = f32[1,8,384,1918]{3,2,1,0:T(8,128)} reshape(f32[5892096]{0:T(1024)} %reshape.639) | data formatting | bytes 47136768 | tf_op jit(solution)/shard_map/reshape | solution.py:53
  392.3 15.6 fusion.116
  423.9 13.0 bitcast_convert_fusion
  454.3 62.1 %all-gather.21.cloned.1.call-done = bf16[3072,1536]{1,0:T(8,128)(2,1)} async-done(((bf16[96,1536]{1,0:T(8,128)(2,1)}), bf16[3072,1536]{1,0:T(8,128)(2,1)}) %all-gather.21.cloned.1.call-update) | async-done | bytes 9437200 | tf_op jit(solution)/shard_map/all_gather | solution.py:100
  546.1 647.8 %while.24 = (s32[]{:T(128)}, bf16[1,384,2048]{1,2,0:T(8,128)(2,1)}, f32[1,384,2048]{1,2,0:T(8,128)}, f32[1,384,8,64]{1,3,2,0:T(8,128)}, f32[1,384,8,64]{1,3,2,0:...) while((s32[]{:T(128)}, bf16[1,384,2048]{1,2,0:T(8,128)(2,1)}, ...), condition=%wide.region_11.14_spmd.clone, body=%wide.region_10.13_spmd.clone.sunk | while | flops 3180527616 | bytes 325966848 | solution.py:295
  629.7 13.4 reshape.652
  683.8 11.5 reshape.655
  695.3 13.5 reshape.656
  785.4 13.4 reshape.652
  839.5 11.5 reshape.655
  851.0 13.5 reshape.656
  940.3 13.4 reshape.652
  1005.9 13.5 reshape.656
  1094.2 13.4 reshape.652
  1159.9 13.5 reshape.656
  1234.2 11.5 fusion.76
  1260.7 40.9 %all-reduce.20 = (f32[1536]{0:T(1024)S(1)}, f32[1536]{0:T(1024)S(1)}, f32[512]{0:T(512)S(1)}, f32[512]{0:T(512)S(1)}, f32[1536]{0:T(1024)S(1)}, /*index=5*/f32[1...) all-reduce(f32[1536]{0:T(1024)S(1)} %get-tuple-element.463, ...), channel_id=4, replica_groups=mesh['win'=8,'seq'=4] {'win','seq'}, use_global_device_ids=true, to_apply=%region_15.18.clone | all-reduce | flops 13312 | bytes 106496
  1328.5 104.4 %reduce-scatter.8.cloned.1.call-done = f32[48,512]{1,0:T(8,128)} async-done(((f32[1536,512]{1,0:T(8,128)}), f32[48,512]{1,0:T(8,128)}) %reduce-scatter.8.cloned.1.call-update) | async-done | bytes 98320 | tf_op jit(solution)/shard_map/reduce_scatter | solution.py:332
  1432.8 107.4 %reduce-scatter.10.cloned.1.call-done = f32[48,512]{1,0:T(8,128)} async-done(((f32[1536,512]{1,0:T(8,128)}), f32[48,512]{1,0:T(8,128)}) %reduce-scatter.10.cloned.1.call-update) | async-done | bytes 98320 | tf_op jit(solution)/shard_map/reduce_scatter | solution.py:333
  1540.3 141.9 %reduce-scatter.12.cloned.1.call-done = f32[48,1536]{1,0:T(8,128)} async-done(((f32[1536,1536]{1,0:T(8,128)}), f32[48,1536]{1,0:T(8,128)}) %reduce-scatter.12.cloned.1.call-update) | async-done | bytes 294928 | tf_op jit(solution)/shard_map/reduce_scatter | solution.py:334
  1682.2 141.1 %reduce-scatter.16.cloned.1.call-done = f32[48,1536]{1,0:T(8,128)} async-done(((f32[1536,1536]{1,0:T(8,128)}), f32[48,1536]{1,0:T(8,128)}) %reduce-scatter.16.cloned.1.call-update) | async-done | bytes 294928 | tf_op jit(solution)/shard_map/reduce_scatter | solution.py:338
  1823.3 213.7 %reduce-scatter.18.cloned.1.call-done = f32[48,3072]{1,0:T(8,128)} async-done(((f32[1536,3072]{1,0:T(8,128)}), f32[48,3072]{1,0:T(8,128)}) %reduce-scatter.18.cloned.1.call-update) | async-done | bytes 589840 | tf_op jit(solution)/shard_map/reduce_scatter | solution.py:342
  2037.1 213.8 %reduce-scatter.20.cloned.1.call-done = f32[96,1536]{1,0:T(8,128)} async-done(((f32[3072,1536]{1,0:T(8,128)}), f32[96,1536]{1,0:T(8,128)}) %reduce-scatter.20.cloned.1.call-update) | async-done | bytes 589840 | tf_op jit(solution)/shard_map/reduce_scatter | solution.py:344
  (473 shorter events, 677.9 us)
Async XLA Ops:
  7.2 61.8 %all-gather.11.cloned.1.call-start = ((), (), s32[]{:S(2)}) async-start(), calls=%async_computation.7 | async-start | bytes 1622016 | tf_op jit(solution)/shard_map/all_gather | solution.py:89
  7.9 126.2 %all-gather.13.cloned.1.call-start = ((), (), s32[]{:S(2)}) async-start(), calls=%async_computation.8 | async-start | bytes 4866048 | tf_op jit(solution)/shard_map/all_gather | solution.py:90
  8.7 213.3 %all-gather.15.cloned.1.call-start = ((), (), s32[]{:S(2)}) async-start(), calls=%async_computation.9 | async-start | bytes 1622016 | tf_op jit(solution)/shard_map/all_gather | solution.py:88
  9.4 380.3 %all-gather.25.cloned.1.call-start = ((), (), s32[]{:S(2)}) async-start(), calls=%async_computation.21 | async-start | bytes 1966080 | tf_op jit(solution)/shard_map/all_gather | solution.py:179
  60.0 162.0 %copy-start.48 = (f32[1536]{0:T(1024)}, f32[1536]{0:T(1024)S(1)}, u32[]{:S(2)}) copy-start(f32[1536]{0:T(1024)S(1)} %convert_element_type.221) | copy-start | bytes 18436
  60.0 162.0 %copy-start.35 = (f32[1536]{0:T(1024)}, f32[1536]{0:T(1024)S(1)}, u32[]{:S(2)}) copy-start(f32[1536]{0:T(1024)S(1)} %convert_element_type.220) | copy-start | bytes 18436
  61.5 160.5 %copy-start.40 = (f32[384]{0:T(512)}, f32[384]{0:T(512)S(1)}, u32[]{:S(2)}) copy-start(f32[384]{0:T(512)S(1)} %broadcast_multiply_fusion.1) | copy-start | bytes 4612
  62.0 77.6 %copy-start.54 = (f32[384]{0:T(512)}, f32[384]{0:T(512)S(1)}, u32[]{:S(2)}) copy-start(f32[384]{0:T(512)S(1)} %fusion.64) | copy-start | bytes 4612
  62.0 160.0 %copy-start.44 = (f32[384]{0:T(512)}, f32[384]{0:T(512)S(1)}, u32[]{:S(2)}) copy-start(f32[384]{0:T(512)S(1)} %fusion.94) | copy-start | bytes 4612
  141.7 275.3 %all-gather.23.cloned.1.call-start = ((), (), s32[]{:S(2)}) async-start(), calls=%async_computation.20 | async-start | bytes 5898240 | tf_op jit(solution)/shard_map/all_gather | solution.py:180
  144.2 292.6 %all-gather.17.cloned.1.call-start = ((), (), s32[]{:S(2)}) async-start(), calls=%async_computation.10 | async-start | bytes 4866048 | tf_op jit(solution)/shard_map/all_gather | solution.py:94
  144.8 298.9 %all-gather.19.cloned.1.call-start = ((), (), s32[]{:S(2)}) async-start(), calls=%async_computation.11 | async-start | bytes 9732096 | tf_op jit(solution)/shard_map/all_gather | solution.py:98
  145.6 370.9 %all-gather.21.cloned.1.call-start = ((), (), s32[]{:S(2)}) async-start(), calls=%async_computation.12 | async-start | bytes 9732096 | tf_op jit(solution)/shard_map/all_gather | solution.py:100
  146.3 1182.2 %reduce-scatter.14.cloned.1.call-start = ((), (), s32[]{:S(2)}) async-start(), calls=%async_computation.16 | async-start | bytes 540672 | tf_op jit(solution)/shard_map/reduce_scatter | solution.py:335
  441.9 93.3 %copy-start.43 = (f32[384]{0:T(512)}, f32[384]{0:T(512)S(1)}, u32[]{:S(2)}) copy-start(f32[384]{0:T(512)S(1)} %broadcast_multiply_fusion) | copy-start | bytes 4612
  443.7 91.5 %copy-start.47 = (f32[384]{0:T(512)}, f32[384]{0:T(512)S(1)}, u32[]{:S(2)}) copy-start(f32[384]{0:T(512)S(1)} %fusion.95) | copy-start | bytes 4612
  569.1 77.0 %copy-start.1 = (bf16[1,384,8,192]{1,3,2,0:T(8,128)(2,1)}, bf16[1,384,8,192]{1,3,2,0:T(8,128)(2,1)S(1)}, u32[]{:S(2)}) copy-start(bf16[1,384,8,192]{1,3,2,0:T(8,128)(2,1)S(1)} %get-tuple-element.696) | copy-start | bytes 3538948 | tf_op jit(solution)/shard_map/while
  653.3 65.5 %collective-permute-start.1 = (bf16[1,384,2048]{1,2,0:T(8,128)(2,1)}, bf16[1,384,2048]{1,2,0:T(8,128)(2,1)}, u32[]{:S(2)}, u32[]{:S(2)}) collective-permute-start(bf16[1,384,2048]{1,2,0:T(8,128)(2,1)} %fusion.197), channel_id=1, source_target_pairs={{3,0},{0,1},{1,2},{2,3},{7,4},{4,5},{5,6},{6,7},{11,8},{8,9},{9,10... | collective-permute-start | bytes 4718600 | tf_op jit(solution)/shard_map/while/body/eval_jaxpr/ppermute | solution.py:17
  654.7 70.1 %collective-permute-start = (bf16[1,384,2048]{1,2,0:T(8,128)(2,1)}, bf16[1,384,2048]{1,2,0:T(8,128)(2,1)}, u32[]{:S(2)}, u32[]{:S(2)}) collective-permute-start(bf16[1,384,2048]{1,2,0:T(8,128)(2,1)} %copy.98), channel_id=1, source_target_pairs={{3,0},{0,1},{1,2},{2,3},{7,4},{4,5},{5,6},{6,7},{11,8},{8,9},{9,10... | collective-permute-start | bytes 4718600 | tf_op jit(solution)/shard_map/while/body/eval_jaxpr/ppermute | solution.py:17
  808.9 65.5 %collective-permute-start.1 = (bf16[1,384,2048]{1,2,0:T(8,128)(2,1)}, bf16[1,384,2048]{1,2,0:T(8,128)(2,1)}, u32[]{:S(2)}, u32[]{:S(2)}) collective-permute-start(bf16[1,384,2048]{1,2,0:T(8,128)(2,1)} %fusion.197), channel_id=1, source_target_pairs={{3,0},{0,1},{1,2},{2,3},{7,4},{4,5},{5,6},{6,7},{11,8},{8,9},{9,10... | collective-permute-start | bytes 4718600 | tf_op jit(solution)/shard_map/while/body/eval_jaxpr/ppermute | solution.py:17
  809.5 70.1 %collective-permute-start = (bf16[1,384,2048]{1,2,0:T(8,128)(2,1)}, bf16[1,384,2048]{1,2,0:T(8,128)(2,1)}, u32[]{:S(2)}, u32[]{:S(2)}) collective-permute-start(bf16[1,384,2048]{1,2,0:T(8,128)(2,1)} %copy.98), channel_id=1, source_target_pairs={{3,0},{0,1},{1,2},{2,3},{7,4},{4,5},{5,6},{6,7},{11,8},{8,9},{9,10... | collective-permute-start | bytes 4718600 | tf_op jit(solution)/shard_map/while/body/eval_jaxpr/ppermute | solution.py:17
  963.8 65.5 %collective-permute-start.1 = (bf16[1,384,2048]{1,2,0:T(8,128)(2,1)}, bf16[1,384,2048]{1,2,0:T(8,128)(2,1)}, u32[]{:S(2)}, u32[]{:S(2)}) collective-permute-start(bf16[1,384,2048]{1,2,0:T(8,128)(2,1)} %fusion.197), channel_id=1, source_target_pairs={{3,0},{0,1},{1,2},{2,3},{7,4},{4,5},{5,6},{6,7},{11,8},{8,9},{9,10... | collective-permute-start | bytes 4718600 | tf_op jit(solution)/shard_map/while/body/eval_jaxpr/ppermute | solution.py:17
  963.8 69.7 %collective-permute-start = (bf16[1,384,2048]{1,2,0:T(8,128)(2,1)}, bf16[1,384,2048]{1,2,0:T(8,128)(2,1)}, u32[]{:S(2)}, u32[]{:S(2)}) collective-permute-start(bf16[1,384,2048]{1,2,0:T(8,128)(2,1)} %copy.98), channel_id=1, source_target_pairs={{3,0},{0,1},{1,2},{2,3},{7,4},{4,5},{5,6},{6,7},{11,8},{8,9},{9,10... | collective-permute-start | bytes 4718600 | tf_op jit(solution)/shard_map/while/body/eval_jaxpr/ppermute | solution.py:17
  1033.6 77.0 %copy-start.1 = (bf16[1,384,8,192]{1,3,2,0:T(8,128)(2,1)}, bf16[1,384,8,192]{1,3,2,0:T(8,128)(2,1)S(1)}, u32[]{:S(2)}) copy-start(bf16[1,384,8,192]{1,3,2,0:T(8,128)(2,1)S(1)} %get-tuple-element.696) | copy-start | bytes 3538948 | tf_op jit(solution)/shard_map/while
  1117.8 65.5 %collective-permute-start.1 = (bf16[1,384,2048]{1,2,0:T(8,128)(2,1)}, bf16[1,384,2048]{1,2,0:T(8,128)(2,1)}, u32[]{:S(2)}, u32[]{:S(2)}) collective-permute-start(bf16[1,384,2048]{1,2,0:T(8,128)(2,1)} %fusion.197), channel_id=1, source_target_pairs={{3,0},{0,1},{1,2},{2,3},{7,4},{4,5},{5,6},{6,7},{11,8},{8,9},{9,10... | collective-permute-start | bytes 4718600 | tf_op jit(solution)/shard_map/while/body/eval_jaxpr/ppermute | solution.py:17
  1117.8 69.1 %collective-permute-start = (bf16[1,384,2048]{1,2,0:T(8,128)(2,1)}, bf16[1,384,2048]{1,2,0:T(8,128)(2,1)}, u32[]{:S(2)}, u32[]{:S(2)}) collective-permute-start(bf16[1,384,2048]{1,2,0:T(8,128)(2,1)} %copy.98), channel_id=1, source_target_pairs={{3,0},{0,1},{1,2},{2,3},{7,4},{4,5},{5,6},{6,7},{11,8},{8,9},{9,10... | collective-permute-start | bytes 4718600 | tf_op jit(solution)/shard_map/while/body/eval_jaxpr/ppermute | solution.py:17
  1196.1 236.8 %reduce-scatter.8.cloned.1.call-start = ((), (), s32[]{:S(2)}) async-start(), calls=%async_computation.13 | async-start | bytes 3244032 | tf_op jit(solution)/shard_map/reduce_scatter | solution.py:332
  1201.3 339.0 %reduce-scatter.10.cloned.1.call-start = ((), (), s32[]{:S(2)}) async-start(), calls=%async_computation.14 | async-start | bytes 3244032 | tf_op jit(solution)/shard_map/reduce_scatter | solution.py:333
  1207.3 474.9 %reduce-scatter.12.cloned.1.call-start = ((), (), s32[]{:S(2)}) async-start(), calls=%async_computation.15 | async-start | bytes 9732096 | tf_op jit(solution)/shard_map/reduce_scatter | solution.py:334
  1214.2 609.1 %reduce-scatter.16.cloned.1.call-start = ((), (), s32[]{:S(2)}) async-start(), calls=%async_computation.17 | async-start | bytes 9732096 | tf_op jit(solution)/shard_map/reduce_scatter | solution.py:338
  1222.1 815.0 %reduce-scatter.18.cloned.1.call-start = ((), (), s32[]{:S(2)}) async-start(), calls=%async_computation.18 | async-start | bytes 19464192 | tf_op jit(solution)/shard_map/reduce_scatter | solution.py:342
  1234.2 1016.7 %reduce-scatter.20.cloned.1.call-start = ((), (), s32[]{:S(2)}) async-start(), calls=%async_computation.19 | async-start | bytes 19464192 | tf_op jit(solution)/shard_map/reduce_scatter | solution.py:344
  (104 other events, 1286.3 us)
Sparse Core Ops, SparseCore 0:
  10.9 58.0 all-gather.10
  71.9 62.1 all-gather.12
  137.0 54.0 all-gather.14
  193.3 30.1 all-gather.24
  225.8 56.9 all-gather.22
  285.5 63.5 all-gather.16
  352.0 80.8 all-gather.18
  435.8 80.6 all-gather.20
  1196.2 132.2 reduce-scatter.13
  1335.2 97.5 reduce-scatter.7
  1439.7 100.4 reduce-scatter.9
  1547.6 134.5 reduce-scatter.11
  1688.7 134.6 reduce-scatter.15
  1831.3 205.7 reduce-scatter.17
  2045.0 205.7 reduce-scatter.19
where the time goes:
time: 2270 us; the launch traced here: 2260 us
  waiting for transfers between devices  1080 us (48%)
  local copies, waits for them, and re-layouts  666 us (29%)
  matrix products  254 us (11%)
  blocking collectives  152 us (7%)
  other arithmetic  49.5 us (2%)
  loops' own time  31.3 us (1%)
    reduce_scatter x1, waiting for transfers between devices, shards(): lax.psum_scatter(grad_w_mlp_out, ('win', 'seq'), scatter_dimension=0, til...  214 us
    reduce_scatter x1, waiting for transfers between devices, shards(): lax.psum_scatter(grad_w_in, ('win', 'seq'), scatter_dimension=0, tiled=True)  214 us
    while x148, local copies, waits for them, and re-layouts  175 us
    reduce_scatter x1, waiting for transfers between devices, shards(): lax.psum_scatter(grad_w_value, ('win', 'seq'), scatter_dimension=0, tiled...  142 us
    reduce_scatter x1, waiting for transfers between devices, shards(): lax.psum_scatter(grad_w_out, ('win', 'seq'), scatter_dimension=0, tiled=T...  141 us
    reduce_scatter x1, waiting for transfers between devices, shards(): lax.psum_scatter(grad_w_key, ('win', 'seq'), scatter_dimension=0, tiled=T...  107 us
    reduce_scatter x1, waiting for transfers between devices, shards(): lax.psum_scatter(grad_w_query, ('win', 'seq'), scatter_dimension=0, tiled...  104 us
    unnamed x2, blocking collectives  83.7 us
  transfers between devices with their start and end apart: 23, of which 13 were waited for; matrix products, arithmetic and copies ran while one was open for 26% of the time, Pallas kernels for 0%

commit v1 on v0

v1 whole, which is shorter than its diff:
```python
import functools
import math

import jax
import jax.numpy as jnp
from jax import lax
from jax.experimental import pallas as pl
from jax.experimental.pallas import tpu as pltpu
from jax.sharding import PartitionSpec as P

HEADS = 8
KD = 64
F = 192
WLEN = 1536
CORES = 2
BLOCK_Q = 256
bfloat = jnp.bfloat16
single = jnp.float32


def rel_features(length, feature_count):
    per_basis = feature_count // 6
    offsets = jnp.arange(-length + 1, length).astype(jnp.float32)
    magnitude = jnp.abs(offsets)[:, None]
    half_life = 2.0 ** jnp.linspace(3.0, math.log2(length), per_basis)
    decaying = jnp.exp(-math.log(2.0) / half_life * magnitude)
    widths = 2.0 ** jnp.arange(1, per_basis + 1).astype(jnp.float32) - 1.0
    central = (widths > magnitude).astype(jnp.float32)
    stddev = length / (2.0 * per_basis)
    centers = jnp.linspace(length / per_basis, float(length), per_basis)
    shape_param = (centers / stddev) ** 2
    inverse_scale = centers / stddev**2
    peak_at = (shape_param - 1.0) / inverse_scale
    log_prob = (shape_param - 1.0) * (
        jnp.log(jnp.maximum(magnitude, 0.5)) - jnp.log(peak_at)
    ) - inverse_scale * (magnitude - peak_at)
    density = jnp.exp(log_prob) + 1e-08
    gamma_pdf = density / jnp.max(density, axis=0, keepdims=True)
    basis_set = jnp.concatenate([decaying, central, gamma_pdf], axis=1)
    return jnp.concatenate([basis_set, jnp.sign(offsets)[:, None] * basis_set], axis=1)


def layer_norm(values, norm_gain, norm_shift):
    centered = values - jnp.mean(values, axis=-1, keepdims=True)
    variance = jnp.mean(centered * centered, axis=-1, keepdims=True)
    return centered * lax.rsqrt(variance + 1e-05) * norm_gain + norm_shift


def fwd_kernel(L, bq, hp, vd, x_ref, tab_ref, att_ref, out_ref):
    qi = pl.program_id(0)
    hk = hp * KD
    i0 = pl.multiple_of(qi * bq, bq)
    a = pl.multiple_of(L - bq - i0, bq)
    W = L + bq
    outs = []
    for h in range(hp):
        qc = x_ref[pl.ds(i0, bq), pl.ds(h * KD, KD)]
        qp = x_ref[pl.ds(i0, bq), pl.ds(hk + h * KD, KD)]
        k = x_ref[:, pl.ds(2 * hk + h * KD, KD)]
        v = x_ref[:, pl.ds(3 * hk + h * vd, vd)]
        raw = jnp.dot(qp, tab_ref[pl.ds(h * KD, KD), pl.ds(a, W)], preferred_element_type=jnp.float32)
        rel = pltpu.roll(raw, W - bq + 1, 1, stride=1, stride_axis=0)[:, :L]
        s = rel + lax.dot_general(qc, k, (((1,), (1,)), ((), ())), preferred_element_type=jnp.float32)
        m = jnp.max(s, axis=-1, keepdims=True)
        e = jnp.exp(s - m)
        inv = 1.0 / jnp.sum(e, axis=-1, keepdims=True)
        att = (e * inv).astype(jnp.bfloat16)
        att_ref[h] = att
        outs.append(jnp.dot(att, v, preferred_element_type=jnp.float32).astype(jnp.bfloat16))
    out_ref[...] = jnp.concatenate(outs, axis=1) if hp > 1 else outs[0]

def attention_forward(x, tab, hp, vd, bq):
    L = x.shape[0]
    return pl.pallas_call(
        functools.partial(fwd_kernel, L, bq, hp, vd),
        grid=(L // bq,),
        in_specs=[pl.BlockSpec(x.shape, lambda i: (0, 0)), pl.BlockSpec(tab.shape, lambda i: (0, 0))],
        out_specs=[pl.BlockSpec((hp, bq, L), lambda i: (0, i, 0)), pl.BlockSpec((bq, hp * vd), lambda i: (i, 0))],
        out_shape=[jax.ShapeDtypeStruct((hp, L, L), jnp.bfloat16), jax.ShapeDtypeStruct((L, hp * vd), jnp.bfloat16)],
        compiler_params=pltpu.CompilerParams(vmem_limit_bytes=56 * 2**20),
    )(x, tab)

def bwd_kernel(L, bq, hp, vd, x_ref, tab_ref, att_ref, gm_ref, dq_ref, dkv_ref, dtab_ref, bias_ref, dkT, dvT):
    qi = pl.program_id(0)
    hk = hp * KD
    i0 = pl.multiple_of(qi * bq, bq)
    a = pl.multiple_of(L - bq - i0, bq)
    W = L + bq

    @pl.when(qi == 0)
    def _():
        dkT[...] = jnp.zeros_like(dkT)
        dvT[...] = jnp.zeros_like(dvT)
        dtab_ref[...] = jnp.zeros_like(dtab_ref)
        bias_ref[...] = jnp.zeros_like(bias_ref)

    row = lax.broadcasted_iota(jnp.int32, (bq, bq), 0)
    col = lax.broadcasted_iota(jnp.int32, (bq, bq), 1)
    flip = jnp.where(row + col == bq - 1, 1.0, 0.0).astype(jnp.bfloat16)

    def flipped(v):
        return jnp.dot(flip, v, preferred_element_type=jnp.float32)

    dqs, bc, bp = [], [], []
    for h in range(hp):
        qc = flipped(x_ref[pl.ds(i0, bq), pl.ds(h * KD, KD)]).astype(jnp.bfloat16)
        qp = flipped(x_ref[pl.ds(i0, bq), pl.ds(hk + h * KD, KD)]).astype(jnp.bfloat16)
        k = x_ref[:, pl.ds(2 * hk + h * KD, KD)]
        v = x_ref[:, pl.ds(3 * hk + h * vd, vd)]
        gm = gm_ref[:, pl.ds(h * vd, vd)]
        att = att_ref[h]
        dvT[pl.ds(h * vd, vd), :] += lax.dot_general(gm, att, (((0,), (0,)), ((), ())), preferred_element_type=jnp.float32)
        gmr = flipped(gm).astype(jnp.bfloat16)
        dp = lax.dot_general(gmr, v, (((1,), (1,)), ((), ())), preferred_element_type=jnp.float32)
        af = flipped(att)
        t = af * dp
        delta = jnp.sum(t, axis=-1, keepdims=True)
        ds = (t - af * delta).astype(jnp.bfloat16)
        dkT[pl.ds(h * KD, KD), :] += lax.dot_general(qc, ds, (((0,), (0,)), ((), ())), preferred_element_type=jnp.float32)
        gc = jnp.dot(ds, k, preferred_element_type=jnp.float32)
        wide = jnp.concatenate([ds.astype(jnp.float32), jnp.zeros((bq, bq), jnp.float32)], axis=1)
        rel = pltpu.roll(wide, 0, 1, stride=1, stride_axis=0).astype(jnp.bfloat16)
        tab = tab_ref[pl.ds(h * KD, KD), pl.ds(a, W)]
        gp = lax.dot_general(rel, tab, (((1,), (1,)), ((), ())), preferred_element_type=jnp.float32)
        dtab_ref[pl.ds(h * KD, KD), pl.ds(a, W)] += lax.dot_general(qp, rel, (((0,), (0,)), ((), ())), preferred_element_type=jnp.float32)
        dqs.append(flipped(((gc + gp) * KD ** -0.5).astype(jnp.bfloat16)).astype(jnp.bfloat16))
        bc.append(jnp.sum(gc, axis=0, keepdims=True))
        bp.append(jnp.sum(gp, axis=0, keepdims=True))
    dq_ref[...] = jnp.concatenate(dqs, axis=1) if hp > 1 else dqs[0]
    bias_ref[0:1, :] += jnp.concatenate(bc, axis=1) if hp > 1 else bc[0]
    bias_ref[1:2, :] += jnp.concatenate(bp, axis=1) if hp > 1 else bp[0]

    @pl.when(qi == pl.num_programs(0) - 1)
    def _():
        dkv_ref[:, :hk] = dkT[...].T.astype(jnp.bfloat16)
        dkv_ref[:, hk:] = dvT[...].T.astype(jnp.bfloat16)

def attention_backward(x, tab, att, gm, hp, vd, bq):
    L = x.shape[0]
    hk = hp * KD
    return pl.pallas_call(
        functools.partial(bwd_kernel, L, bq, hp, vd),
        grid=(L // bq,),
        in_specs=[pl.BlockSpec(x.shape, lambda i: (0, 0)), pl.BlockSpec(tab.shape, lambda i: (0, 0)),
                  pl.BlockSpec((hp, bq, L), lambda i: (0, i, 0)), pl.BlockSpec((bq, hp * vd), lambda i: (i, 0))],
        out_specs=[pl.BlockSpec((bq, hk), lambda i: (i, 0)), pl.BlockSpec((L, hk + hp * vd), lambda i: (0, 0)),
                   pl.BlockSpec(tab.shape, lambda i: (0, 0)), pl.BlockSpec((8, hk), lambda i: (0, 0))],
        out_shape=[jax.ShapeDtypeStruct((L, hk), jnp.bfloat16), jax.ShapeDtypeStruct((L, hk + hp * vd), jnp.bfloat16),
                   jax.ShapeDtypeStruct(tab.shape, jnp.float32), jax.ShapeDtypeStruct((8, hk), jnp.float32)],
        scratch_shapes=[pltpu.VMEM((hk, L), jnp.float32), pltpu.VMEM((hp * vd, L), jnp.float32)],
        compiler_params=pltpu.CompilerParams(vmem_limit_bytes=56 * 2**20),
    )(x, tab, att, gm)


def pick(stacked, index, axis):
    return lax.dynamic_index_in_dim(stacked, index, axis, keepdims=False)


def place(stacked, piece, index, axis):
    return lax.dynamic_update_slice_in_dim(stacked, jnp.expand_dims(piece, axis), index, axis)


def swap_cores(value):
    size = lax.axis_size("win")
    return lax.ppermute(value, "win", [(i, i ^ 1) for i in range(size)])


def swap_seq(value, distance):
    size = lax.axis_size("seq")
    return lax.ppermute(value, "seq", [(i, i ^ distance) for i in range(size)])


def move_chips(value, direction, first):
    size = lax.axis_size("win")
    chips = size // CORES
    if direction > 0:
        pairs = [(i, i + CORES) for i in range(size - CORES) if i // CORES >= first]
    else:
        pairs = [(i, i - CORES) for i in range(CORES, size) if i // CORES < chips - first]
    return lax.ppermute(value, "win", pairs)


def gather_chips(shard):
    chips = lax.axis_size("win") // CORES
    here = lax.axis_index("win") // CORES
    out = place(jnp.zeros((chips,) + shard.shape, shard.dtype), shard, here, 0)
    above, below = [shard], [shard]
    for step in range(1, chips):
        below.append(move_chips(below[-1], 1, step - 1))
        above.append(move_chips(above[-1], -1, step - 1))
    for step in range(1, chips):
        piece = jnp.where(here + step < chips, above[step], below[chips - step])
        out = place(out, piece, (here + step) % chips, 0)
    return out


def gather_seq(value, axis, rising):
    size = lax.axis_size("seq")
    here = lax.axis_index("seq")
    bits = [1 << b for b in range(size.bit_length() - 1)]
    shape = value.shape
    lead, tail = shape[:axis], shape[axis:]
    value = value.reshape(lead + (1,) * len(bits) + tail)
    for bit in bits if rising else bits[::-1]:
        at = axis + len(bits) - bit.bit_length()
        other = swap_seq(value, bit)
        own_low = (here & bit) == 0
        value = jnp.concatenate(
            [jnp.where(own_low, value, other), jnp.where(own_low, other, value)], axis=at
        )
    return value.reshape(lead + (size,) + tail)


def gather_cores(value, axis):
    other = swap_cores(value)
    first = lax.axis_index("win") % CORES == 0
    return jnp.stack([jnp.where(first, value, other), jnp.where(first, other, value)], axis=axis)


def gather(shard, rising):
    value = gather_chips(shard)
    value = gather_seq(value, 1, rising)
    return gather_cores(value, 1)


def total(first, *others):
    result = first.astype(single)
    for other in others:
        result = result + other.astype(single)
    return result


def scatter_cores(value, axis):
    core = lax.axis_index("win") % CORES
    arrived = swap_cores(pick(value, 1 - core, axis))
    return total(pick(value, core, axis), arrived).astype(value.dtype)


def scatter_seq(value, axis, rising):
    size = lax.axis_size("seq")
    here = lax.axis_index("seq")
    bits = [1 << b for b in range(size.bit_length() - 1)]
    shape = value.shape
    lead, tail = shape[:axis], shape[axis + 1 :]
    value = value.reshape(lead + (2,) * len(bits) + tail)
    for bit in bits[::-1] if rising else bits:
        at = axis + len(bits) - bit.bit_length()
        mine = (here & bit) // bit
        arrived = swap_seq(lax.dynamic_slice_in_dim(value, 1 - mine, 1, at), bit)
        value = total(lax.dynamic_slice_in_dim(value, mine, 1, at), arrived).astype(value.dtype)
    return value.reshape(lead + tail)


def scatter_chips(value):
    chips = lax.axis_size("win") // CORES
    here = lax.axis_index("win") // CORES
    from_below = from_above = None
    for step in range(chips - 1, 0, -1):
        up = pick(value, jnp.minimum(here + step, chips - 1), 0)
        down = pick(value, jnp.maximum(here - step, 0), 0)
        if from_below is not None:
            up = total(up, from_below).astype(value.dtype)
            down = total(down, from_above).astype(value.dtype)
        from_below = move_chips(up, 1, 0)
        from_above = move_chips(down, -1, 0)
    return total(pick(value, here, 0), from_below, from_above)


def scatter(value, rising):
    value = scatter_cores(value, 1)
    value = scatter_seq(value, 1, rising)
    return scatter_chips(value)


def exchange(blocks):
    size = lax.axis_size("seq")
    here = lax.axis_index("seq")
    out = place(jnp.zeros(blocks.shape, blocks.dtype), pick(blocks, here, 0), here, 0)
    for distance in range(1, size):
        peer = here ^ distance
        out = place(out, swap_seq(pick(blocks, peer, 0), distance), peer, 0)
    return out


def shards(
    inputs,
    cotangent,
    ln1_scale,
    ln1_offset,
    w_query,
    w_key,
    w_value,
    w_rel,
    content_bias,
    position_bias,
    w_out,
    b_out,
    ln2_scale,
    ln2_offset,
    w_in,
    b_in,
    w_mlp_out,
    b_mlp_out,
):
    win_size, seq_size = lax.axis_size("win"), lax.axis_size("seq")
    devices = win_size * seq_size
    grid = (win_size // CORES, CORES, seq_size)
    seq = lax.axis_index("seq")
    window_count, row_count, width = inputs.shape
    tokens = window_count * row_count
    hk = HEADS * KD
    vd = width // HEADS
    hp = HEADS // seq_size
    hidden = w_in.shape[1]
    scale_factor = KD ** (-0.5)

    vectors = (
        ln1_scale,
        ln1_offset,
        content_bias,
        position_bias,
        b_out,
        ln2_scale,
        ln2_offset,
        b_in,
        b_mlp_out,
    )
    packed = jnp.concatenate(vectors + (w_rel.T.reshape(-1),))
    packed_size = packed.shape[0]
    lines = -(-packed_size // 512) * 4
    packed = jnp.pad(packed, (0, lines * 128 - packed_size)).reshape(lines, 128)
    packed = gather(packed, True).reshape(devices, lines * 128)
    whole_vectors = []
    at = 0
    for vector in vectors:
        length = vector.shape[0]
        whole_vectors.append(packed[:, at : at + length].reshape(devices * length).astype(single))
        at += length
    whole_rel = packed[:, at:packed_size].reshape(hk, F)
    (
        ln1_gain,
        ln1_shift,
        bias_content,
        bias_position,
        bias_out,
        ln2_gain,
        ln2_shift,
        bias_in,
        bias_mlp,
    ) = whole_vectors

    whole_qk = gather(jnp.concatenate([w_query, w_key], axis=1), True).reshape(width, 2 * hk)
    whole_v = gather(w_value, False).reshape(width, width)
    whole_out = gather(w_out, True).reshape(width, width)
    whole_in = gather(w_in, False).reshape(width, hidden)
    whole_mlp = gather(w_mlp_out, True).reshape(hidden, width)

    features = jnp.pad(rel_features(WLEN, F).astype(bfloat), ((0, 1), (0, 0)))
    own_rel = lax.dynamic_slice_in_dim(whole_rel, seq * hp * KD, hp * KD, 0)
    table = jnp.einsum("cf,tf->ct", own_rel, features, preferred_element_type=single).astype(bfloat)

    source = inputs.reshape(tokens, width).astype(single)
    normed_one_f, norm_one_back = jax.vjp(layer_norm, source, ln1_gain, ln1_shift)
    normed_one = normed_one_f.astype(bfloat)
    proj_qk = jnp.dot(normed_one, whole_qk, preferred_element_type=single)
    query = proj_qk[:, :hk] * scale_factor
    proj_v = jnp.dot(normed_one, whole_v, preferred_element_type=single)
    parts = (
        (query + bias_content).astype(bfloat),
        (query + bias_position).astype(bfloat),
        proj_qk[:, hk:].astype(bfloat),
        proj_v.astype(bfloat),
    )
    outgoing = jnp.concatenate([part.reshape(tokens, seq_size, -1) for part in parts], axis=2)
    heads_in = exchange(jnp.transpose(outgoing, (1, 0, 2))).reshape(seq_size * tokens, -1)
    attention, mixed = attention_forward(heads_in, table, hp, vd, BLOCK_Q)
    attended = exchange(mixed.reshape(seq_size, tokens, hp * vd))
    attended = jnp.transpose(attended, (1, 0, 2)).reshape(tokens, width)

    hidden_in = source + jnp.dot(attended, whole_out, preferred_element_type=single) + bias_out
    normed_two_f, norm_two_back = jax.vjp(layer_norm, hidden_in, ln2_gain, ln2_shift)
    normed_two = normed_two_f.astype(bfloat)
    pre_act = jnp.dot(normed_two, whole_in, preferred_element_type=single) + bias_in
    gelu_out, gelu_back = jax.vjp(jax.nn.gelu, pre_act)
    activation = gelu_out.astype(bfloat)
    result = hidden_in + jnp.dot(activation, whole_mlp, preferred_element_type=single) + bias_mlp
    layer_out = result.astype(bfloat).reshape(inputs.shape)

    def weight_grad(left, right, rising):
        grad = jnp.einsum("td,te->de", left, right, preferred_element_type=single).astype(bfloat)
        rows, cols = grad.shape
        return scatter(grad.reshape(grid + (rows // devices, cols)), rising)

    cot_rows = cotangent.reshape(tokens, width)
    grad_mlp = weight_grad(activation, cot_rows, True)
    grad_bias_mlp = jnp.sum(cot_rows.astype(single), axis=0)
    grad_act = jnp.einsum("td,fd->tf", cot_rows, whole_mlp, preferred_element_type=single)
    grad_pre = gelu_back(grad_act)[0].astype(bfloat)
    grad_in = weight_grad(normed_two, grad_pre, False)
    grad_bias_in = jnp.sum(grad_pre.astype(single), axis=0)
    grad_normed_two = jnp.einsum("tf,df->td", grad_pre, whole_in, preferred_element_type=single)
    hidden_term, grad_ln2_gain, grad_ln2_shift = norm_two_back(grad_normed_two)
    grad_hidden = cot_rows.astype(single) + hidden_term
    grad_branch = grad_hidden.astype(bfloat)
    grad_out = weight_grad(attended, grad_branch, True)
    grad_bias_out = jnp.sum(grad_branch.astype(single), axis=0)
    grad_mixed = jnp.einsum(
        "te,de->td", grad_branch, whole_out, preferred_element_type=single
    ).astype(bfloat)
    grad_mixed = jnp.transpose(grad_mixed.reshape(tokens, seq_size, hp * vd), (1, 0, 2))
    grad_heads = exchange(grad_mixed).reshape(seq_size * tokens, hp * vd)
    grad_q, grad_kv, grad_table, grad_bias = attention_backward(
        heads_in, table, attention, grad_heads, hp, vd, BLOCK_Q
    )
    own = hp * KD
    returned = exchange(
        jnp.concatenate([grad_q, grad_kv], axis=1).reshape(seq_size, tokens, 2 * own + hp * vd)
    )
    returned = jnp.transpose(returned, (1, 0, 2))
    grad_qk_rows = jnp.concatenate(
        [
            returned[:, :, :own].reshape(tokens, hk),
            returned[:, :, own : 2 * own].reshape(tokens, hk),
        ],
        axis=1,
    )
    grad_v_rows = returned[:, :, 2 * own :].reshape(tokens, width)
    grad_qk = weight_grad(normed_one, grad_qk_rows, True)
    grad_v = weight_grad(normed_one, grad_v_rows, False)
    grad_normed_one = jnp.einsum(
        "tk,dk->td", grad_qk_rows, whole_qk, preferred_element_type=single
    ) + jnp.einsum("tk,dk->td", grad_v_rows, whole_v, preferred_element_type=single)
    source_term, grad_ln1_gain, grad_ln1_shift = norm_one_back(grad_normed_one)
    grad_inputs = (grad_hidden + source_term).reshape(inputs.shape)

    grad_rel = jnp.dot(grad_table, features.astype(single), precision=lax.Precision.HIGHEST)
    whole_grad_rel = lax.dynamic_update_slice_in_dim(
        jnp.zeros((hk, F), single), grad_rel, seq * own, 0
    )

    def spread(own_heads):
        return lax.dynamic_update_slice_in_dim(jnp.zeros((hk,), single), own_heads, seq * own, 0)

    vector_grads = (
        grad_ln1_gain,
        grad_ln1_shift,
        spread(grad_bias[0]),
        spread(grad_bias[1]),
        grad_bias_out,
        grad_ln2_gain,
        grad_ln2_shift,
        grad_bias_in,
        grad_bias_mlp,
    )
    small = jnp.concatenate(
        [v.reshape(devices, -1) for v in vector_grads + (whole_grad_rel,)], axis=1
    )
    small = jnp.pad(small, ((0, 0), (0, lines * 128 - packed_size)))
    small = scatter(small.reshape(grid + (lines, 128)), True).reshape(-1)[:packed_size]
    small_grads = []
    at = 0
    for vector in vectors:
        length = vector.shape[0]
        small_grads.append(small[at : at + length])
        at += length
    g = small_grads
    own_grad_rel = small[at:].reshape(-1, F).T
    return (
        layer_out,
        grad_inputs,
        g[0],
        g[1],
        grad_qk[:, :hk],
        grad_qk[:, hk:],
        grad_v,
        own_grad_rel,
        g[2],
        g[3],
        grad_out,
        g[4],
        g[5],
        g[6],
        grad_in,
        g[7],
        grad_mlp,
        g[8],
    )


def solution(mesh):
    in_specs = (
        P("win", "seq", None),
        P("win", "seq", None),
        P(("win", "seq")),
        P(("win", "seq")),
        P(("win", "seq"), None),
        P(("win", "seq"), None),
        P(("win", "seq"), None),
        P(None, ("win", "seq")),
        P(("win", "seq")),
        P(("win", "seq")),
        P(("win", "seq"), None),
        P(("win", "seq")),
        P(("win", "seq")),
        P(("win", "seq")),
        P(("win", "seq"), None),
        P(("win", "seq")),
        P(("win", "seq"), None),
        P(("win", "seq")),
    )
    out_specs = (
        P("win", "seq", None),
        P("win", "seq", None),
        P(("win", "seq")),
        P(("win", "seq")),
        P(("win", "seq"), None),
        P(("win", "seq"), None),
        P(("win", "seq"), None),
        P(None, ("win", "seq")),
        P(("win", "seq")),
        P(("win", "seq")),
        P(("win", "seq"), None),
        P(("win", "seq")),
        P(("win", "seq")),
        P(("win", "seq")),
        P(("win", "seq"), None),
        P(("win", "seq")),
        P(("win", "seq"), None),
        P(("win", "seq")),
    )
    return jax.shard_map(shards, mesh=mesh, in_specs=in_specs, out_specs=out_specs, check_vma=False)
```

time: 2270 us -> 874 us (0.39)
  waiting for transfers between devices: 1080 us -> 320 us
  local copies, waits for them, and re-layouts: 666 us -> 89.7 us
  starting transfers between devices: 12.5 us -> 211 us
  matrix products: 254 us -> 77.4 us
  blocking collectives: 152 us -> 0 us
  other arithmetic: 49.5 us -> 108 us
  Pallas kernels: 0 us -> 53.9 us
  loops' own time: 31.3 us -> 0 us
    reduce_scatter x7 -> x0, waiting for transfers between devices: 934 us -> none  [the longest x1 214 us: shards(): lax.psum_scatter(grad_w_mlp_out, ('win', 'seq'), scatter_dimension=0, til...]
    ppermute x8 -> x120, waiting for transfers between devices: 4.68 us -> 320 us  [the longest x36 255 us: swap_seq(): return lax.ppermute(value, 'seq', [(i, i ^ distance) for i in range(size)])]
    ppermute x8 -> x120, starting transfers between devices: 11.9 us -> 211 us  [the longest x72 169 us: move_chips(): return lax.ppermute(value, 'win', pairs)]
    while x149 -> x0, local copies, waits for them, and re-layouts: 177 us -> none
    dot_general x57 -> x17, matrix products: 254 us -> 77.4 us  [the longest x5 26.7 us: weight_grad(): jnp.einsum('td,te->de', left, right, preferred_element_type=single)]
    reshape x18 -> x22, local copies, waits for them, and re-layouts: 184 us -> 12.3 us  [the longest x10 6.1 us: shards(): v.reshape(devices, -1)]
    all_gather x8 -> x0, waiting for transfers between devices: 134 us -> none  [the longest x1 65 us: shards(): lax.all_gather(w_value, ('win', 'seq'), axis=0, tiled=True)]
    unnamed x2 -> x0, blocking collectives: 83.7 us -> none
  transfers between devices with their start and end apart: 23 -> 120, of which waited for: 13 -> 48; matrix products, arithmetic and copies ran while one was open for 26% -> 20% of each run, Pallas kernels for 0% -> 2%
where the time goes in v1:
time: 874 us; the launch traced here: 864 us
  waiting for transfers between devices  320 us (37%)
  starting transfers between devices  211 us (24%)
  other arithmetic  108 us (12%)
  local copies, waits for them, and re-layouts  89.7 us (10%)
  matrix products  77.4 us (9%)
  Pallas kernels  53.9 us (6%)
    ppermute x36, waiting for transfers between devices, swap_seq(): return lax.ppermute(value, 'seq', [(i, i ^ distance) for i in range(size)])  255 us
    ppermute x72, starting transfers between devices, move_chips(): return lax.ppermute(value, 'win', pairs)  169 us
    ppermute x72, waiting for transfers between devices, move_chips(): return lax.ppermute(value, 'win', pairs)  64.4 us
    ppermute x36, starting transfers between devices, swap_seq(): return lax.ppermute(value, 'seq', [(i, i ^ distance) for i in range(size)])  40.9 us
    another operation x12, other arithmetic, gather_cores(): jnp.stack([jnp.where(first, value, other), jnp.where(first, other, value)...  38.4 us
    pallas_call x1, Pallas kernels, attention_backward(): pl.pallas_call(functools.partial(bwd_kernel, L, bq, hp, vd), grid=(L // b...  32.4 us
    dot_general x5, matrix products, weight_grad(): jnp.einsum('td,te->de', left, right, preferred_element_type=single)  26.7 us
    pallas_call x1, Pallas kernels, attention_forward(): pl.pallas_call(functools.partial(fwd_kernel, L, bq, hp, vd), grid=(L // b...  21.5 us
  transfers between devices with their start and end apart: 120, of which 48 were waited for; matrix products, arithmetic and copies ran while one was open for 20% of the time, Pallas kernels for 2%

profile of v1, /device:TPU:0, one launch (start us, length us, event | category | flops | bytes accessed | tf_op | source)
XLA Modules:
  0.0 864.1 jit_solution(12327039091796791373)
XLA Ops:
  1.5 6.1 concatenate.68
  9.5 6.2 collective-permute-start.1
  40.0 5.5 collective-permute-done.4
  111.2 5.4 collective-permute-start.52
  158.8 5.3 collective-permute-done.55
  183.6 13.6 %collective-permute-done.16 = bf16[4,1,2,48,1024]{4,3,2,1,0:T(8,128)(2,1)S(1)} collective-permute-done((bf16[4,1,2,48,1024]{4,3,2,1,0:T(8,128)(2,1)S(1)}, bf16[4,1,2,48,1024]{4,3,2,1,0:T(8,128)(2,1)S(1)}, u32[]{:S(2)}, u32[]{:S(2)}) %collective-permute-start.16) | collective-permute-done | bytes 786464 | tf_op jit(solution)/shard_map/ppermute | solution.py:170
  197.6 9.8 %collective-permute-done.57 = bf16[4,1,1,96,1536]{4,3,2,1,0:T(8,128)(2,1)S(1)} collective-permute-done((bf16[4,1,1,96,1536]{4,3,2,1,0:T(8,128)(2,1)S(1)}, bf16[4,1,1,96,1536]{4,3,2,1,0:T(8,128)(2,1)S(1)}, u32[]{:S(2)}, u32[]{:S(2)}) %collective-permute-start.57) | collective-permute-done | bytes 1179680 | tf_op jit(solution)/shard_map/ppermute | solution.py:170
  208.3 14.2 %collective-permute-done.48 = bf16[4,1,1,48,3072]{4,3,2,1,0:T(8,128)(2,1)S(1)} collective-permute-done((bf16[4,1,1,48,3072]{4,3,2,1,0:T(8,128)(2,1)S(1)}, bf16[4,1,1,48,3072]{4,3,2,1,0:T(8,128)(2,1)S(1)}, u32[]{:S(2)}, u32[]{:S(2)}) %collective-permute-start.48) | collective-permute-done | bytes 1179680 | tf_op jit(solution)/shard_map/ppermute | solution.py:170
  224.0 8.6 collective-permute-done.25
  233.1 14.7 %collective-permute-done.40 = bf16[4,1,2,48,1536]{4,3,2,1,0:T(8,128)(2,1)S(1)} collective-permute-done((bf16[4,1,2,48,1536]{4,3,2,1,0:T(8,128)(2,1)S(1)}, bf16[4,1,2,48,1536]{4,3,2,1,0:T(8,128)(2,1)S(1)}, u32[]{:S(2)}, u32[]{:S(2)}) %collective-permute-start.40) | collective-permute-done | bytes 1179680 | tf_op jit(solution)/shard_map/ppermute | solution.py:170
  251.2 40.8 %collective-permute-done.58 = bf16[4,1,2,96,1536]{4,3,2,1,0:T(8,128)(2,1)} collective-permute-done((bf16[4,1,2,96,1536]{4,3,2,1,0:T(8,128)(2,1)S(1)}, bf16[4,1,2,96,1536]{4,3,2,1,0:T(8,128)(2,1)}, u32[]{:S(2)}, u32[]{:S(2)}) %collective-permute-start.58) | collective-permute-done | bytes 2359328 | tf_op jit(solution)/shard_map/ppermute | solution.py:170
  308.7 10.8 %collective-permute-done.27 = bf16[384,768]{1,0:T(8,128)(2,1)S(1)} collective-permute-done((bf16[384,768]{1,0:T(8,128)(2,1)S(1)}, bf16[384,768]{1,0:T(8,128)(2,1)S(1)}, u32[]{:S(2)}, u32[]{:S(2)}) %collective-permute-start.27) | collective-permute-done | bytes 589856 | tf_op jit(solution)/shard_map/ppermute | solution.py:170
  319.5 12.5 %collective-permute-done.29 = bf16[384,768]{1,0:T(8,128)(2,1)S(1)} collective-permute-done((bf16[384,768]{1,0:T(8,128)(2,1)S(1)}, bf16[384,768]{1,0:T(8,128)(2,1)S(1)}, u32[]{:S(2)}, u32[]{:S(2)}) %collective-permute-start.29) | collective-permute-done | bytes 589856 | tf_op jit(solution)/shard_map/ppermute | solution.py:170
  333.5 21.5 %shard_map.313 = (bf16[2,1536,1536]{2,1,0:T(8,128)(2,1)}, bf16[1536,384]{1,0:T(8,128)(2,1)}) custom-call(bf16[1536,768]{1,0:T(8,128)(2,1)} %bitcast.438, bf16[128,3072]{1,0:T(8,128)(2,1)} %convolution_convert_fusion.5.tab_ref), custom_call_target="tpu_custom_call" | custom-call | tf_op jit(solution)/shard_map/pallas_call | solution.py:74
  369.2 9.6 %collective-permute-done.31 = bf16[384,384]{0,1:T(8,128)(2,1)S(1)} collective-permute-done((bf16[384,384]{0,1:T(8,128)(2,1)S(1)}, bf16[384,384]{0,1:T(8,128)(2,1)S(1)}, u32[]{:S(2)}, u32[]{:S(2)}) %collective-permute-start.31) | collective-permute-done | bytes 294944 | tf_op jit(solution)/shard_map/ppermute | solution.py:170
  386.0 8.0 select_bitcast_fusion.1
  394.0 8.2 pad_maximum_fusion.1
  402.2 8.0 select_bitcast_fusion.3
  410.2 8.2 pad_maximum_fusion
  418.4 6.7 convolution_add_fusion
  425.1 11.4 %convert_reduce_fusion = (f32[3072]{0:T(1024)}, bf16[384,3072]{1,0:T(8,128)(2,1)S(1)}) fusion(f32[384,3072]{1,0:T(8,128)S(1)} %convolution_add_fusion, bf16[3072,1536]{1,0:T(8,128)(2,1)} %bitcast.448, bf16[1,384,1536]{2,1,0:T(8,128)(2,1)S(1)} %copy-done.6), kind=kOutput, calls=%fused_computation.36 | convolution fusion | flops 3649827840 | bytes 17707008 | tf_op jit(solution)/shard_map/td,fd->tf/dot_general | solution.py:397
  441.6 7.9 convolution_convert_fusion.1
  449.6 8.0 convolution_convert_fusion
  476.3 5.4 convolution_convert_fusion.2
  498.9 32.4 %shard_map.314 = (bf16[1536,128]{1,0:T(8,128)(2,1)}, bf16[1536,512]{1,0:T(8,128)(2,1)}, f32[128,3072]{1,0:T(8,128)}, f32[8,128]{1,0:T(8,128)}) custom-call(bf16[1536,768]{1,0:T(8,128)(2,1)} %bitcast.439, bf16[128,3072]{1,0:T(8,128)(2,1)} %convolution_convert_fusion.5.tab_ref, bf16[2,1536,1536]{2,1,0:T(8,128)(2,1)} %get-tuple-element.27.att_ref, ...), custom_call_target="tpu_custom_call" | custom-call | tf_op jit(solution)/shard_map/pallas_call | solution.py:141
  551.8 7.6 collective-permute-done.64
  618.3 13.3 %collective-permute-done.76 = bf16[4,1,2,48,1024]{4,3,2,1,0:T(8,128)(2,1)S(1)} collective-permute-done((bf16[4,1,2,48,1024]{4,3,2,1,0:T(8,128)(2,1)S(1)}, bf16[4,1,2,48,1024]{4,3,2,1,0:T(8,128)(2,1)S(1)}, u32[]{:S(2)}, u32[]{:S(2)}) %collective-permute-start.76) | collective-permute-done | bytes 786464 | tf_op jit(solution)/shard_map/ppermute | solution.py:170
  655.4 8.5 collective-permute-done.94
  694.9 9.7 %collective-permute-done.85 = bf16[4,2,1,48,1536]{4,3,2,1,0:T(8,128)(2,1)S(1)} collective-permute-done((bf16[4,2,1,48,1536]{4,3,2,1,0:T(8,128)(2,1)S(1)}, bf16[4,2,1,48,1536]{4,3,2,1,0:T(8,128)(2,1)S(1)}, u32[]{:S(2)}, u32[]{:S(2)}) %collective-permute-start.85) | collective-permute-done | bytes 1179680 | tf_op jit(solution)/shard_map/ppermute | solution.py:170
  750.0 18.6 %collective-permute-done.103 = bf16[4,2,1,48,3072]{4,3,2,1,0:T(8,128)(2,1)S(1)} collective-permute-done((bf16[4,2,1,48,3072]{4,3,2,1,0:T(8,128)(2,1)S(1)}, bf16[4,2,1,48,3072]{4,3,2,1,0:T(8,128)(2,1)S(1)}, u32[]{:S(2)}, u32[]{:S(2)}) %collective-permute-start.103) | collective-permute-done | bytes 2359328 | tf_op jit(solution)/shard_map/ppermute | solution.py:170
  770.9 21.5 %collective-permute-done.112 = bf16[4,1,2,96,1536]{4,3,2,1,0:T(8,128)(2,1)S(1)} collective-permute-done((bf16[4,1,2,96,1536]{4,3,2,1,0:T(8,128)(2,1)S(1)}, bf16[4,1,2,96,1536]{4,3,2,1,0:T(8,128)(2,1)S(1)}, u32[]{:S(2)}, u32[]{:S(2)}) %collective-permute-start.112) | collective-permute-done | bytes 2359328 | tf_op jit(solution)/shard_map/ppermute | solution.py:170
  795.3 16.3 %collective-permute-done.104 = bf16[4,1,1,48,3072]{4,3,2,1,0:T(8,128)(2,1)S(1)} collective-permute-done((bf16[4,1,1,48,3072]{4,3,2,1,0:T(8,128)(2,1)S(1)}, bf16[4,1,1,48,3072]{4,3,2,1,0:T(8,128)(2,1)S(1)}, u32[]{:S(2)}, u32[]{:S(2)}) %collective-permute-start.104) | collective-permute-done | bytes 1179680 | tf_op jit(solution)/shard_map/ppermute | solution.py:170
  (639 shorter events, 475.9 us)
Async XLA Ops:
  8.2 28.0 %collective-permute-start = (bf16[28,128]{1,0:T(8,128)(2,1)}, bf16[28,128]{1,0:T(8,128)(2,1)}, u32[]{:S(2)}, u32[]{:S(2)}) collective-permute-start(bf16[28,128]{1,0:T(8,128)(2,1)} %pad_bitcast_fusion), channel_id=1, source_target_pairs={{8,0},{12,4},{16,8},{20,12},{24,16},{28,20},{9,1},{13,5},{17,9},{2... | collective-permute-start | bytes 21512 | tf_op jit(solution)/shard_map/ppermute | solution.py:180
  18.5 51.3 %collective-permute-start.9 = (bf16[48,1024]{1,0:T(8,128)(2,1)}, bf16[48,1024]{1,0:T(8,128)(2,1)}, u32[]{:S(2)}, u32[]{:S(2)}) collective-permute-start(bf16[48,1024]{1,0:T(8,128)(2,1)} %constant_dynamic-update-slice_fusion.7), channel_id=1, source_target_pairs={{8,0},{12,4},{16,8},{20,12},{24,16},{28,20},{9,1},{13,5},{17,9},{2... | collective-permute-start | bytes 294920 | tf_op jit(solution)/shard_map/ppermute | solution.py:180
  19.8 45.3 %collective-permute-start.10 = (bf16[48,1024]{1,0:T(8,128)(2,1)}, bf16[48,1024]{1,0:T(8,128)(2,1)}, u32[]{:S(2)}, u32[]{:S(2)}) collective-permute-start(bf16[48,1024]{1,0:T(8,128)(2,1)} %constant_dynamic-update-slice_fusion.7), channel_id=1, source_target_pairs={{0,8},{4,12},{8,16},{12,20},{16,24},{20,28},{1,9},{5,13},{9,17},{1... | collective-permute-start | bytes 294920 | tf_op jit(solution)/shard_map/ppermute | solution.py:180
  24.9 86.3 %collective-permute-start.18 = (bf16[48,1536]{1,0:T(8,128)(2,1)}, bf16[48,1536]{1,0:T(8,128)(2,1)}, u32[]{:S(2)}, u32[]{:S(2)}) collective-permute-start(bf16[48,1536]{1,0:T(8,128)(2,1)} %param.28), channel_id=1, source_target_pairs={{8,0},{12,4},{16,8},{20,12},{24,16},{28,20},{9,1},{13,5},{17,9},{2... | collective-permute-start | bytes 442376 | tf_op jit(solution)/shard_map/ppermute | solution.py:180
  45.5 48.6 %collective-permute-start.19 = (bf16[48,1536]{1,0:T(8,128)(2,1)}, bf16[48,1536]{1,0:T(8,128)(2,1)}, u32[]{:S(2)}, u32[]{:S(2)}) collective-permute-start(bf16[48,1536]{1,0:T(8,128)(2,1)} %param.28), channel_id=1, source_target_pairs={{0,8},{4,12},{8,16},{12,20},{16,24},{20,28},{1,9},{5,13},{9,17},{1... | collective-permute-start | bytes 442376 | tf_op jit(solution)/shard_map/ppermute | solution.py:180
  69.8 56.9 %collective-permute-start.33 = (bf16[48,1536]{1,0:T(8,128)(2,1)}, bf16[48,1536]{1,0:T(8,128)(2,1)}, u32[]{:S(2)}, u32[]{:S(2)}) collective-permute-start(bf16[48,1536]{1,0:T(8,128)(2,1)} %param.32), channel_id=1, source_target_pairs={{8,0},{12,4},{16,8},{20,12},{24,16},{28,20},{9,1},{13,5},{17,9},{2... | collective-permute-start | bytes 442376 | tf_op jit(solution)/shard_map/ppermute | solution.py:180
  71.1 28.2 %collective-permute-start.13 = (bf16[48,1024]{1,0:T(8,128)(2,1)}, bf16[48,1024]{1,0:T(8,128)(2,1)}, u32[]{:S(2)}, u32[]{:S(2)}) collective-permute-start(bf16[48,1024]{1,0:T(8,128)(2,1)} %collective-permute-done.9), channel_id=1, source_target_pairs={{8,0},{12,4},{16,8},{20,12},{9,1},{13,5},{17,9},{21,13},{10,2},{14... | collective-permute-start | bytes 294920 | tf_op jit(solution)/shard_map/ppermute | solution.py:180
  108.6 39.8 %collective-permute-start.51 = (bf16[96,1536]{1,0:T(8,128)(2,1)}, bf16[96,1536]{1,0:T(8,128)(2,1)S(1)}, u32[]{:S(2)}, u32[]{:S(2)}) collective-permute-start(bf16[96,1536]{1,0:T(8,128)(2,1)} %param.38), channel_id=1, source_target_pairs={{8,0},{12,4},{16,8},{20,12},{24,16},{28,20},{9,1},{13,5},{17,9},{2... | collective-permute-start | bytes 884744 | tf_op jit(solution)/shard_map/ppermute | solution.py:180
  111.2 38.6 %collective-permute-start.52 = (bf16[96,1536]{1,0:T(8,128)(2,1)}, bf16[96,1536]{1,0:T(8,128)(2,1)S(1)}, u32[]{:S(2)}, u32[]{:S(2)}) collective-permute-start(bf16[96,1536]{1,0:T(8,128)(2,1)} %param.38), channel_id=1, source_target_pairs={{0,8},{4,12},{8,16},{12,20},{16,24},{20,28},{1,9},{5,13},{9,17},{1... | collective-permute-start | bytes 884744 | tf_op jit(solution)/shard_map/ppermute | solution.py:180
  178.3 29.0 %collective-permute-start.57 = (bf16[4,1,1,96,1536]{4,3,2,1,0:T(8,128)(2,1)S(1)}, bf16[4,1,1,96,1536]{4,3,2,1,0:T(8,128)(2,1)S(1)}, u32[]{:S(2)}, u32[]{:S(2)}) collective-permute-start(bf16[4,1,1,96,1536]{4,3,2,1,0:T(8,128)(2,1)S(1)} %bitcast_dynamic-update-slice_fusion.14), channel_id=1, source_target_pairs={{0,1},{1,0},{2,3},{3,2},{4,5},{5,4},{6,7},{7,6},{8,9},{9,8},{10,11... | collective-permute-start | bytes 3538952 | tf_op jit(solution)/shard_map/ppermute | solution.py:170
  180.4 42.1 %collective-permute-start.48 = (bf16[4,1,1,48,3072]{4,3,2,1,0:T(8,128)(2,1)S(1)}, bf16[4,1,1,48,3072]{4,3,2,1,0:T(8,128)(2,1)S(1)}, u32[]{:S(2)}, u32[]{:S(2)}) collective-permute-start(bf16[4,1,1,48,3072]{4,3,2,1,0:T(8,128)(2,1)S(1)} %bitcast_dynamic-update-slice_fusion.18), channel_id=1, source_target_pairs={{0,2},{1,3},{2,0},{3,1},{4,6},{5,7},{6,4},{7,5},{8,10},{9,11},{10,... | collective-permute-start | bytes 3538952 | tf_op jit(solution)/shard_map/ppermute | solution.py:170
  182.3 50.3 %collective-permute-start.25 = (bf16[4,2,1,48,1536]{4,3,2,1,0:T(8,128)(2,1)S(1)}, bf16[4,2,1,48,1536]{4,3,2,1,0:T(8,128)(2,1)S(1)}, u32[]{:S(2)}, u32[]{:S(2)}) collective-permute-start(bf16[4,2,1,48,1536]{4,3,2,1,0:T(8,128)(2,1)S(1)} %pad_maximum_fusion.13), channel_id=1, source_target_pairs={{0,1},{1,0},{2,3},{3,2},{4,5},{5,4},{6,7},{7,6},{8,9},{9,8},{10,11... | collective-permute-start | bytes 3538952 | tf_op jit(solution)/shard_map/ppermute | solution.py:170
  183.1 64.7 %collective-permute-start.40 = (bf16[4,1,2,48,1536]{4,3,2,1,0:T(8,128)(2,1)S(1)}, bf16[4,1,2,48,1536]{4,3,2,1,0:T(8,128)(2,1)S(1)}, u32[]{:S(2)}, u32[]{:S(2)}) collective-permute-start(bf16[4,1,2,48,1536]{4,3,2,1,0:T(8,128)(2,1)S(1)} %pad_maximum_fusion.14), channel_id=1, source_target_pairs={{0,2},{1,3},{2,0},{3,1},{4,6},{5,7},{6,4},{7,5},{8,10},{9,11},{10,... | collective-permute-start | bytes 3538952 | tf_op jit(solution)/shard_map/ppermute | solution.py:170
  197.5 50.8 %collective-permute-start.17 = (bf16[4,4,48,1024]{3,2,1,0:T(8,128)(2,1)S(1)}, bf16[4,4,48,1024]{3,2,1,0:T(8,128)(2,1)S(1)}, u32[]{:S(2)}, u32[]{:S(2)}) collective-permute-start(bf16[4,4,48,1024]{3,2,1,0:T(8,128)(2,1)S(1)} %bitcast.477), channel_id=1, source_target_pairs={{0,4},{4,0},{8,12},{12,8},{16,20},{20,16},{24,28},{28,24},{1,5},{5... | collective-permute-start | bytes 4718600 | tf_op jit(solution)/shard_map/ppermute | solution.py:165
  207.7 84.3 %collective-permute-start.58 = (bf16[4,1,2,96,1536]{4,3,2,1,0:T(8,128)(2,1)S(1)}, bf16[4,1,2,96,1536]{4,3,2,1,0:T(8,128)(2,1)}, u32[]{:S(2)}, u32[]{:S(2)}) collective-permute-start(bf16[4,1,2,96,1536]{4,3,2,1,0:T(8,128)(2,1)S(1)} %pad_maximum_fusion.10), channel_id=1, source_target_pairs={{0,2},{1,3},{2,0},{3,1},{4,6},{5,7},{6,4},{7,5},{8,10},{9,11},{10,... | collective-permute-start | bytes 7077896 | tf_op jit(solution)/shard_map/ppermute | solution.py:170
  223.0 73.5 %collective-permute-start.49 = (bf16[4,2,1,48,3072]{4,3,2,1,0:T(8,128)(2,1)S(1)}, bf16[4,2,1,48,3072]{4,3,2,1,0:T(8,128)(2,1)S(1)}, u32[]{:S(2)}, u32[]{:S(2)}) collective-permute-start(bf16[4,2,1,48,3072]{4,3,2,1,0:T(8,128)(2,1)S(1)} %pad_maximum_fusion.9), channel_id=1, source_target_pairs={{0,1},{1,0},{2,3},{3,2},{4,5},{5,4},{6,7},{7,6},{8,9},{9,8},{10,11... | collective-permute-start | bytes 7077896 | tf_op jit(solution)/shard_map/ppermute | solution.py:170
  233.0 66.9 %collective-permute-start.26 = (bf16[4,4,48,1536]{3,2,1,0:T(8,128)(2,1)S(1)}, bf16[4,4,48,1536]{3,2,1,0:T(8,128)(2,1)S(1)}, u32[]{:S(2)}, u32[]{:S(2)}) collective-permute-start(bf16[4,4,48,1536]{3,2,1,0:T(8,128)(2,1)S(1)} %bitcast.468), channel_id=1, source_target_pairs={{0,4},{4,0},{8,12},{12,8},{16,20},{20,16},{24,28},{28,24},{1,5},{5... | collective-permute-start | bytes 7077896 | tf_op jit(solution)/shard_map/ppermute | solution.py:165
  248.2 56.7 %collective-permute-start.41 = (bf16[4,4,48,1536]{3,2,1,0:T(8,128)(2,1)S(1)}, bf16[4,4,48,1536]{3,2,1,0:T(8,128)(2,1)S(1)}, u32[]{:S(2)}, u32[]{:S(2)}) collective-permute-start(bf16[4,4,48,1536]{3,2,1,0:T(8,128)(2,1)S(1)} %bitcast.466), channel_id=1, source_target_pairs={{0,4},{4,0},{8,12},{12,8},{16,20},{20,16},{24,28},{28,24},{1,5},{5... | collective-permute-start | bytes 7077896 | tf_op jit(solution)/shard_map/ppermute | solution.py:165
  296.5 89.5 %collective-permute-start.59 = (bf16[4,4,96,1536]{3,2,1,0:T(8,128)(2,1)}, bf16[4,4,96,1536]{3,2,1,0:T(8,128)(2,1)}, u32[]{:S(2)}, u32[]{:S(2)}) collective-permute-start(bf16[4,4,96,1536]{3,2,1,0:T(8,128)(2,1)} %bitcast.70), channel_id=1, source_target_pairs={{0,4},{4,0},{8,12},{12,8},{16,20},{20,16},{24,28},{28,24},{1,5},{5... | collective-permute-start | bytes 14155784 | tf_op jit(solution)/shard_map/ppermute | solution.py:165
  299.4 102.8 %collective-permute-start.50 = (bf16[4,4,48,3072]{3,2,1,0:T(8,128)(2,1)}, bf16[4,4,48,3072]{3,2,1,0:T(8,128)(2,1)}, u32[]{:S(2)}, u32[]{:S(2)}) collective-permute-start(bf16[4,4,48,3072]{3,2,1,0:T(8,128)(2,1)} %bitcast.61), channel_id=1, source_target_pairs={{0,4},{4,0},{8,12},{12,8},{16,20},{20,16},{24,28},{28,24},{1,5},{5... | collective-permute-start | bytes 14155784 | tf_op jit(solution)/shard_map/ppermute | solution.py:165
  577.4 56.0 %collective-permute-start.93 = (bf16[4,4,48,1536]{3,2,1,0:T(8,128)(2,1)}, bf16[4,4,48,1536]{3,2,1,0:T(8,128)(2,1)}, u32[]{:S(2)}, u32[]{:S(2)}) collective-permute-start(bf16[4,4,48,1536]{3,2,1,0:T(8,128)(2,1)} %dynamic-slice_bitcast_fusion.2), channel_id=1, source_target_pairs={{0,4},{4,0},{8,12},{12,8},{16,20},{20,16},{24,28},{28,24},{1,5},{5... | collective-permute-start | bytes 7077896 | tf_op jit(solution)/shard_map/ppermute | solution.py:165
  605.2 41.4 %collective-permute-start.84 = (bf16[4,4,48,1536]{3,2,1,0:T(8,128)(2,1)}, bf16[4,4,48,1536]{3,2,1,0:T(8,128)(2,1)}, u32[]{:S(2)}, u32[]{:S(2)}) collective-permute-start(bf16[4,4,48,1536]{3,2,1,0:T(8,128)(2,1)} %dynamic-slice_bitcast_fusion.3), channel_id=1, source_target_pairs={{0,4},{4,0},{8,12},{12,8},{16,20},{20,16},{24,28},{28,24},{1,5},{5... | collective-permute-start | bytes 7077896 | tf_op jit(solution)/shard_map/ppermute | solution.py:165
  615.3 99.2 %collective-permute-start.102 = (bf16[4,4,48,3072]{3,2,1,0:T(8,128)(2,1)}, bf16[4,4,48,3072]{3,2,1,0:T(8,128)(2,1)}, u32[]{:S(2)}, u32[]{:S(2)}) collective-permute-start(bf16[4,4,48,3072]{3,2,1,0:T(8,128)(2,1)} %dynamic-slice_bitcast_fusion.1), channel_id=1, source_target_pairs={{0,4},{4,0},{8,12},{12,8},{16,20},{20,16},{24,28},{28,24},{1,5},{5... | collective-permute-start | bytes 14155784 | tf_op jit(solution)/shard_map/ppermute | solution.py:165
  615.4 110.4 %collective-permute-start.111 = (bf16[4,4,96,1536]{3,2,1,0:T(8,128)(2,1)}, bf16[4,4,96,1536]{3,2,1,0:T(8,128)(2,1)}, u32[]{:S(2)}, u32[]{:S(2)}) collective-permute-start(bf16[4,4,96,1536]{3,2,1,0:T(8,128)(2,1)} %dynamic-slice_bitcast_fusion), channel_id=1, source_target_pairs={{0,4},{4,0},{8,12},{12,8},{16,20},{20,16},{24,28},{28,24},{1,5},{5... | collective-permute-start | bytes 14155784 | tf_op jit(solution)/shard_map/ppermute | solution.py:165
  673.2 31.5 %collective-permute-start.85 = (bf16[4,2,1,48,1536]{4,3,2,1,0:T(8,128)(2,1)S(1)}, bf16[4,2,1,48,1536]{4,3,2,1,0:T(8,128)(2,1)S(1)}, u32[]{:S(2)}, u32[]{:S(2)}) collective-permute-start(bf16[4,2,1,48,1536]{4,3,2,1,0:T(8,128)(2,1)S(1)} %constant_dynamic-slice_fusion.7), channel_id=1, source_target_pairs={{0,1},{1,0},{2,3},{3,2},{4,5},{5,4},{6,7},{7,6},{8,9},{9,8},{10,11... | collective-permute-start | bytes 3538952 | tf_op jit(solution)/shard_map/ppermute | solution.py:170
  706.6 34.5 %collective-permute-start.98 = (bf16[48,1536]{1,0:T(8,128)(2,1)S(1)}, bf16[48,1536]{1,0:T(8,128)(2,1)S(1)}, u32[]{:S(2)}, u32[]{:S(2)}) collective-permute-start(bf16[48,1536]{1,0:T(8,128)(2,1)S(1)} %get-tuple-element.105), channel_id=1, source_target_pairs={{0,8},{4,12},{8,16},{12,20},{16,24},{20,28},{1,9},{5,13},{9,17},{1... | collective-permute-start | bytes 442376 | tf_op jit(solution)/shard_map/ppermute | solution.py:180
  713.2 27.9 %collective-permute-start.101 = (bf16[48,1536]{1,0:T(8,128)(2,1)}, bf16[48,1536]{1,0:T(8,128)(2,1)S(1)}, u32[]{:S(2)}, u32[]{:S(2)}) collective-permute-start(bf16[48,1536]{1,0:T(8,128)(2,1)} %fusion.68), channel_id=1, source_target_pairs={{8,0},{12,4},{16,8},{20,12},{24,16},{28,20},{9,1},{13,5},{17,9},{2... | collective-permute-start | bytes 442376 | tf_op jit(solution)/shard_map/ppermute | solution.py:180
  719.0 49.5 %collective-permute-start.103 = (bf16[4,2,1,48,3072]{4,3,2,1,0:T(8,128)(2,1)S(1)}, bf16[4,2,1,48,3072]{4,3,2,1,0:T(8,128)(2,1)S(1)}, u32[]{:S(2)}, u32[]{:S(2)}) collective-permute-start(bf16[4,2,1,48,3072]{4,3,2,1,0:T(8,128)(2,1)S(1)} %constant_dynamic-slice_fusion.3), channel_id=1, source_target_pairs={{0,1},{1,0},{2,3},{3,2},{4,5},{5,4},{6,7},{7,6},{8,9},{9,8},{10,11... | collective-permute-start | bytes 7077896 | tf_op jit(solution)/shard_map/ppermute | solution.py:170
  738.2 54.2 %collective-permute-start.112 = (bf16[4,1,2,96,1536]{4,3,2,1,0:T(8,128)(2,1)S(1)}, bf16[4,1,2,96,1536]{4,3,2,1,0:T(8,128)(2,1)S(1)}, u32[]{:S(2)}, u32[]{:S(2)}) collective-permute-start(bf16[4,1,2,96,1536]{4,3,2,1,0:T(8,128)(2,1)S(1)} %constant_dynamic-slice_fusion.1), channel_id=1, source_target_pairs={{0,2},{1,3},{2,0},{3,1},{4,6},{5,7},{6,4},{7,5},{8,10},{9,11},{10,... | collective-permute-start | bytes 7077896 | tf_op jit(solution)/shard_map/ppermute | solution.py:170
  741.9 52.6 %collective-permute-start.89 = (bf16[48,1536]{1,0:T(8,128)(2,1)S(1)}, bf16[48,1536]{1,0:T(8,128)(2,1)S(1)}, u32[]{:S(2)}, u32[]{:S(2)}) collective-permute-start(bf16[48,1536]{1,0:T(8,128)(2,1)S(1)} %get-tuple-element.109), channel_id=1, source_target_pairs={{0,8},{4,12},{8,16},{12,20},{16,24},{20,28},{1,9},{5,13},{9,17},{1... | collective-permute-start | bytes 442376 | tf_op jit(solution)/shard_map/ppermute | solution.py:180
  748.7 45.8 %collective-permute-start.92 = (bf16[48,1536]{1,0:T(8,128)(2,1)S(1)}, bf16[48,1536]{1,0:T(8,128)(2,1)S(1)}, u32[]{:S(2)}, u32[]{:S(2)}) collective-permute-start(bf16[48,1536]{1,0:T(8,128)(2,1)S(1)} %fusion.73), channel_id=1, source_target_pairs={{8,0},{12,4},{16,8},{20,12},{24,16},{28,20},{9,1},{13,5},{17,9},{2... | collective-permute-start | bytes 442376 | tf_op jit(solution)/shard_map/ppermute | solution.py:180
  769.5 42.1 %collective-permute-start.104 = (bf16[4,1,1,48,3072]{4,3,2,1,0:T(8,128)(2,1)S(1)}, bf16[4,1,1,48,3072]{4,3,2,1,0:T(8,128)(2,1)S(1)}, u32[]{:S(2)}, u32[]{:S(2)}) collective-permute-start(bf16[4,1,1,48,3072]{4,3,2,1,0:T(8,128)(2,1)S(1)} %constant_dynamic-slice_fusion.2), channel_id=1, source_target_pairs={{0,2},{1,3},{2,0},{3,1},{4,6},{5,7},{6,4},{7,5},{8,10},{9,11},{10,... | collective-permute-start | bytes 3538952 | tf_op jit(solution)/shard_map/ppermute | solution.py:170
  (166 other events, 1772.4 us)

commit v2 on v1

--- a/solution.py
+++ b/solution.py
@@ -160,116 +160,395 @@
     return lax.dynamic_update_slice_in_dim(stacked, jnp.expand_dims(piece, axis), index, axis)
 
 
-def swap_cores(value):
-    size = lax.axis_size("win")
-    return lax.ppermute(value, "win", [(i, i ^ 1) for i in range(size)])
-
-
 def swap_seq(value, distance):
     size = lax.axis_size("seq")
     return lax.ppermute(value, "seq", [(i, i ^ distance) for i in range(size)])
 
 
-def move_chips(value, direction, first):
-    size = lax.axis_size("win")
-    chips = size // CORES
-    if direction > 0:
-        pairs = [(i, i + CORES) for i in range(size - CORES) if i // CORES >= first]
-    else:
-        pairs = [(i, i - CORES) for i in range(CORES, size) if i // CORES < chips - first]
-    return lax.ppermute(value, "win", pairs)
-
-
-def gather_chips(shard):
+def partners():
+    win, seq = lax.axis_index("win"), lax.axis_index("seq")
     chips = lax.axis_size("win") // CORES
-    here = lax.axis_index("win") // CORES
-    out = place(jnp.zeros((chips,) + shard.shape, shard.dtype), shard, here, 0)
-    above, below = [shard], [shard]
-    for step in range(1, chips):
-        below.append(move_chips(below[-1], 1, step - 1))
-        above.append(move_chips(above[-1], -1, step - 1))
-    for step in range(1, chips):
-        piece = jnp.where(here + step < chips, above[step], below[chips - step])
-        out = place(out, piece, (here + step) % chips, 0)
-    return out
-
-
-def gather_seq(value, axis, rising):
-    size = lax.axis_size("seq")
-    here = lax.axis_index("seq")
-    bits = [1 << b for b in range(size.bit_length() - 1)]
-    shape = value.shape
-    lead, tail = shape[:axis], shape[axis:]
-    value = value.reshape(lead + (1,) * len(bits) + tail)
-    for bit in bits if rising else bits[::-1]:
-        at = axis + len(bits) - bit.bit_length()
-        other = swap_seq(value, bit)
-        own_low = (here & bit) == 0
-        value = jnp.concatenate(
-            [jnp.where(own_low, value, other), jnp.where(own_low, other, value)], axis=at
+    bits = lax.axis_size("seq").bit_length() - 1
+    return win, seq, win // CORES, win % CORES, chips, bits
+
+
+def start_together():
+    win, seq, here, core, chips, bits = partners()
+    barrier = pltpu.get_barrier_semaphore()
+
+    def greet(to_win, to_seq):
+        pl.semaphore_signal(
+            barrier, inc=1, device_id=(to_win, to_seq), device_id_type=pl.DeviceIdType.MESH
         )
-    return value.reshape(lead + (size,) + tail)
-
-
-def gather_cores(value, axis):
-    other = swap_cores(value)
-    first = lax.axis_index("win") % CORES == 0
-    return jnp.stack([jnp.where(first, value, other), jnp.where(first, other, value)], axis=axis)
-
-
-def gather(shard, rising):
-    value = gather_chips(shard)
-    value = gather_seq(value, 1, rising)
-    return gather_cores(value, 1)
-
-
-def total(first, *others):
-    result = first.astype(single)
-    for other in others:
-        result = result + other.astype(single)
-    return result
-
-
-def scatter_cores(value, axis):
-    core = lax.axis_index("win") % CORES
-    arrived = swap_cores(pick(value, 1 - core, axis))
-    return total(pick(value, core, axis), arrived).astype(value.dtype)
-
-
-def scatter_seq(value, axis, rising):
-    size = lax.axis_size("seq")
-    here = lax.axis_index("seq")
-    bits = [1 << b for b in range(size.bit_length() - 1)]
-    shape = value.shape
-    lead, tail = shape[:axis], shape[axis + 1 :]
-    value = value.reshape(lead + (2,) * len(bits) + tail)
-    for bit in bits[::-1] if rising else bits:
-        at = axis + len(bits) - bit.bit_length()
-        mine = (here & bit) // bit
-        arrived = swap_seq(lax.dynamic_slice_in_dim(value, 1 - mine, 1, at), bit)
-        value = total(lax.dynamic_slice_in_dim(value, mine, 1, at), arrived).astype(value.dtype)
-    return value.reshape(lead + tail)
-
-
-def scatter_chips(value):
+
+    greet(win ^ 1, seq)
+    for bit in range(bits):
+        greet(win, seq ^ (1 << bit))
+
+    @pl.when(here > 0)
+    def _():
+        greet(win - CORES, seq)
+
+    @pl.when(here < chips - 1)
+    def _():
+        greet(win + CORES, seq)
+
+    ends = jnp.where(here > 0, 1, 0) + jnp.where(here < chips - 1, 1, 0)
+    pl.semaphore_wait(barrier, 1 + bits + ends)
+
+
+def gather_kernel(plan, count, spacing, *refs):
+    shards, outs = refs[:count], refs[count : 2 * count]
+    send_sem, recv_sem, local_sem = refs[2 * count :]
+    win, seq, here, core, chips, bits = partners()
+    own_bits = tuple((seq >> bit) & 1 for bit in reversed(range(bits)))
+    own_seq = {bit: (seq >> bit) & 1 for bit in range(bits)}
+
+    def region(chunk, chip, done, lead=0, span=None):
+        which, col, cols, _ = chunk
+        start, size = (col + lead, cols) if span is None else (col + lead, span)
+        index = tuple(slice(None) if bit in done else own_seq[bit] for bit in reversed(range(bits)))
+        return outs[which].at[(chip, core) + index + (slice(None), pl.ds(start, size))]
+
+    def copy(ref, number, kind, to_win, to_seq):
+        return pltpu.make_async_remote_copy(
+            src_ref=ref,
+            dst_ref=ref,
+            send_sem=send_sem.at[number, kind],
+            recv_sem=recv_sem.at[number, kind],
+            device_id=(to_win, to_seq),
+            device_id_type=pl.DeviceIdType.MESH,
+        )
+
+    chip_steps = chips - 1
+    every_bit = frozenset(range(bits))
+
+    def guarded(condition, action):
+        pl.when(condition)(action)
+
+    def chip_stage(chunk, number, step, done):
+        up_shard, down_shard = here - step, here + step
+        up = copy(region(chunk, jnp.maximum(up_shard, 0), done), number, step, win + CORES, seq)
+        down = copy(
+            region(chunk, jnp.minimum(down_shard, chips - 1), done),
+            number,
+            chip_steps + step,
+            win - CORES,
+            seq,
+        )
+        sends_up = (up_shard >= 0) & (here < chips - 1)
+        sends_down = (down_shard < chips) & (here > 0)
+        gets_up = here >= step + 1
+        gets_down = here + step + 1 < chips
+
+        def start():
+            guarded(sends_up, up.start)
+            guarded(sends_down, down.start)
+
+        def arrive():
+            guarded(gets_up, up.wait_recv)
+            guarded(gets_down, down.wait_recv)
+
+        def finish():
+            guarded(sends_up, up.wait_send)
+            guarded(sends_down, down.wait_send)
+
+        return start, arrive, finish
+
+    def bit_stage(chunk, number, step, chip):
+        half = chunk[2] // 2
+        copies = []
+        for part in range(2):
+            order = list(range(bits)) if part == 0 else list(reversed(range(bits)))
+            ref = region(chunk, chip, frozenset(order[:step]), part * half, half)
+            kind = 2 * chip_steps + part * bits + step
+            copies.append(copy(ref, number, kind, win, seq ^ (1 << order[step])))
+
+        def start():
+            for item in copies:
+                item.start()
+
+        def arrive():
+            for item in copies:
+                item.wait_recv()
+
+        def finish():
+            for item in copies:
+                item.wait_send()
+
+        return start, arrive, finish
+
+    def core_stage(chunk, number):
+        kind = 2 * chip_steps + 2 * bits
+        item = copy(region(chunk, slice(None), every_bit), number, kind, win ^ 1, seq)
+        return item.start, item.wait_recv, item.wait_send
+
+    def stages(chunk, number):
+        if chunk[3]:
+            line = [chip_stage(chunk, number, step, frozenset()) for step in range(chip_steps)]
+            cube = [bit_stage(chunk, number, step, slice(None)) for step in range(bits)]
+            return line + cube + [core_stage(chunk, number)]
+        cube = [bit_stage(chunk, number, step, here) for step in range(bits)]
+        line = [chip_stage(chunk, number, step, every_bit) for step in range(chip_steps)]
+        return cube + line + [core_stage(chunk, number)]
+
+    locals_ = []
+    for which in range(count):
+        target = outs[which].at[(here, core) + own_bits]
+        locals_.append(pltpu.make_async_copy(shards[which], target, local_sem.at[which]))
+    for item in locals_:
+        item.start()
+    start_together()
+    for item in locals_:
+        item.wait()
+    work = [stages(chunk, number) for number, chunk in enumerate(plan)]
+    depth = chip_steps + bits + 1
+    for turn in range(len(plan) + spacing * depth):
+        for number in range(len(plan)):
+            at, off = divmod(turn - number, spacing)
+            if off == 0 and 0 < at <= depth:
+                work[number][at - 1][1]()
+            if off == 0 and 0 <= at < depth:
+                work[number][at][0]()
+    for items in work:
+        for item in items:
+            item[2]()
+
+
+def gather_all(shards, widths, lines_first, spacing, collective_id):
     chips = lax.axis_size("win") // CORES
-    here = lax.axis_index("win") // CORES
-    from_below = from_above = None
-    for step in range(chips - 1, 0, -1):
-        up = pick(value, jnp.minimum(here + step, chips - 1), 0)
-        down = pick(value, jnp.maximum(here - step, 0), 0)
-        if from_below is not None:
-            up = total(up, from_below).astype(value.dtype)
-            down = total(down, from_above).astype(value.dtype)
-        from_below = move_chips(up, 1, 0)
-        from_above = move_chips(down, -1, 0)
-    return total(pick(value, here, 0), from_below, from_above)
-
-
-def scatter(value, rising):
-    value = scatter_cores(value, 1)
-    value = scatter_seq(value, 1, rising)
-    return scatter_chips(value)
+    bits = lax.axis_size("seq").bit_length() - 1
+    plan = []
+    for which, (shard, width) in enumerate(zip(shards, widths)):
+        for col in range(0, shard.shape[1], width):
+            plan.append((which, col, width, lines_first(len(plan))))
+    kinds = 2 * (chips - 1) + 2 * bits + 1
+    return pl.pallas_call(
+        functools.partial(gather_kernel, tuple(plan), len(shards), spacing),
+        in_specs=[pl.BlockSpec(memory_space=pl.ANY)] * len(shards),
+        out_specs=[pl.BlockSpec(memory_space=pl.ANY)] * len(shards),
+        out_shape=[
+            jax.ShapeDtypeStruct((chips, CORES) + (2,) * bits + s.shape, s.dtype) for s in shards
+        ],
+        scratch_shapes=[
+            pltpu.SemaphoreType.DMA((len(plan), kinds)),
+            pltpu.SemaphoreType.DMA((len(plan), kinds)),
+            pltpu.SemaphoreType.DMA((len(shards),)),
+        ],
+        compiler_params=pltpu.CompilerParams(collective_id=collective_id, has_side_effects=True),
+    )(*shards)
+
+
+def scatter_kernel(plan, arrays, spacing, *refs):
+    count = len(arrays)
+    grads, outs, rest = refs[:count], refs[count : 2 * count], refs[2 * count :]
+    win, seq, here, core, chips, bits = partners()
+    chip_steps = chips - 1
+    kept, from_core, rest = rest[:count], rest[count : 2 * count], rest[2 * count :]
+    from_bits, rest = rest[: count * bits], rest[count * bits :]
+    from_chips, rest = rest[:count], rest[count:]
+    send_sem, recv_sem, local_sem = rest
+    own_seq = {bit: (seq >> bit) & 1 for bit in range(bits)}
+
+    def add(target, source):
+        target[...] = (target[...].astype(single) + source[...].astype(single)).astype(bfloat)
+
+    def slabs(chunk, chip, bit_index, lead=0, span=None):
+        which, slot, _ = chunk
+        index = tuple(bit_index.get(bit, slice(None)) for bit in reversed(range(bits)))
+        width = arrays[which][1]
+        columns = pl.ds(lead, width if span is None else span)
+        return kept[which].at[(slot, chip) + index + (slice(None), columns)]
+
+    def copy(src, dst, number, kind, to_win, to_seq):
+        return pltpu.make_async_remote_copy(
+            src_ref=src,
+            dst_ref=dst,
+            send_sem=send_sem.at[number, kind],
+            recv_sem=recv_sem.at[number, kind],
+            device_id=(to_win, to_seq),
+            device_id_type=pl.DeviceIdType.MESH,
+        )
+
+    def core_stage(chunk, number):
+        which, slot, _ = chunk
+        width = arrays[which][1]
+        columns = (slice(None),) * bits + (slice(None), pl.ds(slot * width, width))
+        kind = 2 * chip_steps + 2 * bits
+        item = copy(
+            grads[which].at[(slice(None), 1 - core) + columns],
+            from_core[which].at[slot],
+            number,
+            kind,
+            win ^ 1,
+            seq,
+        )
+        own = pltpu.make_async_copy(
+            grads[which].at[(slice(None), core) + columns],
+            kept[which].at[slot],
+            local_sem.at[number],
+        )
+
+        def start():
+            item.start()
+            own.start()
+
+        def arrive():
+            own.wait()
+            item.wait_recv()
+            add(kept[which].at[slot], from_core[which].at[slot])
+
+        return start, arrive, item.wait_send
+
+    def bit_stage(chunk, number, step, chip):
+        which, slot, _ = chunk
+        half = arrays[which][1] // 2
+        items = []
+        for part in range(2):
+            order = list(range(bits)) if part else list(reversed(range(bits)))
+            bit = order[step]
+            done = {b: own_seq[b] for b in order[:step]}
+            kind = 2 * chip_steps + part * bits + step
+            buffer = from_bits[which * bits + step]
+            target = buffer.at[(slot, part) if isinstance(chip, slice) else (slot, part, 0)]
+            leaving = slabs(chunk, chip, done | {bit: 1 - own_seq[bit]}, part * half, half)
+            staying = slabs(chunk, chip, done | {bit: own_seq[bit]}, part * half, half)
+            sent = copy(leaving, target, number, kind, win, seq ^ (1 << bit))
+            items.append((sent, staying, target))
+
+        def start():
+            for sent, _, _ in items:
+                sent.start()
+
+        def arrive():
+            for sent, staying, target in items:
+                sent.wait_recv()
+                add(staying, target)
+
+        def finish():
+            for sent, _, _ in items:
+                sent.wait_send()
+
+        return start, arrive, finish
+
+    def chip_stage(chunk, number, step, bit_index):
+        which, slot, lines_last = chunk
+        part = (0,) * bits if lines_last else ()
+        up_to, down_to = here + step, here - step
+        up_slot = from_chips[which].at[(slot, step - 1) + part]
+        down_slot = from_chips[which].at[(slot, chip_steps + step - 1) + part]
+        up = copy(
+            slabs(chunk, jnp.minimum(up_to, chips - 1), bit_index),
+            up_slot,
+            number,
+            step - 1,
+            win + CORES,
+            seq,
+        )
+        down = copy(
+            slabs(chunk, jnp.maximum(down_to, 0), bit_index),
+            down_slot,
+            number,
+            chip_steps + step - 1,
+            win - CORES,
+            seq,
+        )
+        sends_up, sends_down = up_to < chips, down_to >= 0
+        gets_up = (here >= 1) & (here - 1 + step < chips)
+        gets_down = (here + 1 < chips) & (here + 1 - step >= 0)
+
+        def start():
+            pl.when(sends_up)(up.start)
+            pl.when(sends_down)(down.start)
+
+        def arrive():
+            @pl.when(gets_up)
+            def _():
+                up.wait_recv()
+                add(slabs(chunk, jnp.minimum(here + step - 1, chips - 1), bit_index), up_slot)
+
+            @pl.when(gets_down)
+            def _():
+                down.wait_recv()
+                add(slabs(chunk, jnp.maximum(here - step + 1, 0), bit_index), down_slot)
+
+        def finish():
+            pl.when(sends_up)(up.wait_send)
+            pl.when(sends_down)(down.wait_send)
+
+        return start, arrive, finish
+
+    def stages(chunk, number):
+        steps = range(chip_steps, 0, -1)
+        if chunk[2]:
+            cube = [bit_stage(chunk, number, step, slice(None)) for step in range(bits)]
+            line = [chip_stage(chunk, number, step, own_seq) for step in steps]
+            return [core_stage(chunk, number)] + cube + line
+        line = [chip_stage(chunk, number, step, {}) for step in steps]
+        cube = [bit_stage(chunk, number, step, here) for step in range(bits)]
+        return [core_stage(chunk, number)] + line + cube
+
+    start_together()
+    work = [stages(chunk, number) for number, chunk in enumerate(plan)]
+    depth = chip_steps + bits + 1
+    for turn in range(len(plan) + spacing * depth):
+        for number, chunk in enumerate(plan):
+            at, off = divmod(turn - number, spacing)
+            if off == 0 and 0 < at <= depth:
+                work[number][at - 1][1]()
+                if at == depth:
+                    which, slot, _ = chunk
+                    width = arrays[which][1]
+                    outs[which][:, pl.ds(slot * width, width)] = slabs(chunk, here, own_seq)[
+                        ...
+                    ].astype(single)
+            if off == 0 and 0 <= at < depth:
+                work[number][at][0]()
+    for items in work:
+        for item in items:
+            item[2]()
+
+
+def scatter_all(grads, widths, lines_last, spacing, collective_id):
+    chips = lax.axis_size("win") // CORES
+    bits = lax.axis_size("seq").bit_length() - 1
+    plan, arrays = [], []
+    kept, from_core, from_bits, from_chips = [], [], [], []
+    for which, (grad, width) in enumerate(zip(grads, widths)):
+        rows, cols = grad.shape[-2:]
+        slots = cols // width
+        lasts = [lines_last(len(plan) + slot) for slot in range(slots)]
+        plan += [(which, slot, last) for slot, last in enumerate(lasts)]
+        arrays.append((rows, width))
+        cube = (2,) * bits
+        kept.append(pltpu.VMEM((slots, chips) + cube + (rows, width), bfloat))
+        from_core.append(pltpu.VMEM((slots, chips) + cube + (rows, width), bfloat))
+        for step in range(bits):
+            left = (2,) * (bits - 1 - step)
+            from_bits.append(
+                pltpu.VMEM((slots, 2, chips) + left + (rows, width // 2), bfloat)
+            )
+        lone = (1,) * bits if all(lasts) else cube
+        from_chips.append(pltpu.VMEM((slots, 2 * (chips - 1)) + lone + (rows, width), bfloat))
+    kinds = 2 * (chips - 1) + 2 * bits + 1
+    return pl.pallas_call(
+        functools.partial(scatter_kernel, tuple(plan), tuple(arrays), spacing),
+        in_specs=[pl.BlockSpec(memory_space=pl.ANY)] * len(grads),
+        out_specs=[pl.BlockSpec(memory_space=pltpu.VMEM)] * len(grads),
+        out_shape=[jax.ShapeDtypeStruct(g.shape[-2:], single) for g in grads],
+        scratch_shapes=kept
+        + from_core
+        + from_bits
+        + from_chips
+        + [
+            pltpu.SemaphoreType.DMA((len(plan), kinds)),
+            pltpu.SemaphoreType.DMA((len(plan), kinds)),
+            pltpu.SemaphoreType.DMA((len(plan),)),
+        ],
+        compiler_params=pltpu.CompilerParams(
+            collective_id=collective_id, has_side_effects=True, vmem_limit_bytes=60 * 2**20
+        ),
+    )(*grads)
 
 
 def exchange(blocks):
@@ -304,7 +583,6 @@
 ):
     win_size, seq_size = lax.axis_size("win"), lax.axis_size("seq")
     devices = win_size * seq_size
-    grid = (win_size // CORES, CORES, seq_size)
     seq = lax.axis_index("seq")
     window_count, row_count, width = inputs.shape
     tokens = window_count * row_count
@@ -327,9 +605,25 @@
     )
     packed = jnp.concatenate(vectors + (w_rel.T.reshape(-1),))
     packed_size = packed.shape[0]
-    lines = -(-packed_size // 512) * 4
-    packed = jnp.pad(packed, (0, lines * 128 - packed_size)).reshape(lines, 128)
-    packed = gather(packed, True).reshape(devices, lines * 128)
+    small_cols = -(-packed_size // 4096) * 256
+    small_size = 16 * small_cols
+    packed = jnp.pad(packed, (0, small_size - packed_size)).reshape(16, small_cols)
+    packed, whole_qk, whole_v = gather_all(
+        (packed, jnp.concatenate([w_query, w_key], axis=1), w_value),
+        (256, 512, 512),
+        lambda number: number % 4 != 3,
+        2,
+        0,
+    )
+    packed = packed.reshape(devices, small_size)
+    whole_qk = whole_qk.reshape(width, 2 * hk)
+    whole_v = whole_v.reshape(width, width)
+    whole_out, whole_in, whole_mlp = gather_all(
+        (w_out, w_in, w_mlp_out), (512, 512, 256), lambda number: number % 4 != 3, 2, 1
+    )
+    whole_out = whole_out.reshape(width, width)
+    whole_in = whole_in.reshape(width, hidden)
+    whole_mlp = whole_mlp.reshape(hidden, width)
     whole_vectors = []
     at = 0
     for vector in vectors:
@@ -349,12 +643,6 @@
         bias_mlp,
     ) = whole_vectors
 
-    whole_qk = gather(jnp.concatenate([w_query, w_key], axis=1), True).reshape(width, 2 * hk)
-    whole_v = gather(w_value, False).reshape(width, width)
-    whole_out = gather(w_out, True).reshape(width, width)
-    whole_in = gather(w_in, False).reshape(width, hidden)
-    whole_mlp = gather(w_mlp_out, True).reshape(hidden, width)
-
     features = jnp.pad(rel_features(WLEN, F).astype(bfloat), ((0, 1), (0, 0)))
     own_rel = lax.dynamic_slice_in_dim(whole_rel, seq * hp * KD, hp * KD, 0)
     table = jnp.einsum("cf,tf->ct", own_rel, features, preferred_element_type=single).astype(bfloat)
@@ -386,23 +674,28 @@
     result = hidden_in + jnp.dot(activation, whole_mlp, preferred_element_type=single) + bias_mlp
     layer_out = result.astype(bfloat).reshape(inputs.shape)
 
-    def weight_grad(left, right, rising):
+    grid = (win_size // CORES, CORES) + (2,) * (seq_size.bit_length() - 1)
+
+    def weight_grad(left, right):
         grad = jnp.einsum("td,te->de", left, right, preferred_element_type=single).astype(bfloat)
         rows, cols = grad.shape
-        return scatter(grad.reshape(grid + (rows // devices, cols)), rising)
+        return grad.reshape(grid + (rows // devices, cols))
 
     cot_rows = cotangent.reshape(tokens, width)
-    grad_mlp = weight_grad(activation, cot_rows, True)
+    grad_mlp = weight_grad(activation, cot_rows)
     grad_bias_mlp = jnp.sum(cot_rows.astype(single), axis=0)
     grad_act = jnp.einsum("td,fd->tf", cot_rows, whole_mlp, preferred_element_type=single)
     grad_pre = gelu_back(grad_act)[0].astype(bfloat)
-    grad_in = weight_grad(normed_two, grad_pre, False)
+    grad_in = weight_grad(normed_two, grad_pre)
+    grad_mlp, grad_in = scatter_all(
+        (grad_mlp, grad_in), (256, 512), lambda number: number % 4 != 0, 2, 2
+    )
     grad_bias_in = jnp.sum(grad_pre.astype(single), axis=0)
     grad_normed_two = jnp.einsum("tf,df->td", grad_pre, whole_in, preferred_element_type=single)
     hidden_term, grad_ln2_gain, grad_ln2_shift = norm_two_back(grad_normed_two)
     grad_hidden = cot_rows.astype(single) + hidden_term
     grad_branch = grad_hidden.astype(bfloat)
-    grad_out = weight_grad(attended, grad_branch, True)
+    grad_out = weight_grad(attended, grad_branch)
     grad_bias_out = jnp.sum(grad_branch.astype(single), axis=0)
     grad_mixed = jnp.einsum(
         "te,de->td", grad_branch, whole_out, preferred_element_type=single
@@ -425,8 +718,8 @@
         axis=1,
     )
     grad_v_rows = returned[:, :, 2 * own :].reshape(tokens, width)
-    grad_qk = weight_grad(normed_one, grad_qk_rows, True)
-    grad_v = weight_grad(normed_one, grad_v_rows, False)
+    grad_qk = weight_grad(normed_one, grad_qk_rows)
+    grad_v = weight_grad(normed_one, grad_v_rows)
     grad_normed_one = jnp.einsum(
         "tk,dk->td", grad_qk_rows, whole_qk, preferred_element_type=single
     ) + jnp.einsum("tk,dk->td", grad_v_rows, whole_v, preferred_element_type=single)
@@ -455,8 +748,15 @@
     small = jnp.concatenate(
         [v.reshape(devices, -1) for v in vector_grads + (whole_grad_rel,)], axis=1
     )
-    small = jnp.pad(small, ((0, 0), (0, lines * 128 - packed_size)))
-    small = scatter(small.reshape(grid + (lines, 128)), True).reshape(-1)[:packed_size]
+    small = jnp.pad(small, ((0, 0), (0, small_size - packed_size))).astype(bfloat)
+    grad_out, grad_qk, grad_v, small = scatter_all(
+        (grad_out, grad_qk, grad_v, small.reshape(grid + (16, small_cols))),
+        (512, 512, 512, 256),
+        lambda number: number % 4 != 0,
+        2,
+        3,
+    )
+    small = small.reshape(-1)[:packed_size]
     small_grads = []
     at = 0
     for vector in vectors:

time: 874 us -> 632 us (0.72)
  Pallas kernels: 53.9 us -> 370 us
  waiting for transfers between devices: 320 us -> 25.7 us
  starting transfers between devices: 211 us -> 14.3 us
  other arithmetic: 108 us -> 22.3 us
  local copies, waits for them, and re-layouts: 89.7 us -> 106 us
    pallas_call x0 -> x4, Pallas kernels: none -> 317 us  [the longest x2 174 us: gather_all(): pl.pallas_call(functools.partial(gather_kernel, tuple(plan), len(shards),...]
    ppermute x36 -> x12, waiting for transfers between devices: 255 us -> 25.7 us  [swap_seq(): return lax.ppermute(value, 'seq', [(i, i ^ distance) for i in range(size)])]
    ppermute x84 -> x0, starting transfers between devices: 170 us -> none  [the longest x72 169 us: move_chips(): return lax.ppermute(value, 'win', pairs)]
    ppermute x84 -> x0, waiting for transfers between devices: 64.4 us -> none  [the longest x72 64.4 us: move_chips(): return lax.ppermute(value, 'win', pairs)]
    another operation x15 -> x5, other arithmetic: 41.2 us -> 4.82 us  [the longest x12 38.4 us: gather_cores(): jnp.stack([jnp.where(first, value, other), jnp.where(first, other, value)...]
    ppermute x36 -> x12, starting transfers between devices: 40.9 us -> 14.3 us  [swap_seq(): return lax.ppermute(value, 'seq', [(i, i ^ distance) for i in range(size)])]
    convert_element_type x30 -> x0, other arithmetic: 22.3 us -> none  [the longest x5 15.9 us: scatter_cores(): return total(pick(value, core, axis), arrived).astype(value.dtype)]
    dynamic_update_slice x18 -> x0, other arithmetic: 13.6 us -> none  [place(): lax.dynamic_update_slice_in_dim(stacked, jnp.expand_dims(piece, axis), in...]
  transfers between devices with their start and end apart: 120 -> 12, of which waited for: 48 -> 3; matrix products, arithmetic and copies ran while one was open for 20% -> 11% of each run, Pallas kernels for 2% -> 32%
where the time goes in v2:
time: 632 us; the launch traced here: 622 us
  Pallas kernels  370 us (59%)
  local copies, waits for them, and re-layouts  106 us (17%)
  matrix products  81.4 us (13%)
  waiting for transfers between devices  25.7 us (4%)
  other arithmetic  22.3 us (4%)
  starting transfers between devices  14.3 us (2%)
    pallas_call x2, Pallas kernels, gather_all(): pl.pallas_call(functools.partial(gather_kernel, tuple(plan), len(shards),...  174 us
    pallas_call x2, Pallas kernels, scatter_all(): pl.pallas_call(functools.partial(scatter_kernel, tuple(plan), tuple(array...  143 us
    pallas_call x1, Pallas kernels, attention_backward(): pl.pallas_call(functools.partial(bwd_kernel, L, bq, hp, vd), grid=(L // b...  32 us
    dot_general x5, matrix products, weight_grad(): jnp.einsum('td,te->de', left, right, preferred_element_type=single)  31.1 us
    ppermute x12, waiting for transfers between devices, swap_seq(): return lax.ppermute(value, 'seq', [(i, i ^ distance) for i in range(size)])  25.7 us
    pallas_call x1, Pallas kernels, attention_forward(): pl.pallas_call(functools.partial(fwd_kernel, L, bq, hp, vd), grid=(L // b...  21.2 us
    dynamic_update_slice x17, local copies, waits for them, and re-layouts, place(): lax.dynamic_update_slice_in_dim(stacked, jnp.expand_dims(piece, axis), in...  19.5 us
    unnamed x117, local copies, waits for them, and re-layouts  17.6 us
  transfers between devices with their start and end apart: 12, of which 3 were waited for; matrix products, arithmetic and copies ran while one was open for 11% of the time, Pallas kernels for 32%

profile of v2, /device:TPU:0, one launch (start us, length us, event | category | flops | bytes accessed | tf_op | source)
XLA Modules:
  0.0 621.5 jit_solution(5448555608993355819)
XLA Ops:
  1.5 6.1 concatenate.33
  9.7 54.6 %shard_map.313 = (bf16[4,2,2,2,16,256]{5,4,3,2,1,0:T(8,128)(2,1)}, bf16[4,2,2,2,48,1024]{5,4,3,2,1,0:T(8,128)(2,1)}, bf16[4,2,2,2,48,1536]{5,4,3,2,1,0:T(8,128)(2,1)}) custom-call(bf16[16,256]{1,0:T(8,128)(2,1)} %reshape.446.refs_0_, bf16[48,1024]{1,0:T(8,128)(2,1)} %pad_maximum_fusion.4.refs_1_, bf16[48,1536]{1,0:T(8,128)(2,1)} %refs_2_.2), custom_call_target="tpu_custom_call" | custom-call | tf_op jit(solution)/shard_map/pallas_call | solution.py:326
  68.5 3.5 fusion.70
  93.3 2.5 convolution_convert_fusion.5.tab_ref
  97.2 8.8 %collective-permute-done.1 = bf16[384,768]{1,0:T(8,128)(2,1)} collective-permute-done((bf16[384,768]{1,0:T(8,128)(2,1)}, bf16[384,768]{1,0:T(8,128)(2,1)}, u32[]{:S(2)}, u32[]{:S(2)}) %collective-permute-start.1) | collective-permute-done | bytes 589856 | tf_op jit(solution)/shard_map/ppermute | solution.py:165
  109.6 21.2 %shard_map.314 = (bf16[2,1536,1536]{2,1,0:T(8,128)(2,1)}, bf16[1536,384]{1,0:T(8,128)(2,1)}) custom-call(bf16[1536,768]{1,0:T(8,128)(2,1)} %bitcast.186, bf16[128,3072]{1,0:T(8,128)(2,1)} %convolution_convert_fusion.5.tab_ref), custom_call_target="tpu_custom_call" | custom-call | tf_op jit(solution)/shard_map/pallas_call | solution.py:74
  138.3 119.8 %shard_map.315 = (bf16[4,2,2,2,48,1536]{5,4,3,2,1,0:T(8,128)(2,1)}, bf16[4,2,2,2,48,3072]{5,4,3,2,1,0:T(8,128)(2,1)}, bf16[4,2,2,2,96,1536]{5,4,3,2,1,0:T(8,128)(2,1)}) custom-call(bf16[48,1536]{1,0:T(8,128)(2,1)} %refs_0_.1, bf16[48,3072]{1,0:T(8,128)(2,1)} %refs_1_.1, bf16[96,1536]{1,0:T(8,128)(2,1)} %refs_2_.3), custom_call_target="tpu_custom_call" | custom-call | tf_op jit(solution)/shard_map/pallas_call | solution.py:326
  263.1 11.4 %collective-permute-done.4 = bf16[384,384]{0,1:T(8,128)(2,1)} collective-permute-done((bf16[384,384]{0,1:T(8,128)(2,1)S(1)}, bf16[384,384]{0,1:T(8,128)(2,1)}, u32[]{:S(2)}, u32[]{:S(2)}) %collective-permute-start.4) | collective-permute-done | bytes 294944 | tf_op jit(solution)/shard_map/ppermute | solution.py:165
  275.6 5.0 fusion.82
  281.4 4.1 convolution_add_fusion
  285.5 8.2 %convolution_convert_fusion.1 = bf16[3072,1536]{1,0:T(8,128)(2,1)} fusion(bf16[1,384,1536]{2,1,0:T(8,128)(2,1)S(1)} %copy-done.2, f32[384,3072]{1,0:T(8,128)S(1)} %convolution_add_fusion), kind=kOutput, calls=%fused_computation.1 | convolution fusion | flops 3639214080 | bytes 15335424 | tf_op jit(solution)/shard_map/td,te->de/dot_general | solution.py:680
  293.7 8.2 %fusion.83 = (bf16[3072]{0:T(1024)(128)(2,1)}, bf16[384,3072]{1,0:T(8,128)(2,1)}) fusion(f32[384,3072]{1,0:T(8,128)S(1)} %convolution_add_fusion, bf16[3072,1536]{1,0:T(8,128)(2,1)S(1)} %bitcast.237, bf16[1,384,1536]{2,1,0:T(8,128)(2,1)S(1)} %copy-done.2), kind=kOutput, calls=%fused_computation.183 | convolution fusion | flops 3648648192 | bytes 17700864 | tf_op jit(solution)/shard_map/td,fd->tf/dot_general | solution.py:687
  301.9 8.8 %multiply_reduce_fusion = (bf16[1536]{0:T(1024)(128)(2,1)S(1)}, f32[384]{0:T(512)S(1)}, bf16[1536]{0:T(1024)(128)(2,1)S(1)}, f32[384,1536]{1,0:T(8,128)S(1)}) fusion(f32[384,1536]{1,0:T(8,128)S(1)} %get-tuple-element.117, f32[384]{0:T(512)S(1)} %fusion.58, f32[384]{0:T(512)S(1)} %broadcast_multiply_fusion, f32[1536]{0:T(1024)S(1)} %copy-done.16, ...), kind=kOutput, calls=%fused_computation.57 | convolution fusion | flops 3628593664 | bytes 16531968 | tf_op jit(solution)/shard_map/tf,df->td/dot_general | solution.py:694
  310.7 8.0 %convolution_convert_fusion = bf16[1536,3072]{1,0:T(8,128)(2,1)} fusion(bf16[384,3072]{1,0:T(8,128)(2,1)S(1)} %copy-done.37, f32[384,1536]{1,0:T(8,128)S(1)} %get-tuple-element.117, f32[1536]{0:T(1024)S(1)} %copy-done.35, f32[1536]{0:T(1024)S(1)} %copy-done.16, f32[384]{0:T(512)S(1)} %fusion.58, f32[384]{0:T(512)S(1)} %broadcast_multiply_fusion), kind=kOutput, calls=%fused_computation | convolution fusion | flops 3631546368 | bytes 14171136 | tf_op jit(solution)/shard_map/td,te->de/dot_general | solution.py:680
  318.7 5.1 fusion.20
  326.6 3.1 convolution_convert_fusion.6
  329.7 3.3 reshape.463
  333.0 6.3 %constant_dynamic-slice_fusion.4 = (bf16[384,1,384]{2,1,0:T(2,128)(2,1)}, bf16[384,1,384]{2,1,0:T(2,128)(2,1)}, bf16[384,1,384]{2,1,0:T(2,128)(2,1)}, bf16[384,1,384]{2,1,0:T(2,128)(2,1)}) fusion(bf16[384,4,384]{2,1,0:T(4,128)(2,1)} %reshape.463, s32[]{:T(128)S(6)} %select_n.52, s32[]{:T(128)S(6)} %select_n.51, s32[]{:T(128)S(6)} %select_n.50, s32[]{:T(128)S(6)} %select_n.49), kind=kLoop, calls=%fused_computation.126 | loop fusion | bytes 2359312 | tf_op jit(solution)/shard_map/dynamic-slice.7
  339.3 2.8 copy.88
  343.4 6.3 %convolution_convert_fusion.3 = bf16[1536,1536]{1,0:T(8,128)(2,1)} fusion(bf16[384,1536]{0,1:T(8,128)(2,1)} %bitcast.195, bf16[384,1536]{1,0:T(8,128)(2,1)} %copy-done.7), kind=kOutput, calls=%fused_computation.3 | convolution fusion | flops 1814298624 | bytes 7077888 | tf_op jit(solution)/shard_map/td,te->de/dot_general | solution.py:680
  352.3 2.8 copy.89
  355.8 2.8 copy.90
  365.7 81.5 %shard_map.318 = (f32[96,1536]{1,0:T(8,128)}, f32[48,3072]{1,0:T(8,128)}) custom-call(bf16[4,2,2,2,96,1536]{5,4,3,2,1,0:T(8,128)(2,1)} %bitcast.192, bf16[4,2,2,2,48,3072]{5,4,3,2,1,0:T(8,128)(2,1)} %bitcast.193), custom_call_target="tpu_custom_call" | custom-call | tf_op jit(solution)/shard_map/pallas_call | solution.py:534
  452.4 2.4 copy.75
  454.7 32.0 %shard_map.316 = (bf16[1536,128]{1,0:T(8,128)(2,1)}, bf16[1536,512]{1,0:T(8,128)(2,1)}, f32[128,3072]{1,0:T(8,128)}, f32[8,128]{1,0:T(8,128)}) custom-call(bf16[1536,768]{1,0:T(8,128)(2,1)} %bitcast.187, bf16[128,3072]{1,0:T(8,128)(2,1)} %convolution_convert_fusion.5.tab_ref, bf16[2,1536,1536]{2,1,0:T(8,128)(2,1)} %get-tuple-element.45.att_ref, ...), custom_call_target="tpu_custom_call" | custom-call | tf_op jit(solution)/shard_map/pallas_call | solution.py:141
  502.0 3.6 convolution_dynamic-update-slice_fusion
  513.1 5.6 collective-permute-done.10
  523.3 3.7 convolution_convert_fusion.4
  527.0 4.8 convolution_convert_fusion.2
  531.8 3.0 fusion.72
  544.3 61.2 %shard_map.317 = (f32[48,1536]{1,0:T(8,128)}, f32[48,1024]{1,0:T(8,128)}, f32[48,1536]{1,0:T(8,128)}, f32[16,256]{1,0:T(8,128)}) custom-call(bf16[4,2,2,2,48,1536]{5,4,3,2,1,0:T(8,128)(2,1)} %bitcast.199, bf16[4,2,2,2,48,1024]{5,4,3,2,1,0:T(8,128)(2,1)} %bitcast.202, bf16[4,2,2,2,48,1536]{5,4,3,2,1,0:T(8,128)(2,1)} %bitcast.200, ...), custom_call_target="tpu_custom_call" | custom-call | tf_op jit(solution)/shard_map/pallas_call | solution.py:534
  608.7 4.5 add_bitcast_fusion
  (248 shorter events, 115.1 us)
Async XLA Ops:
  0.7 67.2 %copy-start = (bf16[1,384,1536]{2,1,0:T(8,128)(2,1)S(1)}, bf16[1,384,1536]{2,1,0:T(8,128)(2,1)}, u32[]{:S(2)}) copy-start(bf16[1,384,1536]{2,1,0:T(8,128)(2,1)} %param.22) | copy-start | bytes 3538948
  76.4 19.6 %collective-permute-start = (bf16[384,768]{1,0:T(8,128)(2,1)}, bf16[384,768]{1,0:T(8,128)(2,1)}, u32[]{:S(2)}, u32[]{:S(2)}) collective-permute-start(bf16[384,768]{1,0:T(8,128)(2,1)} %get-tuple-element.72), channel_id=1, source_target_pairs={{0,1},{1,0},{2,3},{3,2},{4,5},{5,4},{6,7},{7,6},{8,9},{9,8},{10,11... | collective-permute-start | bytes 1769480 | tf_op jit(solution)/shard_map/ppermute | solution.py:165
  77.6 28.3 %collective-permute-start.1 = (bf16[384,768]{1,0:T(8,128)(2,1)}, bf16[384,768]{1,0:T(8,128)(2,1)}, u32[]{:S(2)}, u32[]{:S(2)}) collective-permute-start(bf16[384,768]{1,0:T(8,128)(2,1)} %get-tuple-element.71), channel_id=1, source_target_pairs={{0,2},{1,3},{2,0},{3,1},{4,6},{5,7},{6,4},{7,5},{8,10},{9,11},{10,... | collective-permute-start | bytes 1769480 | tf_op jit(solution)/shard_map/ppermute | solution.py:165
  78.5 28.6 %collective-permute-start.2 = (bf16[384,768]{1,0:T(8,128)(2,1)}, bf16[384,768]{1,0:T(8,128)(2,1)}, u32[]{:S(2)}, u32[]{:S(2)}) collective-permute-start(bf16[384,768]{1,0:T(8,128)(2,1)} %get-tuple-element.70), channel_id=1, source_target_pairs={{0,3},{1,2},{2,1},{3,0},{4,7},{5,6},{6,5},{7,4},{8,11},{9,10},{10,... | collective-permute-start | bytes 1769480 | tf_op jit(solution)/shard_map/ppermute | solution.py:165
  109.6 27.1 %copy-start.13 = (f32[32,48]{1,0:T(8,128)S(1)}, f32[32,48]{1,0:T(8,128)}, u32[]{:S(2)}) copy-start(f32[32,48]{1,0:T(8,128)} %get-tuple-element.89) | copy-start | bytes 18436
  109.6 27.8 %copy-start.2 = (bf16[1,384,1536]{2,1,0:T(8,128)(2,1)S(1)}, bf16[1,384,1536]{2,1,0:T(8,128)(2,1)}, u32[]{:S(2)}) copy-start(bf16[1,384,1536]{2,1,0:T(8,128)(2,1)} %param.23) | copy-start | bytes 3538948
  133.1 128.8 %collective-permute-start.3 = (bf16[384,384]{0,1:T(8,128)(2,1)}, bf16[384,384]{0,1:T(8,128)(2,1)}, u32[]{:S(2)}, u32[]{:S(2)}) collective-permute-start(bf16[384,384]{0,1:T(8,128)(2,1)} %bitcast.224), channel_id=1, source_target_pairs={{0,1},{1,0},{2,3},{3,2},{4,5},{5,4},{6,7},{7,6},{8,9},{9,8},{10,11... | collective-permute-start | bytes 884744 | tf_op jit(solution)/shard_map/ppermute | solution.py:165
  258.3 17.3 %copy-start.15 = (f32[1536]{0:T(1024)S(1)}, f32[1536]{0:T(1024)}, u32[]{:S(2)}) copy-start(f32[1536]{0:T(1024)} %reshape.492) | copy-start | bytes 18436
  258.5 15.9 %collective-permute-start.4 = (bf16[384,384]{0,1:T(8,128)(2,1)S(1)}, bf16[384,384]{0,1:T(8,128)(2,1)}, u32[]{:S(2)}, u32[]{:S(2)}) collective-permute-start(bf16[384,384]{0,1:T(8,128)(2,1)S(1)} %bitcast.225), channel_id=1, source_target_pairs={{0,2},{1,3},{2,0},{3,1},{4,6},{5,7},{6,4},{7,5},{8,10},{9,11},{10,... | collective-permute-start | bytes 884744 | tf_op jit(solution)/shard_map/ppermute | solution.py:165
  260.2 15.3 %collective-permute-start.5 = (bf16[384,384]{0,1:T(8,128)(2,1)S(1)}, bf16[384,384]{0,1:T(8,128)(2,1)S(1)}, u32[]{:S(2)}, u32[]{:S(2)}) collective-permute-start(bf16[384,384]{0,1:T(8,128)(2,1)S(1)} %bitcast.226), channel_id=1, source_target_pairs={{0,3},{1,2},{2,1},{3,0},{4,7},{5,6},{6,5},{7,4},{8,11},{9,10},{10,... | collective-permute-start | bytes 884744 | tf_op jit(solution)/shard_map/ppermute | solution.py:165
  261.9 19.2 %slice-start.5 = ((s8[9437184]{0:T(1024)(128)(4,1)}), s8[4194304]{0:T(1024)(128)(4,1)S(1)}, s32[]{:S(2)}) async-start(s8[9437184]{0:T(1024)(128)(4,1)} %bitcast.240), calls=%async_computation.5 | async-start | bytes 8388608
  281.4 12.3 %slice-start.2 = ((s8[9437184]{0:T(1024)(128)(4,1)}), s8[4194304]{0:T(1024)(128)(4,1)S(1)}, s32[]{:S(2)}) async-start(s8[9437184]{0:T(1024)(128)(4,1)} %bitcast.235), calls=%async_computation.2 | async-start | bytes 8388608
  281.4 12.3 %slice-start.3 = ((s8[9437184]{0:T(1024)(128)(4,1)}), s8[4194304]{0:T(1024)(128)(4,1)S(1)}, s32[]{:S(2)}) async-start(s8[9437184]{0:T(1024)(128)(4,1)} %bitcast.235), calls=%async_computation.3 | async-start | bytes 8388608
  285.4 8.2 %copy-start.38 = (f32[384,3072]{1,0:T(8,128)}, f32[384,3072]{1,0:T(8,128)S(1)}, u32[]{:S(2)}) copy-start(f32[384,3072]{1,0:T(8,128)S(1)} %convolution_add_fusion) | copy-start | bytes 14155780
  285.4 8.2 %slice-start.4 = ((s8[9437184]{0:T(1024)(128)(4,1)}), s8[1048576]{0:T(1024)(128)(4,1)S(1)}, s32[]{:S(2)}) async-start(s8[9437184]{0:T(1024)(128)(4,1)} %bitcast.235), calls=%async_computation.4 | async-start | bytes 2097152
  301.9 8.8 %copy-start.37 = (bf16[384,3072]{1,0:T(8,128)(2,1)S(1)}, bf16[384,3072]{1,0:T(8,128)(2,1)}, u32[]{:S(2)}) copy-start(bf16[384,3072]{1,0:T(8,128)(2,1)} %get-tuple-element.121) | copy-start | bytes 7077892
  310.6 8.1 %copy-start.34 = (f32[1536]{0:T(1024)S(1)}, f32[1536]{0:T(1024)}, u32[]{:S(2)}) copy-start(f32[1536]{0:T(1024)} %reshape.496) | copy-start | bytes 18436
  310.7 8.1 %copy-start.39 = (f32[384,3072]{1,0:T(8,128)S(1)}, f32[384,3072]{1,0:T(8,128)}, u32[]{:S(2)}) copy-start(f32[384,3072]{1,0:T(8,128)} %copy-done.38) | copy-start | bytes 14155780
  310.7 16.0 %slice-start = ((s8[4718592]{0:T(1024)(128)(4,1)}), s8[4194304]{0:T(1024)(128)(4,1)S(1)}, s32[]{:S(2)}) async-start(s8[4718592]{0:T(1024)(128)(4,1)} %bitcast.189), calls=%async_computation | async-start | bytes 8388608
  318.7 7.9 %slice-start.1 = ((s8[4718592]{0:T(1024)(128)(4,1)}), s8[524288]{0:T(1024)(128)(4,1)S(1)}, s32[]{:S(2)}) async-start(s8[4718592]{0:T(1024)(128)(4,1)} %bitcast.189), calls=%async_computation.1 | async-start | bytes 1048576
  342.0 105.2 %collective-permute-start.6 = (bf16[384,384]{0,1:T(8,128)(2,1)}, bf16[384,384]{0,1:T(8,128)(2,1)}, u32[]{:S(2)}, u32[]{:S(2)}) collective-permute-start(bf16[384,384]{0,1:T(8,128)(2,1)} %bitcast.221), channel_id=1, source_target_pairs={{0,1},{1,0},{2,3},{3,2},{4,5},{5,4},{6,7},{7,6},{8,9},{9,8},{10,11... | collective-permute-start | bytes 884744 | tf_op jit(solution)/shard_map/ppermute | solution.py:165
  355.1 93.8 %collective-permute-start.7 = (bf16[384,384]{0,1:T(8,128)(2,1)}, bf16[384,384]{0,1:T(8,128)(2,1)}, u32[]{:S(2)}, u32[]{:S(2)}) collective-permute-start(bf16[384,384]{0,1:T(8,128)(2,1)} %bitcast.222), channel_id=1, source_target_pairs={{0,2},{1,3},{2,0},{3,1},{4,6},{5,7},{6,4},{7,5},{8,10},{9,11},{10,... | collective-permute-start | bytes 884744 | tf_op jit(solution)/shard_map/ppermute | solution.py:165
  358.6 92.1 %collective-permute-start.8 = (bf16[384,384]{0,1:T(8,128)(2,1)}, bf16[384,384]{0,1:T(8,128)(2,1)}, u32[]{:S(2)}, u32[]{:S(2)}) collective-permute-start(bf16[384,384]{0,1:T(8,128)(2,1)} %bitcast.223), channel_id=1, source_target_pairs={{0,3},{1,2},{2,1},{3,0},{4,7},{5,6},{6,5},{7,4},{8,11},{9,10},{10,... | collective-permute-start | bytes 884744 | tf_op jit(solution)/shard_map/ppermute | solution.py:165
  493.8 18.2 %collective-permute-start.9 = (bf16[384,640]{0,1:T(8,128)(2,1)}, bf16[384,640]{0,1:T(8,128)(2,1)}, u32[]{:S(2)}, u32[]{:S(2)}) collective-permute-start(bf16[384,640]{0,1:T(8,128)(2,1)} %bitcast.216), channel_id=1, source_target_pairs={{0,1},{1,0},{2,3},{3,2},{4,5},{5,4},{6,7},{7,6},{8,9},{9,8},{10,11... | collective-permute-start | bytes 1474568 | tf_op jit(solution)/shard_map/ppermute | solution.py:165
  497.0 21.6 %collective-permute-start.10 = (bf16[384,640]{0,1:T(8,128)(2,1)}, bf16[384,640]{0,1:T(8,128)(2,1)}, u32[]{:S(2)}, u32[]{:S(2)}) collective-permute-start(bf16[384,640]{0,1:T(8,128)(2,1)} %bitcast.215), channel_id=1, source_target_pairs={{0,2},{1,3},{2,0},{3,1},{4,6},{5,7},{6,4},{7,5},{8,10},{9,11},{10,... | collective-permute-start | bytes 1474568 | tf_op jit(solution)/shard_map/ppermute | solution.py:165
  499.9 19.9 %collective-permute-start.11 = (bf16[384,640]{0,1:T(8,128)(2,1)}, bf16[384,640]{0,1:T(8,128)(2,1)}, u32[]{:S(2)}, u32[]{:S(2)}) collective-permute-start(bf16[384,640]{0,1:T(8,128)(2,1)} %bitcast.214), channel_id=1, source_target_pairs={{0,3},{1,2},{2,1},{3,0},{4,7},{5,6},{6,5},{7,4},{8,11},{9,10},{10,... | collective-permute-start | bytes 1474568 | tf_op jit(solution)/shard_map/ppermute | solution.py:165
  523.3 8.5 %slice-start.10 = ((s8[4718592]{0:T(1024)(128)(4,1)}), s8[4194304]{0:T(1024)(128)(4,1)S(1)}, s32[]{:S(2)}) async-start(s8[4718592]{0:T(1024)(128)(4,1)} %bitcast.246), calls=%async_computation.10 | async-start | bytes 8388608
  544.2 64.4 %copy-start.30 = (f32[384]{0:T(512)S(1)}, f32[384]{0:T(512)}, u32[]{:S(2)}) copy-start(f32[384]{0:T(512)} %get-tuple-element.59) | copy-start | bytes 4612
  544.2 64.4 %copy-start.19 = (f32[384]{0:T(512)S(1)}, f32[384]{0:T(512)}, u32[]{:S(2)}) copy-start(f32[384]{0:T(512)} %copy-done.17) | copy-start | bytes 4612
  544.2 64.4 %copy-start.23 = (f32[384]{0:T(512)S(1)}, f32[384]{0:T(512)}, u32[]{:S(2)}) copy-start(f32[384]{0:T(512)} %copy-done.22) | copy-start | bytes 4612
  544.2 64.4 %copy-start.25 = (f32[384]{0:T(512)S(1)}, f32[384]{0:T(512)}, u32[]{:S(2)}) copy-start(f32[384]{0:T(512)} %copy-done.24) | copy-start | bytes 4612
  544.2 64.4 %copy-start.28 = (f32[384]{0:T(512)S(1)}, f32[384]{0:T(512)}, u32[]{:S(2)}) copy-start(f32[384]{0:T(512)} %copy-done.26) | copy-start | bytes 4612
  (32 other events, 103.3 us)

commit v3 on v2

--- a/solution.py
+++ b/solution.py
@@ -14,6 +14,7 @@
 WLEN = 1536
 CORES = 2
 BLOCK_Q = 256
+FIRST_BLOCK_TURN = 8
 bfloat = jnp.bfloat16
 single = jnp.float32
 
@@ -46,39 +47,28 @@
     return centered * lax.rsqrt(variance + 1e-05) * norm_gain + norm_shift
 
 
-def fwd_kernel(L, bq, hp, vd, x_ref, tab_ref, att_ref, out_ref):
-    qi = pl.program_id(0)
+def attend_block(length, bq, hp, vd, block, x_ref, tab_ref, att_ref, mixed_ref):
     hk = hp * KD
-    i0 = pl.multiple_of(qi * bq, bq)
-    a = pl.multiple_of(L - bq - i0, bq)
-    W = L + bq
+    first = block * bq
+    rows = pl.ds(first, bq)
+    span = length + bq
     outs = []
     for h in range(hp):
-        qc = x_ref[pl.ds(i0, bq), pl.ds(h * KD, KD)]
-        qp = x_ref[pl.ds(i0, bq), pl.ds(hk + h * KD, KD)]
+        qc = x_ref[rows, pl.ds(h * KD, KD)]
+        qp = x_ref[rows, pl.ds(hk + h * KD, KD)]
         k = x_ref[:, pl.ds(2 * hk + h * KD, KD)]
         v = x_ref[:, pl.ds(3 * hk + h * vd, vd)]
-        raw = jnp.dot(qp, tab_ref[pl.ds(h * KD, KD), pl.ds(a, W)], preferred_element_type=jnp.float32)
-        rel = pltpu.roll(raw, W - bq + 1, 1, stride=1, stride_axis=0)[:, :L]
-        s = rel + lax.dot_general(qc, k, (((1,), (1,)), ((), ())), preferred_element_type=jnp.float32)
-        m = jnp.max(s, axis=-1, keepdims=True)
-        e = jnp.exp(s - m)
-        inv = 1.0 / jnp.sum(e, axis=-1, keepdims=True)
-        att = (e * inv).astype(jnp.bfloat16)
+        table = tab_ref[pl.ds(h * KD, KD), pl.ds(length - bq - first, span)]
+        raw = jnp.dot(qp, table, preferred_element_type=single)
+        rel = pltpu.roll(raw, span - bq + 1, 1, stride=1, stride_axis=0)[:, :length]
+        s = rel + lax.dot_general(qc, k, (((1,), (1,)), ((), ())), preferred_element_type=single)
+        e = jnp.exp(s - jnp.max(s, axis=-1, keepdims=True))
+        inverse = 1.0 / jnp.sum(e, axis=-1, keepdims=True)
+        att = (e * inverse).astype(bfloat)
         att_ref[h] = att
-        outs.append(jnp.dot(att, v, preferred_element_type=jnp.float32).astype(jnp.bfloat16))
-    out_ref[...] = jnp.concatenate(outs, axis=1) if hp > 1 else outs[0]
-
-def attention_forward(x, tab, hp, vd, bq):
-    L = x.shape[0]
-    return pl.pallas_call(
-        functools.partial(fwd_kernel, L, bq, hp, vd),
-        grid=(L // bq,),
-        in_specs=[pl.BlockSpec(x.shape, lambda i: (0, 0)), pl.BlockSpec(tab.shape, lambda i: (0, 0))],
-        out_specs=[pl.BlockSpec((hp, bq, L), lambda i: (0, i, 0)), pl.BlockSpec((bq, hp * vd), lambda i: (i, 0))],
-        out_shape=[jax.ShapeDtypeStruct((hp, L, L), jnp.bfloat16), jax.ShapeDtypeStruct((L, hp * vd), jnp.bfloat16)],
-        compiler_params=pltpu.CompilerParams(vmem_limit_bytes=56 * 2**20),
-    )(x, tab)
+        outs.append(jnp.dot(att, v, preferred_element_type=single).astype(bfloat))
+    mixed_ref[rows, :] = jnp.concatenate(outs, axis=1) if hp > 1 else outs[0]
+
 
 def bwd_kernel(L, bq, hp, vd, x_ref, tab_ref, att_ref, gm_ref, dq_ref, dkv_ref, dtab_ref, bias_ref, dkT, dvT):
     qi = pl.program_id(0)
@@ -172,7 +162,7 @@
     return win, seq, win // CORES, win % CORES, chips, bits
 
 
-def start_together():
+def start_together(whole_seq=False):
     win, seq, here, core, chips, bits = partners()
     barrier = pltpu.get_barrier_semaphore()
 
@@ -182,8 +172,9 @@
         )
 
     greet(win ^ 1, seq)
-    for bit in range(bits):
-        greet(win, seq ^ (1 << bit))
+    across = range(1, 1 << bits) if whole_seq else [1 << bit for bit in range(bits)]
+    for distance in across:
+        greet(win, seq ^ distance)
 
     @pl.when(here > 0)
     def _():
@@ -194,12 +185,10 @@
         greet(win + CORES, seq)
 
     ends = jnp.where(here > 0, 1, 0) + jnp.where(here < chips - 1, 1, 0)
-    pl.semaphore_wait(barrier, 1 + bits + ends)
-
-
-def gather_kernel(plan, count, spacing, *refs):
-    shards, outs = refs[:count], refs[count : 2 * count]
-    send_sem, recv_sem, local_sem = refs[2 * count :]
+    pl.semaphore_wait(barrier, 1 + len(across) + ends)
+
+
+def gather_work(plan, shards, outs, send_sem, recv_sem, local_sem):
     win, seq, here, core, chips, bits = partners()
     own_bits = tuple((seq >> bit) & 1 for bit in reversed(range(bits)))
     own_seq = {bit: (seq >> bit) & 1 for bit in range(bits)}
@@ -292,51 +281,212 @@
         line = [chip_stage(chunk, number, step, every_bit) for step in range(chip_steps)]
         return cube + line + [core_stage(chunk, number)]
 
-    locals_ = []
-    for which in range(count):
-        target = outs[which].at[(here, core) + own_bits]
-        locals_.append(pltpu.make_async_copy(shards[which], target, local_sem.at[which]))
-    for item in locals_:
+    own = [
+        pltpu.make_async_copy(shard, out.at[(here, core) + own_bits], local_sem.at[which])
+        for which, (shard, out) in enumerate(zip(shards, outs))
+    ]
+    return own, [stages(chunk, number) for number, chunk in enumerate(plan)]
+
+
+def run_turn(work, spacing, turn, last=None):
+    for number, stages in enumerate(work):
+        at, off = divmod(turn - number, spacing)
+        if off == 0 and 0 < at <= len(stages):
+            stages[at - 1][1]()
+            if at == len(stages) and last is not None:
+                last(number)
+        if off == 0 and 0 <= at < len(stages):
+            stages[at][0]()
+
+
+def turns_of(work, spacing):
+    return len(work) + spacing * len(work[0])
+
+
+def finish_sends(work):
+    for stages in work:
+        for stage in stages:
+            stage[2]()
+
+
+def gather_kernel(plan, count, spacing, *refs):
+    shards, outs, sems = refs[:count], refs[count : 2 * count], refs[2 * count :]
+    own, work = gather_work(plan, shards, outs, *sems)
+    for item in own:
         item.start()
     start_together()
-    for item in locals_:
+    for item in own:
         item.wait()
-    work = [stages(chunk, number) for number, chunk in enumerate(plan)]
-    depth = chip_steps + bits + 1
-    for turn in range(len(plan) + spacing * depth):
-        for number in range(len(plan)):
-            at, off = divmod(turn - number, spacing)
-            if off == 0 and 0 < at <= depth:
-                work[number][at - 1][1]()
-            if off == 0 and 0 <= at < depth:
-                work[number][at][0]()
-    for items in work:
-        for item in items:
-            item[2]()
-
-
-def gather_all(shards, widths, lines_first, spacing, collective_id):
-    chips = lax.axis_size("win") // CORES
-    bits = lax.axis_size("seq").bit_length() - 1
+    for turn in range(turns_of(work, spacing)):
+        run_turn(work, spacing, turn)
+    finish_sends(work)
+
+
+def gather_plan(shards, widths, lines_first):
     plan = []
     for which, (shard, width) in enumerate(zip(shards, widths)):
         for col in range(0, shard.shape[1], width):
             plan.append((which, col, width, lines_first(len(plan))))
+    return tuple(plan)
+
+
+def gather_sems(plan, count):
+    chips = lax.axis_size("win") // CORES
+    bits = lax.axis_size("seq").bit_length() - 1
     kinds = 2 * (chips - 1) + 2 * bits + 1
+    return [
+        pltpu.SemaphoreType.DMA((len(plan), kinds)),
+        pltpu.SemaphoreType.DMA((len(plan), kinds)),
+        pltpu.SemaphoreType.DMA((count,)),
+    ]
+
+
+def gathered_shapes(shards):
+    chips = lax.axis_size("win") // CORES
+    bits = lax.axis_size("seq").bit_length() - 1
+    return [jax.ShapeDtypeStruct((chips, CORES) + (2,) * bits + s.shape, s.dtype) for s in shards]
+
+
+def gather_all(shards, widths, lines_first, spacing, collective_id):
+    plan = gather_plan(shards, widths, lines_first)
     return pl.pallas_call(
-        functools.partial(gather_kernel, tuple(plan), len(shards), spacing),
-        in_specs=[pl.BlockSpec(memory_space=pl.ANY)] * len(shards),
+        functools.partial(gather_kernel, plan, len(shards), spacing),
+        in_specs=[pl.BlockSpec(memory_space=pltpu.VMEM)] * len(shards),
         out_specs=[pl.BlockSpec(memory_space=pl.ANY)] * len(shards),
-        out_shape=[
-            jax.ShapeDtypeStruct((chips, CORES) + (2,) * bits + s.shape, s.dtype) for s in shards
+        out_shape=gathered_shapes(shards),
+        scratch_shapes=gather_sems(plan, len(shards)),
+        compiler_params=pltpu.CompilerParams(collective_id=collective_id, has_side_effects=True),
+    )(*shards)
+
+
+def exchange_work(parts, target, send_sem, recv_sem, local_sem):
+    win, seq = lax.axis_index("win"), lax.axis_index("seq")
+    items = []
+    for peer, part in enumerate(parts):
+        sent = pltpu.make_async_remote_copy(
+            src_ref=part,
+            dst_ref=target(seq),
+            send_sem=send_sem.at[peer],
+            recv_sem=recv_sem.at[seq],
+            device_id=(win, peer),
+            device_id_type=pl.DeviceIdType.MESH,
+        )
+        got = pltpu.make_async_remote_copy(
+            src_ref=part,
+            dst_ref=target(peer),
+            send_sem=send_sem.at[peer],
+            recv_sem=recv_sem.at[peer],
+            device_id=(win, peer),
+            device_id_type=pl.DeviceIdType.MESH,
+        )
+        own = pltpu.make_async_copy(part, target(peer), local_sem.at[peer])
+
+        def start(peer=peer, sent=sent, own=own):
+            pl.when(peer != seq)(sent.start)
+            pl.when(peer == seq)(own.start)
+
+        def arrive(peer=peer, got=got, own=own):
+            pl.when(peer != seq)(got.wait_recv)
+            pl.when(peer == seq)(own.wait)
+
+        def finish(peer=peer, sent=sent):
+            pl.when(peer != seq)(sent.wait_send)
+
+        items.append((start, arrive, finish))
+    return items
+
+
+def attend_kernel(plan, count, spacing, first_turn, dims, *refs):
+    hp, vd, bq = dims
+    shards, (outgoing, tab_ref), refs = refs[:count], refs[count : count + 2], refs[count + 2 :]
+    outs, (x_ref, att_out, attended), refs = refs[:count], refs[count : count + 3], refs[count + 3 :]
+    att_ref, mixed_ref, *gather_refs = refs[:-7]
+    in_send, in_recv, in_local, out_send, out_recv, out_local, att_sem = refs[-7:]
+    length = x_ref.shape[0]
+    peers, rows = outgoing.shape[0], outgoing.shape[1]
+    own, work = gather_work(plan, shards, outs, *gather_refs)
+    incoming = exchange_work(
+        [outgoing.at[peer] for peer in range(peers)],
+        lambda peer: x_ref.at[pl.ds(peer * rows, rows)],
+        in_send,
+        in_recv,
+        in_local,
+    )
+    leaving = exchange_work(
+        [mixed_ref.at[pl.ds(peer * rows, rows)] for peer in range(peers)],
+        lambda peer: attended.at[peer],
+        out_send,
+        out_recv,
+        out_local,
+    )
+    for item in own:
+        item.start()
+    start_together(True)
+    for item in own:
+        item.wait()
+    for start, _, _ in incoming:
+        start()
+    blocks = length // bq
+    kept = [
+        pltpu.make_async_copy(
+            att_ref.at[block % 2], att_out.at[:, pl.ds(block * bq, bq)], att_sem.at[block]
+        )
+        for block in range(blocks)
+    ]
+    sent = 0
+    for turn in range(turns_of(work, spacing)):
+        run_turn(work, spacing, turn)
+        block = turn - first_turn
+        if block == 0:
+            for _, arrive, _ in incoming:
+                arrive()
+        if 0 <= block < blocks:
+            if block >= 2:
+                kept[block - 2].wait()
+            attend_block(length, bq, hp, vd, block, x_ref, tab_ref, att_ref.at[block % 2], mixed_ref)
+            kept[block].start()
+            while sent < peers and (sent + 1) * rows <= (block + 1) * bq:
+                leaving[sent][0]()
+                sent += 1
+    for _, arrive, _ in leaving:
+        arrive()
+    for _, _, finish in incoming + leaving:
+        finish()
+    for item in kept[-2:]:
+        item.wait()
+    finish_sends(work)
+
+
+def gather_and_attend(shards, widths, lines_first, spacing, first_turn, outgoing, tab, dims):
+    hp, vd, bq = dims
+    peers, rows, cols = outgoing.shape
+    length = peers * rows
+    plan = gather_plan(shards, widths, lines_first)
+    count = len(shards)
+    anywhere = pl.BlockSpec(memory_space=pl.ANY)
+    vmem = pl.BlockSpec(memory_space=pltpu.VMEM)
+    dma = pltpu.SemaphoreType.DMA
+    return pl.pallas_call(
+        functools.partial(attend_kernel, plan, count, spacing, first_turn, dims),
+        in_specs=[vmem] * count + [anywhere, vmem],
+        out_specs=[anywhere] * count + [vmem, anywhere, vmem],
+        out_shape=gathered_shapes(shards)
+        + [
+            jax.ShapeDtypeStruct((length, cols), bfloat),
+            jax.ShapeDtypeStruct((hp, length, length), bfloat),
+            jax.ShapeDtypeStruct((peers, rows, hp * vd), bfloat),
         ],
         scratch_shapes=[
-            pltpu.SemaphoreType.DMA((len(plan), kinds)),
-            pltpu.SemaphoreType.DMA((len(plan), kinds)),
-            pltpu.SemaphoreType.DMA((len(shards),)),
-        ],
-        compiler_params=pltpu.CompilerParams(collective_id=collective_id, has_side_effects=True),
-    )(*shards)
+            pltpu.VMEM((2, hp, bq, length), bfloat),
+            pltpu.VMEM((length, hp * vd), bfloat),
+        ]
+        + gather_sems(plan, count)
+        + [dma((peers,))] * 6
+        + [dma((length // bq,))],
+        compiler_params=pltpu.CompilerParams(
+            collective_id=1, has_side_effects=True, vmem_limit_bytes=56 * 2**20
+        ),
+    )(*shards, outgoing, tab)
 
 
 def scatter_kernel(plan, arrays, spacing, *refs):
@@ -488,25 +638,18 @@
         cube = [bit_stage(chunk, number, step, here) for step in range(bits)]
         return [core_stage(chunk, number)] + line + cube
 
+    def last(number):
+        chunk = plan[number]
+        which, slot, _ = chunk
+        width = arrays[which][1]
+        total = slabs(chunk, here, own_seq)[...].astype(single)
+        outs[which][:, pl.ds(slot * width, width)] = total
+
     start_together()
     work = [stages(chunk, number) for number, chunk in enumerate(plan)]
-    depth = chip_steps + bits + 1
-    for turn in range(len(plan) + spacing * depth):
-        for number, chunk in enumerate(plan):
-            at, off = divmod(turn - number, spacing)
-            if off == 0 and 0 < at <= depth:
-                work[number][at - 1][1]()
-                if at == depth:
-                    which, slot, _ = chunk
-                    width = arrays[which][1]
-                    outs[which][:, pl.ds(slot * width, width)] = slabs(chunk, here, own_seq)[
-                        ...
-                    ].astype(single)
-            if off == 0 and 0 <= at < depth:
-                work[number][at][0]()
-    for items in work:
-        for item in items:
-            item[2]()
+    for turn in range(turns_of(work, spacing)):
+        run_turn(work, spacing, turn, last)
+    finish_sends(work)
 
 
 def scatter_all(grads, widths, lines_last, spacing, collective_id):
@@ -618,12 +761,6 @@
     packed = packed.reshape(devices, small_size)
     whole_qk = whole_qk.reshape(width, 2 * hk)
     whole_v = whole_v.reshape(width, width)
-    whole_out, whole_in, whole_mlp = gather_all(
-        (w_out, w_in, w_mlp_out), (512, 512, 256), lambda number: number % 4 != 3, 2, 1
-    )
-    whole_out = whole_out.reshape(width, width)
-    whole_in = whole_in.reshape(width, hidden)
-    whole_mlp = whole_mlp.reshape(hidden, width)
     whole_vectors = []
     at = 0
     for vector in vectors:
@@ -660,9 +797,20 @@
         proj_v.astype(bfloat),
     )
     outgoing = jnp.concatenate([part.reshape(tokens, seq_size, -1) for part in parts], axis=2)
-    heads_in = exchange(jnp.transpose(outgoing, (1, 0, 2))).reshape(seq_size * tokens, -1)
-    attention, mixed = attention_forward(heads_in, table, hp, vd, BLOCK_Q)
-    attended = exchange(mixed.reshape(seq_size, tokens, hp * vd))
+    outgoing = jnp.transpose(outgoing, (1, 0, 2))
+    whole_out, whole_in, whole_mlp, heads_in, attention, attended = gather_and_attend(
+        (w_out, w_in, w_mlp_out),
+        (512, 512, 256),
+        lambda number: number % 4 != 3,
+        3,
+        FIRST_BLOCK_TURN,
+        outgoing,
+        table,
+        (hp, vd, BLOCK_Q),
+    )
+    whole_out = whole_out.reshape(width, width)
+    whole_in = whole_in.reshape(width, hidden)
+    whole_mlp = whole_mlp.reshape(hidden, width)
     attended = jnp.transpose(attended, (1, 0, 2)).reshape(tokens, width)
 
     hidden_in = source + jnp.dot(attended, whole_out, preferred_element_type=single) + bias_out

time: 632 us -> 572 us (0.905)
  local copies, waits for them, and re-layouts: 106 us -> 71.8 us
  waiting for transfers between devices: 25.7 us -> 11.1 us
  Pallas kernels: 370 us -> 359 us
  matrix products: 81.4 us -> 88.9 us
  starting transfers between devices: 14.3 us -> 7.04 us
    dynamic_update_slice x17 -> x8, local copies, waits for them, and re-layouts: 19.5 us -> 4.47 us  [place(): lax.dynamic_update_slice_in_dim(stacked, jnp.expand_dims(piece, axis), in...]
    ppermute x12 -> x6, waiting for transfers between devices: 25.7 us -> 11.1 us  [swap_seq(): return lax.ppermute(value, 'seq', [(i, i ^ distance) for i in range(size)])]
    pallas_call x3 -> x2, Pallas kernels: 196 us -> 183 us  [the longest x1 135 us: gather_and_attend(): pl.pallas_call(functools.partial(attend_kernel, plan, count, spacing, fir...]
    squeeze x4 -> x0, local copies, waits for them, and re-layouts: 9.56 us -> none  [pick(): return lax.dynamic_index_in_dim(stacked, index, axis, keepdims=False)]
    dynamic_slice x9 -> x4, local copies, waits for them, and re-layouts: 11.9 us -> 3.98 us  [pick(): return lax.dynamic_index_in_dim(stacked, index, axis, keepdims=False)]
    ppermute x12 -> x6, starting transfers between devices: 14.3 us -> 7.04 us  [swap_seq(): return lax.ppermute(value, 'seq', [(i, i ^ distance) for i in range(size)])]
    unnamed x117 -> x145, local copies, waits for them, and re-layouts: 17.6 us -> 20.4 us
  transfers between devices with their start and end apart: 12 -> 6, of which waited for: 3 -> 2; matrix products, arithmetic and copies ran while one was open for 11% -> 9% of each run, Pallas kernels for 32% -> 15%
where the time goes in v3:
time: 572 us; the launch traced here: 564 us
  Pallas kernels  359 us (63%)
  matrix products  88.9 us (16%)
  local copies, waits for them, and re-layouts  71.8 us (13%)
  other arithmetic  24.2 us (4%)
  waiting for transfers between devices  11.1 us (2%)
  starting transfers between devices  7.04 us (1%)
    pallas_call x2, Pallas kernels, scatter_all(): pl.pallas_call(functools.partial(scatter_kernel, tuple(plan), tuple(array...  144 us
    pallas_call x1, Pallas kernels, gather_and_attend(): pl.pallas_call(functools.partial(attend_kernel, plan, count, spacing, fir...  135 us
    pallas_call x1, Pallas kernels, gather_all(): pl.pallas_call(functools.partial(gather_kernel, plan, len(shards), spacin...  47.9 us
    pallas_call x1, Pallas kernels, attention_backward(): pl.pallas_call(functools.partial(bwd_kernel, L, bq, hp, vd), grid=(L // b...  32.2 us
    dot_general x5, matrix products, weight_grad(): jnp.einsum('td,te->de', left, right, preferred_element_type=single)  31.7 us
    unnamed x145, local copies, waits for them, and re-layouts  20.4 us
  transfers between devices with their start and end apart: 6, of which 2 were waited for; matrix products, arithmetic and copies ran while one was open for 9% of the time, Pallas kernels for 15%

profile of v3, /device:TPU:0, one launch (start us, length us, event | category | flops | bytes accessed | tf_op | source)
XLA Modules:
  0.0 564.2 jit_solution(1161831692387122618)
XLA Ops:
  1.5 6.1 %concatenate.33 = bf16[3488]{0:T(1024)(128)(2,1)S(1)} concatenate(bf16[48]{0:T(256)(128)(2,1)} %param.24, bf16[48]{0:T(256)(128)(2,1)} %param.25, bf16[16]{0:T(256)(128)(2,1)} %param.30, bf16[16]{0:T(256)(128)(2,1)} %param.31, bf16[48]{0:T(256)(128)(2,1)} %param.33, bf16[48]{0:T(256)(128)(2,1)} %param.34, bf16[48]{0:T(256)(128)(2,1)} %param.35, bf16[96]{0:T(256)(128)(2,1)} %param.37, ...), dimensions={0} | concatenate | bytes 13952 | tf_op jit(solution)/shard_map/concatenate | solution.py:749
  9.7 47.9 %shard_map.313 = (bf16[4,2,2,2,16,256]{5,4,3,2,1,0:T(8,128)(2,1)}, bf16[4,2,2,2,48,1024]{5,4,3,2,1,0:T(8,128)(2,1)}, bf16[4,2,2,2,48,1536]{5,4,3,2,1,0:T(8,128)(2,1)}) custom-call(bf16[16,256]{1,0:T(8,128)(2,1)} %reshape.433.refs_0_, bf16[48,1024]{1,0:T(8,128)(2,1)} %pad_maximum_fusion.4.refs_1_, bf16[48,1536]{1,0:T(8,128)(2,1)} %refs_2_.2), custom_call_target="tpu_custom_call" | custom-call | tf_op jit(solution)/shard_map/pallas_call | solution.py:352
  65.4 4.4 convolution_convert_fusion.7
  71.3 3.4 fusion.68
  76.7 2.0 add_convert_fusion.2
  79.1 1.9 copy.55
  82.3 2.0 reshape.441
  90.9 2.1 convolution_convert_fusion.5.refs_4_.tab_ref
  93.0 135.0 %shard_map.314 = (bf16[4,2,2,2,48,1536]{5,4,3,2,1,0:T(8,128)(2,1)}, bf16[4,2,2,2,48,3072]{5,4,3,2,1,0:T(8,128)(2,1)}, bf16[4,2,2,2,96,1536]{5,4,3,2,1,0:T(8,128)...) custom-call(bf16[48,1536]{1,0:T(8,128)(2,1)} %refs_0_.1, ...), custom_call_target="tpu_custom_call" | custom-call | tf_op jit(solution)/shard_map/pallas_call | solution.py:469
  228.0 2.6 copy.63
  232.0 4.9 fusion.80
  237.7 6.9 %convolution_add_fusion = f32[384,3072]{1,0:T(8,128)S(1)} fusion(bf16[1536,3072]{1,0:T(8,128)(2,1)} %bitcast.201, f32[3072]{0:T(1024)S(1)} %copy-done.48, f32[384,1536]{1,0:T(8,128)S(1)} %get-tuple-element.112, f32[1536]{0:T(1024)S(1)} %copy-done.53, f32[1536]{0:T(1024)S(1)} %reshape.478, f32[384]{0:T(512)S(1)} %fusion.56, f32[384]{0:T(512)S(1)} %broadcast_multiply_fusion), kind=kOutput, calls=%fused_computation.19 | convolution fusion | flops 3628007424 | bytes 16542720 | tf_op jit(solution)/shard_map/dot_general | solution.py:819
  244.6 7.1 %fusion.81 = (bf16[3072]{0:T(1024)(128)(2,1)}, bf16[384,3072]{1,0:T(8,128)(2,1)S(1)}) fusion(f32[384,3072]{1,0:T(8,128)S(1)} %convolution_add_fusion, bf16[3072,1536]{1,0:T(8,128)(2,1)S(1)} %bitcast.200, bf16[1,384,1536]{2,1,0:T(8,128)(2,1)S(1)} %copy-done.3), kind=kOutput, calls=%fused_computation.165 | convolution fusion | flops 3648648192 | bytes 17700864 | tf_op jit(solution)/shard_map/td,fd->tf/dot_general | solution.py:835
  251.7 8.4 %multiply_reduce_fusion = (bf16[1536]{0:T(1024)(128)(2,1)}, f32[384]{0:T(512)S(1)}, bf16[1536]{0:T(1024)(128)(2,1)}, f32[384,1536]{1,0:T(8,128)S(1)}) fusion(f32[384,1536]{1,0:T(8,128)S(1)} %get-tuple-element.112, f32[384]{0:T(512)S(1)} %fusion.56, f32[384]{0:T(512)S(1)} %broadcast_multiply_fusion, f32[1536]{0:T(1024)S(1)} %reshape.478, ...), kind=kOutput, calls=%fused_computation.58 | convolution fusion | flops 3628593664 | bytes 16531968 | tf_op jit(solution)/shard_map/tf,df->td/dot_general | solution.py:842
  263.3 3.0 convolution_convert_fusion.6
  266.3 3.6 reshape.448
  270.0 6.0 %constant_dynamic-slice_fusion.4 = (bf16[384,1,384]{2,1,0:T(2,128)(2,1)S(1)}, bf16[384,1,384]{2,1,0:T(2,128)(2,1)S(1)}, bf16[384,1,384]{2,1,0:T(2,128)(2,1)S(1)}, bf16[384,1,384]{2,1,0:T(2,128)(2,1)}) fusion(bf16[384,4,384]{2,1,0:T(4,128)(2,1)} %reshape.448, s32[]{:T(128)S(6)} %select_n.36, s32[]{:T(128)S(6)} %select_n.35, s32[]{:T(128)S(6)} %select_n.34, ...), kind=kLoop, calls=%fused_computation.123 | loop fusion | bytes 2359312 | tf_op jit(solution)/shard_map/dynamic-slice.3
  281.9 10.5 %convolution_convert_fusion.1 = bf16[3072,1536]{1,0:T(8,128)(2,1)} fusion(bf16[1,384,1536]{2,1,0:T(8,128)(2,1)S(1)} %copy-done.4, f32[384,3072]{1,0:T(8,128)} %copy-done.59), kind=kOutput, calls=%fused_computation.1 | convolution fusion | flops 3639214080 | bytes 15335424 | tf_op jit(solution)/shard_map/td,te->de/dot_general | solution.py:828
  292.4 8.0 %convolution_convert_fusion = bf16[1536,3072]{1,0:T(8,128)(2,1)} fusion(bf16[384,3072]{1,0:T(8,128)(2,1)S(1)} %copy-done.58, f32[384,1536]{1,0:T(8,128)S(1)} %get-tuple-element.112, f32[1536]{0:T(1024)S(1)} %copy-done.54, f32[1536]{0:T(1024)S(1)} %copy-done.33, f32[384]{0:T(512)S(1)} %copy-done.50, f32[384]{0:T(512)S(1)} %copy-done.40), kind=kOutput, calls=%fused_computation | convolution fusion | flops 3631546368 | bytes 14171136 | tf_op jit(solution)/shard_map/td,te->de/dot_general | solution.py:828
  301.1 10.3 %fusion.20 = bf16[1,384,1536]{2,1,0:T(8,128)(2,1)} fusion(f32[384,1536]{1,0:T(8,128)S(1)} %get-tuple-element.112, bf16[3072,1536]{1,0:T(8,128)(2,1)} %bitcast.197, f32[1536]{0:T(1024)} %reshape.481, f32[384,3072]{1,0:T(8,128)} %copy-done.59), kind=kOutput, calls=%fused_computation.42 | convolution fusion | flops 3636264960 | bytes 17700864 | tf_op jit(solution)/shard_map/dot_general | solution.py:822
  311.4 4.4 convolution_convert_fusion.3
  322.2 82.2 %shard_map.317 = (f32[96,1536]{1,0:T(8,128)}, f32[48,3072]{1,0:T(8,128)}) custom-call(bf16[4,2,2,2,96,1536]{5,4,3,2,1,0:T(8,128)(2,1)} %bitcast.158, bf16[4,2,2,2,48,3072]{5,4,3,2,1,0:T(8,128)(2,1)} %bitcast.159), custom_call_target="tpu_custom_call" | custom-call | tf_op jit(solution)/shard_map/pallas_call | solution.py:677
  408.5 32.2 %shard_map.315 = (bf16[1536,128]{1,0:T(8,128)(2,1)}, bf16[1536,512]{1,0:T(8,128)(2,1)}, f32[128,3072]{1,0:T(8,128)}, f32[8,128]{1,0:T(8,128)}) custom-call(bf16[1536,768]{1,0:T(8,128)(2,1)} %get-tuple-element.46.x_ref, bf16[128,3072]{1,0:T(8,128)(2,1)} %convolution_convert_fusion.5.refs_4_.tab_ref, bf16[2,1536,1536]{2,1,0:T(8,128)(2,1)} %get-tuple-element.47.att_ref, ...), custom_call_target="tpu_custom_call" | custom-call | tf_op jit(solution)/shard_map/pallas_call | solution.py:131
  451.2 2.9 convolution_dynamic-update-slice_fusion
  456.4 3.8 collective-permute-done.3
  461.3 7.3 %collective-permute-done.4 = bf16[384,640]{0,1:T(8,128)(2,1)S(1)} collective-permute-done((bf16[384,640]{0,1:T(8,128)(2,1)}, bf16[384,640]{0,1:T(8,128)(2,1)S(1)}, u32[]{:S(2)}, u32[]{:S(2)}) %collective-permute-start.4) | collective-permute-done | bytes 491552 | tf_op jit(solution)/shard_map/ppermute | solution.py:155
  472.0 3.7 convolution_convert_fusion.4
  475.8 5.0 convolution_convert_fusion.2
  480.8 2.5 fusion.70
  486.9 62.0 %shard_map.316 = (f32[48,1536]{1,0:T(8,128)}, f32[48,1024]{1,0:T(8,128)}, f32[48,1536]{1,0:T(8,128)}, f32[16,256]{1,0:T(8,128)}) custom-call(bf16[4,2,2,2,48,1536]{5,4,3,2,1,0:T(8,128)(2,1)} %bitcast.165, bf16[4,2,2,2,48,1024]{5,4,3,2,1,0:T(8,128)(2,1)} %bitcast.169, bf16[4,2,2,2,48,1536]{5,4,3,2,1,0:T(8,128)(2,1)} %bitcast.166, ...), custom_call_target="tpu_custom_call" | custom-call | tf_op jit(solution)/shard_map/pallas_call | solution.py:677
  552.2 4.5 add_bitcast_fusion
  558.7 1.7 copy.106
  (251 shorter events, 74.0 us)
Async XLA Ops:
  0.7 63.4 %copy-start = (bf16[1,384,1536]{2,1,0:T(8,128)(2,1)S(1)}, bf16[1,384,1536]{2,1,0:T(8,128)(2,1)}, u32[]{:S(2)}) copy-start(bf16[1,384,1536]{2,1,0:T(8,128)(2,1)} %param.22) | copy-start | bytes 3538948
  92.9 137.6 %copy-start.27 = (f32[32,96]{1,0:T(8,128)S(1)}, f32[32,96]{1,0:T(8,128)}, u32[]{:S(2)}) copy-start(f32[32,96]{1,0:T(8,128)} %slice_convert_fusion.2) | copy-start | bytes 36868
  93.0 138.3 %copy-start.26 = (f32[32,48]{1,0:T(8,128)S(1)}, f32[32,48]{1,0:T(8,128)}, u32[]{:S(2)}) copy-start(f32[32,48]{1,0:T(8,128)} %get-tuple-element.86) | copy-start | bytes 18436
  93.0 139.0 %copy-start.25 = (f32[32,48]{1,0:T(8,128)S(1)}, f32[32,48]{1,0:T(8,128)}, u32[]{:S(2)}) copy-start(f32[32,48]{1,0:T(8,128)} %get-tuple-element.84) | copy-start | bytes 18436
  93.0 139.1 %copy-start.31 = (f32[1536]{0:T(1024)S(1)}, f32[1536]{0:T(1024)}, u32[]{:S(2)}) copy-start(f32[1536]{0:T(1024)} %reshape.477) | copy-start | bytes 18436
  232.0 28.1 %copy-start.32 = (f32[1536]{0:T(1024)}, f32[1536]{0:T(1024)S(1)}, u32[]{:S(2)}) copy-start(f32[1536]{0:T(1024)S(1)} %reshape.478) | copy-start | bytes 18436
  237.0 23.2 %copy-start.39 = (f32[384]{0:T(512)}, f32[384]{0:T(512)S(1)}, u32[]{:S(2)}) copy-start(f32[384]{0:T(512)S(1)} %broadcast_multiply_fusion) | copy-start | bytes 4612
  237.0 7.6 %slice-start.2 = ((s8[9437184]{0:T(1024)(128)(4,1)}), s8[4194304]{0:T(1024)(128)(4,1)S(1)}, s32[]{:S(2)}) async-start(s8[9437184]{0:T(1024)(128)(4,1)} %bitcast.198), calls=%async_computation.2 | async-start | bytes 8388608
  237.4 22.8 %copy-start.49 = (f32[384]{0:T(512)}, f32[384]{0:T(512)S(1)}, u32[]{:S(2)}) copy-start(f32[384]{0:T(512)S(1)} %fusion.56) | copy-start | bytes 4612
  237.6 25.6 %slice-start = ((s8[4718592]{0:T(1024)(128)(4,1)}), s8[4194304]{0:T(1024)(128)(4,1)S(1)}, s32[]{:S(2)}) async-start(s8[4718592]{0:T(1024)(128)(4,1)} %bitcast.155), calls=%async_computation | async-start | bytes 8388608
  244.5 7.2 %copy-start.59 = (f32[384,3072]{1,0:T(8,128)}, f32[384,3072]{1,0:T(8,128)S(1)}, u32[]{:S(2)}) copy-start(f32[384,3072]{1,0:T(8,128)S(1)} %convolution_add_fusion) | copy-start | bytes 14155780
  244.6 18.7 %slice-start.1 = ((s8[4718592]{0:T(1024)(128)(4,1)}), s8[524288]{0:T(1024)(128)(4,1)S(1)}, s32[]{:S(2)}) async-start(s8[4718592]{0:T(1024)(128)(4,1)} %bitcast.155), calls=%async_computation.1 | async-start | bytes 1048576
  251.7 8.4 %copy-start.57 = (bf16[384,3072]{1,0:T(8,128)(2,1)}, bf16[384,3072]{1,0:T(8,128)(2,1)S(1)}, u32[]{:S(2)}) copy-start(bf16[384,3072]{1,0:T(8,128)(2,1)S(1)} %get-tuple-element.116) | copy-start | bytes 7077892
  276.8 127.6 %collective-permute-start = (bf16[384,384]{1,0:T(8,128)(2,1)}, bf16[384,384]{1,0:T(8,128)(2,1)}, u32[]{:S(2)}, u32[]{:S(2)}) collective-permute-start(bf16[384,384]{1,0:T(8,128)(2,1)} %bitcast.153), channel_id=1, source_target_pairs={{0,1},{1,0},{2,3},{3,2},{4,5},{5,4},{6,7},{7,6},{8,9},{9,8},{10,11... | collective-permute-start | bytes 884744 | tf_op jit(solution)/shard_map/ppermute | solution.py:155
  279.0 126.4 %collective-permute-start.1 = (bf16[384,384]{1,0:T(8,128)(2,1)}, bf16[384,384]{1,0:T(8,128)(2,1)}, u32[]{:S(2)}, u32[]{:S(2)}) collective-permute-start(bf16[384,384]{1,0:T(8,128)(2,1)} %bitcast.152), channel_id=1, source_target_pairs={{0,2},{1,3},{2,0},{3,1},{4,6},{5,7},{6,4},{7,5},{8,10},{9,11},{10,... | collective-permute-start | bytes 884744 | tf_op jit(solution)/shard_map/ppermute | solution.py:155
  281.1 11.3 %copy-start.33 = (f32[1536]{0:T(1024)S(1)}, f32[1536]{0:T(1024)}, u32[]{:S(2)}) copy-start(f32[1536]{0:T(1024)} %copy-done.32) | copy-start | bytes 18436
  281.1 11.3 %copy-start.40 = (f32[384]{0:T(512)S(1)}, f32[384]{0:T(512)}, u32[]{:S(2)}) copy-start(f32[384]{0:T(512)} %copy-done.39) | copy-start | bytes 4612
  281.1 11.3 %copy-start.50 = (f32[384]{0:T(512)S(1)}, f32[384]{0:T(512)}, u32[]{:S(2)}) copy-start(f32[384]{0:T(512)} %copy-done.49) | copy-start | bytes 4612
  281.1 11.3 %copy-start.54 = (f32[1536]{0:T(1024)S(1)}, f32[1536]{0:T(1024)}, u32[]{:S(2)}) copy-start(f32[1536]{0:T(1024)} %reshape.479) | copy-start | bytes 18436
  281.1 11.3 %copy-start.58 = (bf16[384,3072]{1,0:T(8,128)(2,1)S(1)}, bf16[384,3072]{1,0:T(8,128)(2,1)}, u32[]{:S(2)}) copy-start(bf16[384,3072]{1,0:T(8,128)(2,1)} %copy-done.57) | copy-start | bytes 7077892
  281.1 125.3 %collective-permute-start.2 = (bf16[384,384]{1,0:T(8,128)(2,1)}, bf16[384,384]{1,0:T(8,128)(2,1)}, u32[]{:S(2)}, u32[]{:S(2)}) collective-permute-start(bf16[384,384]{1,0:T(8,128)(2,1)} %bitcast.151), channel_id=1, source_target_pairs={{0,3},{1,2},{2,1},{3,0},{4,7},{5,6},{6,5},{7,4},{8,11},{9,10},{10,... | collective-permute-start | bytes 884744 | tf_op jit(solution)/shard_map/ppermute | solution.py:155
  292.4 8.0 %copy-start.24 = (f32[32,48]{1,0:T(8,128)S(1)}, f32[32,48]{1,0:T(8,128)}, u32[]{:S(2)}) copy-start(f32[32,48]{1,0:T(8,128)} %get-tuple-element.85) | copy-start | bytes 18436
  301.1 10.3 %copy-start.7 = (bf16[384,4,384]{0,2,1:T(8,128)(2,1)S(1)}, bf16[384,4,384]{0,2,1:T(8,128)(2,1)}, u32[]{:S(2)}) copy-start(bf16[384,4,384]{0,2,1:T(8,128)(2,1)} %copy.63) | copy-start | bytes 3538948
  301.1 10.3 %copy-start.11 = (bf16[384,1536]{1,0:T(8,128)(2,1)S(1)}, bf16[384,1536]{1,0:T(8,128)(2,1)}, u32[]{:S(2)}) copy-start(bf16[384,1536]{1,0:T(8,128)(2,1)} %copy-done.10) | copy-start | bytes 3538948
  443.3 7.9 %copy-start.18 = (bf16[3071,32]{0,1:T(8,128)(2,1)S(1)}, bf16[3071,32]{0,1:T(8,128)(2,1)}, u32[]{:S(2)}) copy-start(bf16[3071,32]{0,1:T(8,128)(2,1)} %copy-done.17) | copy-start | bytes 589636
  443.3 7.9 %copy-start.20 = (bf16[3071,32]{0,1:T(8,128)(2,1)S(1)}, bf16[3071,32]{0,1:T(8,128)(2,1)}, u32[]{:S(2)}) copy-start(bf16[3071,32]{0,1:T(8,128)(2,1)} %copy-done.19) | copy-start | bytes 589636
  445.7 14.5 %collective-permute-start.3 = (bf16[384,640]{0,1:T(8,128)(2,1)}, bf16[384,640]{0,1:T(8,128)(2,1)}, u32[]{:S(2)}, u32[]{:S(2)}) collective-permute-start(bf16[384,640]{0,1:T(8,128)(2,1)} %bitcast.184), channel_id=1, source_target_pairs={{0,1},{1,0},{2,3},{3,2},{4,5},{5,4},{6,7},{7,6},{8,9},{9,8},{10,11... | collective-permute-start | bytes 1474568 | tf_op jit(solution)/shard_map/ppermute | solution.py:155
  447.8 20.8 %collective-permute-start.4 = (bf16[384,640]{0,1:T(8,128)(2,1)}, bf16[384,640]{0,1:T(8,128)(2,1)S(1)}, u32[]{:S(2)}, u32[]{:S(2)}) collective-permute-start(bf16[384,640]{0,1:T(8,128)(2,1)} %bitcast.183), channel_id=1, source_target_pairs={{0,2},{1,3},{2,0},{3,1},{4,6},{5,7},{6,4},{7,5},{8,10},{9,11},{10,... | collective-permute-start | bytes 1474568 | tf_op jit(solution)/shard_map/ppermute | solution.py:155
  449.7 19.0 %collective-permute-start.5 = (bf16[384,640]{0,1:T(8,128)(2,1)}, bf16[384,640]{0,1:T(8,128)(2,1)S(1)}, u32[]{:S(2)}, u32[]{:S(2)}) collective-permute-start(bf16[384,640]{0,1:T(8,128)(2,1)} %bitcast.182), channel_id=1, source_target_pairs={{0,3},{1,2},{2,1},{3,0},{4,7},{5,6},{6,5},{7,4},{8,11},{9,10},{10,... | collective-permute-start | bytes 1474568 | tf_op jit(solution)/shard_map/ppermute | solution.py:155
  472.0 8.8 %slice-start.5 = ((s8[4718592]{0:T(1024)(128)(4,1)}), s8[4194304]{0:T(1024)(128)(4,1)S(1)}, s32[]{:S(2)}) async-start(s8[4718592]{0:T(1024)(128)(4,1)} %bitcast.204), calls=%async_computation.5 | async-start | bytes 8388608
  486.9 65.2 %copy-start.2 = (f32[384,1536]{1,0:T(8,128)S(1)}, f32[384,1536]{1,0:T(8,128)}, u32[]{:S(2)}) copy-start(f32[384,1536]{1,0:T(8,128)} %copy-done.1) | copy-start | bytes 7077892
  552.2 9.9 %copy-start.15 = (f32[48,3072]{1,0:T(8,128)S(1)}, f32[48,3072]{1,0:T(8,128)}, u32[]{:S(2)}) copy-start(f32[48,3072]{1,0:T(8,128)} %get-tuple-element.152) | copy-start | bytes 1769476
  (41 other events, 105.0 us)

commit v4 on v3

--- a/solution.py
+++ b/solution.py
@@ -15,6 +15,8 @@
 CORES = 2
 BLOCK_Q = 256
 FIRST_BLOCK_TURN = 8
+BLOCK_TURNS = (4, 6, 8, 10, 12, 13)
+VMEM_LIMIT = 62 * 2**20
 bfloat = jnp.bfloat16
 single = jnp.float32
 
@@ -70,89 +72,52 @@
     mixed_ref[rows, :] = jnp.concatenate(outs, axis=1) if hp > 1 else outs[0]
 
 
-def bwd_kernel(L, bq, hp, vd, x_ref, tab_ref, att_ref, gm_ref, dq_ref, dkv_ref, dtab_ref, bias_ref, dkT, dvT):
-    qi = pl.program_id(0)
+def attend_back(length, bq, hp, vd, block, x_ref, tab_ref, att_ref, gm_ref, ret_ref, sums):
+    dk_ref, dv_ref, dtab_ref, bias_ref = sums
     hk = hp * KD
-    i0 = pl.multiple_of(qi * bq, bq)
-    a = pl.multiple_of(L - bq - i0, bq)
-    W = L + bq
-
-    @pl.when(qi == 0)
-    def _():
-        dkT[...] = jnp.zeros_like(dkT)
-        dvT[...] = jnp.zeros_like(dvT)
-        dtab_ref[...] = jnp.zeros_like(dtab_ref)
-        bias_ref[...] = jnp.zeros_like(bias_ref)
-
+    first = block * bq
+    rows = pl.ds(first, bq)
+    span = length + bq
     row = lax.broadcasted_iota(jnp.int32, (bq, bq), 0)
     col = lax.broadcasted_iota(jnp.int32, (bq, bq), 1)
-    flip = jnp.where(row + col == bq - 1, 1.0, 0.0).astype(jnp.bfloat16)
+    flip = jnp.where(row + col == bq - 1, 1.0, 0.0).astype(bfloat)
 
     def flipped(v):
-        return jnp.dot(flip, v, preferred_element_type=jnp.float32)
+        return jnp.dot(flip, v, preferred_element_type=single)
+
+    def dot(left, right, left_dim, right_dim):
+        return lax.dot_general(
+            left, right, (((left_dim,), (right_dim,)), ((), ())), preferred_element_type=single
+        )
 
     dqs, bc, bp = [], [], []
     for h in range(hp):
-        qc = flipped(x_ref[pl.ds(i0, bq), pl.ds(h * KD, KD)]).astype(jnp.bfloat16)
-        qp = flipped(x_ref[pl.ds(i0, bq), pl.ds(hk + h * KD, KD)]).astype(jnp.bfloat16)
+        own = pl.ds(h * KD, KD)
+        table_cols = pl.ds(length - bq - first, span)
+        qc = flipped(x_ref[rows, own]).astype(bfloat)
+        qp = flipped(x_ref[rows, pl.ds(hk + h * KD, KD)]).astype(bfloat)
         k = x_ref[:, pl.ds(2 * hk + h * KD, KD)]
         v = x_ref[:, pl.ds(3 * hk + h * vd, vd)]
-        gm = gm_ref[:, pl.ds(h * vd, vd)]
+        gm = gm_ref[rows, pl.ds(h * vd, vd)]
         att = att_ref[h]
-        dvT[pl.ds(h * vd, vd), :] += lax.dot_general(gm, att, (((0,), (0,)), ((), ())), preferred_element_type=jnp.float32)
-        gmr = flipped(gm).astype(jnp.bfloat16)
-        dp = lax.dot_general(gmr, v, (((1,), (1,)), ((), ())), preferred_element_type=jnp.float32)
+        dv_ref[pl.ds(h * vd, vd), :] += dot(gm, att, 0, 0)
+        dp = dot(flipped(gm).astype(bfloat), v, 1, 1)
         af = flipped(att)
         t = af * dp
         delta = jnp.sum(t, axis=-1, keepdims=True)
-        ds = (t - af * delta).astype(jnp.bfloat16)
-        dkT[pl.ds(h * KD, KD), :] += lax.dot_general(qc, ds, (((0,), (0,)), ((), ())), preferred_element_type=jnp.float32)
-        gc = jnp.dot(ds, k, preferred_element_type=jnp.float32)
-        wide = jnp.concatenate([ds.astype(jnp.float32), jnp.zeros((bq, bq), jnp.float32)], axis=1)
-        rel = pltpu.roll(wide, 0, 1, stride=1, stride_axis=0).astype(jnp.bfloat16)
-        tab = tab_ref[pl.ds(h * KD, KD), pl.ds(a, W)]
-        gp = lax.dot_general(rel, tab, (((1,), (1,)), ((), ())), preferred_element_type=jnp.float32)
-        dtab_ref[pl.ds(h * KD, KD), pl.ds(a, W)] += lax.dot_general(qp, rel, (((0,), (0,)), ((), ())), preferred_element_type=jnp.float32)
-        dqs.append(flipped(((gc + gp) * KD ** -0.5).astype(jnp.bfloat16)).astype(jnp.bfloat16))
+        ds = (t - af * delta).astype(bfloat)
+        dk_ref[own, :] += dot(qc, ds, 0, 0)
+        gc = jnp.dot(ds, k, preferred_element_type=single)
+        wide = jnp.concatenate([ds.astype(single), jnp.zeros((bq, bq), single)], axis=1)
+        rel = pltpu.roll(wide, 0, 1, stride=1, stride_axis=0).astype(bfloat)
+        gp = dot(rel, tab_ref[own, table_cols], 1, 1)
+        dtab_ref[own, table_cols] += dot(qp, rel, 0, 0)
+        dqs.append(flipped(((gc + gp) * KD**-0.5).astype(bfloat)).astype(bfloat))
         bc.append(jnp.sum(gc, axis=0, keepdims=True))
         bp.append(jnp.sum(gp, axis=0, keepdims=True))
-    dq_ref[...] = jnp.concatenate(dqs, axis=1) if hp > 1 else dqs[0]
+    ret_ref[rows, :hk] = jnp.concatenate(dqs, axis=1) if hp > 1 else dqs[0]
     bias_ref[0:1, :] += jnp.concatenate(bc, axis=1) if hp > 1 else bc[0]
     bias_ref[1:2, :] += jnp.concatenate(bp, axis=1) if hp > 1 else bp[0]
-
-    @pl.when(qi == pl.num_programs(0) - 1)
-    def _():
-        dkv_ref[:, :hk] = dkT[...].T.astype(jnp.bfloat16)
-        dkv_ref[:, hk:] = dvT[...].T.astype(jnp.bfloat16)
-
-def attention_backward(x, tab, att, gm, hp, vd, bq):
-    L = x.shape[0]
-    hk = hp * KD
-    return pl.pallas_call(
-        functools.partial(bwd_kernel, L, bq, hp, vd),
-        grid=(L // bq,),
-        in_specs=[pl.BlockSpec(x.shape, lambda i: (0, 0)), pl.BlockSpec(tab.shape, lambda i: (0, 0)),
-                  pl.BlockSpec((hp, bq, L), lambda i: (0, i, 0)), pl.BlockSpec((bq, hp * vd), lambda i: (i, 0))],
-        out_specs=[pl.BlockSpec((bq, hk), lambda i: (i, 0)), pl.BlockSpec((L, hk + hp * vd), lambda i: (0, 0)),
-                   pl.BlockSpec(tab.shape, lambda i: (0, 0)), pl.BlockSpec((8, hk), lambda i: (0, 0))],
-        out_shape=[jax.ShapeDtypeStruct((L, hk), jnp.bfloat16), jax.ShapeDtypeStruct((L, hk + hp * vd), jnp.bfloat16),
-                   jax.ShapeDtypeStruct(tab.shape, jnp.float32), jax.ShapeDtypeStruct((8, hk), jnp.float32)],
-        scratch_shapes=[pltpu.VMEM((hk, L), jnp.float32), pltpu.VMEM((hp * vd, L), jnp.float32)],
-        compiler_params=pltpu.CompilerParams(vmem_limit_bytes=56 * 2**20),
-    )(x, tab, att, gm)
-
-
-def pick(stacked, index, axis):
-    return lax.dynamic_index_in_dim(stacked, index, axis, keepdims=False)
-
-
-def place(stacked, piece, index, axis):
-    return lax.dynamic_update_slice_in_dim(stacked, jnp.expand_dims(piece, axis), index, axis)
-
-
-def swap_seq(value, distance):
-    size = lax.axis_size("seq")
-    return lax.ppermute(value, "seq", [(i, i ^ distance) for i in range(size)])
 
 
 def partners():
@@ -469,7 +434,7 @@
     return pl.pallas_call(
         functools.partial(attend_kernel, plan, count, spacing, first_turn, dims),
         in_specs=[vmem] * count + [anywhere, vmem],
-        out_specs=[anywhere] * count + [vmem, anywhere, vmem],
+        out_specs=[anywhere] * count + [vmem, anywhere, anywhere],
         out_shape=gathered_shapes(shards)
         + [
             jax.ShapeDtypeStruct((length, cols), bfloat),
@@ -484,17 +449,17 @@
         + [dma((peers,))] * 6
         + [dma((length // bq,))],
         compiler_params=pltpu.CompilerParams(
-            collective_id=1, has_side_effects=True, vmem_limit_bytes=56 * 2**20
+            collective_id=1, has_side_effects=True, vmem_limit_bytes=VMEM_LIMIT
         ),
     )(*shards, outgoing, tab)
 
 
-def scatter_kernel(plan, arrays, spacing, *refs):
+def scatter_work(plan, arrays, spacing, refs):
     count = len(arrays)
-    grads, outs, rest = refs[:count], refs[count : 2 * count], refs[2 * count :]
+    sources, outs, rest = refs
     win, seq, here, core, chips, bits = partners()
     chip_steps = chips - 1
-    kept, from_core, rest = rest[:count], rest[count : 2 * count], rest[2 * count :]
+    ring, kept, rest = rest[:count], rest[count : 2 * count], rest[2 * count :]
     from_bits, rest = rest[: count * bits], rest[count * bits :]
     from_chips, rest = rest[:count], rest[count:]
     send_sem, recv_sem, local_sem = rest
@@ -523,32 +488,42 @@
     def core_stage(chunk, number):
         which, slot, _ = chunk
         width = arrays[which][1]
+        product = isinstance(sources[which], tuple)
+        held = ring[which].at[slot % spacing]
         columns = (slice(None),) * bits + (slice(None), pl.ds(slot * width, width))
+        if product:
+            leaving, own = held.at[:, 1 - core], held.at[:, core]
+        else:
+            leaving, own = sources[which].at[(slice(None), 1 - core) + columns], held
         kind = 2 * chip_steps + 2 * bits
-        item = copy(
-            grads[which].at[(slice(None), 1 - core) + columns],
-            from_core[which].at[slot],
-            number,
-            kind,
-            win ^ 1,
-            seq,
-        )
-        own = pltpu.make_async_copy(
-            grads[which].at[(slice(None), core) + columns],
-            kept[which].at[slot],
-            local_sem.at[number],
-        )
+        item = copy(leaving, kept[which].at[slot], number, kind, win ^ 1, seq)
+        if not product:
+            placed = pltpu.make_async_copy(
+                sources[which].at[(slice(None), core) + columns], held, local_sem.at[number]
+            )
 
         def start():
+            if product:
+                left, right = sources[which]
+                grad = lax.dot_general(
+                    left[...],
+                    right[:, pl.ds(slot * width, width)],
+                    (((0,), (0,)), ((), ())),
+                    preferred_element_type=single,
+                )
+                held[...] = grad.astype(bfloat).reshape(held.shape)
+            else:
+                placed.start()
             item.start()
-            own.start()
 
         def arrive():
-            own.wait()
+            if not product:
+                placed.wait()
             item.wait_recv()
-            add(kept[which].at[slot], from_core[which].at[slot])
-
-        return start, arrive, item.wait_send
+            add(kept[which].at[slot], own)
+            item.wait_send()
+
+        return start, arrive, lambda: None
 
     def bit_stage(chunk, number, step, chip):
         which, slot, _ = chunk
@@ -645,63 +620,201 @@
         total = slabs(chunk, here, own_seq)[...].astype(single)
         outs[which][:, pl.ds(slot * width, width)] = total
 
+    return [stages(chunk, number) for number, chunk in enumerate(plan)], last
+
+
+def scatter_plan(grads, widths, lines_last):
+    devices = lax.axis_size("win") * lax.axis_size("seq")
+    plan, arrays = [], []
+    for which, (grad, width) in enumerate(zip(grads, widths)):
+        if isinstance(grad, tuple):
+            rows, cols = grad[0].shape[1] // devices, grad[1].shape[1]
+        else:
+            rows, cols = grad.shape[-2:]
+        slots = cols // width
+        lasts = [lines_last(len(plan) + slot) for slot in range(slots)]
+        plan += [(which, slot, last) for slot, last in enumerate(lasts)]
+        arrays.append((rows, width, slots, isinstance(grad, tuple)))
+    return tuple(plan), tuple(arrays)
+
+
+def scatter_scratch(plan, arrays, spacing):
+    chips = lax.axis_size("win") // CORES
+    bits = lax.axis_size("seq").bit_length() - 1
+    cube = (2,) * bits
+    ring, kept, from_bits, from_chips = [], [], [], []
+    for which, (rows, width, slots, product) in enumerate(arrays):
+        halves = (CORES,) if product else ()
+        ring.append(pltpu.VMEM((spacing, chips) + halves + cube + (rows, width), bfloat))
+        kept.append(pltpu.VMEM((slots, chips) + cube + (rows, width), bfloat))
+        for step in range(bits):
+            left = (2,) * (bits - 1 - step)
+            from_bits.append(pltpu.VMEM((slots, 2, chips) + left + (rows, width // 2), bfloat))
+        lone = (1,) * bits if all(c[2] for c in plan if c[0] == which) else cube
+        from_chips.append(pltpu.VMEM((slots, 2 * (chips - 1)) + lone + (rows, width), bfloat))
+    kinds = 2 * (chips - 1) + 2 * bits + 1
+    dma = pltpu.SemaphoreType.DMA
+    sems = [dma((len(plan), kinds)), dma((len(plan), kinds)), dma((len(plan),))]
+    return ring + kept + from_bits + from_chips + sems
+
+
+def flat_sources(grads):
+    flat, specs = [], []
+    for grad in grads:
+        whole = isinstance(grad, tuple)
+        flat += grad if whole else (grad,)
+        specs += [pl.BlockSpec(memory_space=pltpu.VMEM if whole else pl.ANY)] * (2 if whole else 1)
+    return flat, specs
+
+
+def group_sources(arrays, refs):
+    sources = []
+    for _, _, _, product in arrays:
+        sources.append((refs[0], refs[1]) if product else refs[0])
+        refs = refs[2 if product else 1 :]
+    return sources, refs
+
+
+def scatter_kernel(plan, arrays, spacing, *refs):
+    count = len(arrays)
+    sources, refs = group_sources(arrays, refs)
     start_together()
-    work = [stages(chunk, number) for number, chunk in enumerate(plan)]
+    work, last = scatter_work(plan, arrays, spacing, (sources, refs[:count], refs[count:]))
     for turn in range(turns_of(work, spacing)):
         run_turn(work, spacing, turn, last)
     finish_sends(work)
 
 
 def scatter_all(grads, widths, lines_last, spacing, collective_id):
-    chips = lax.axis_size("win") // CORES
-    bits = lax.axis_size("seq").bit_length() - 1
-    plan, arrays = [], []
-    kept, from_core, from_bits, from_chips = [], [], [], []
-    for which, (grad, width) in enumerate(zip(grads, widths)):
-        rows, cols = grad.shape[-2:]
-        slots = cols // width
-        lasts = [lines_last(len(plan) + slot) for slot in range(slots)]
-        plan += [(which, slot, last) for slot, last in enumerate(lasts)]
-        arrays.append((rows, width))
-        cube = (2,) * bits
-        kept.append(pltpu.VMEM((slots, chips) + cube + (rows, width), bfloat))
-        from_core.append(pltpu.VMEM((slots, chips) + cube + (rows, width), bfloat))
-        for step in range(bits):
-            left = (2,) * (bits - 1 - step)
-            from_bits.append(
-                pltpu.VMEM((slots, 2, chips) + left + (rows, width // 2), bfloat)
+    plan, arrays = scatter_plan(grads, widths, lines_last)
+    flat, specs = flat_sources(grads)
+    return pl.pallas_call(
+        functools.partial(scatter_kernel, plan, arrays, spacing),
+        in_specs=specs,
+        out_specs=[pl.BlockSpec(memory_space=pltpu.VMEM)] * len(grads),
+        out_shape=[jax.ShapeDtypeStruct((a[0], a[1] * a[2]), single) for a in arrays],
+        scratch_shapes=scatter_scratch(plan, arrays, spacing),
+        compiler_params=pltpu.CompilerParams(
+            collective_id=collective_id, has_side_effects=True, vmem_limit_bytes=VMEM_LIMIT
+        ),
+    )(*flat)
+
+
+def attend_back_kernel(plan, arrays, spacing, block_turns, dims, *refs):
+    hp, vd, bq = dims
+    count = len(arrays)
+    sources, refs = group_sources(arrays, refs)
+    (leaving_ref, x_ref, tab_ref, att_in), refs = refs[:4], refs[4:]
+    outs, (returned, dtab_ref, bias_ref), refs = refs[:count], refs[count : count + 3], refs[count + 3 :]
+    gm_ref, ret_ref, att_ref, dk_ref, dv_ref, *scatter_refs = refs[:-7]
+    in_send, in_recv, in_local, out_send, out_recv, out_local, att_sem = refs[-7:]
+    length = x_ref.shape[0]
+    hk = hp * KD
+    peers, rows = leaving_ref.shape[:2]
+    blocks = length // bq
+    incoming = exchange_work(
+        [leaving_ref.at[peer] for peer in range(peers)],
+        lambda peer: gm_ref.at[pl.ds(peer * rows, rows)],
+        in_send,
+        in_recv,
+        in_local,
+    )
+    leaving = exchange_work(
+        [ret_ref.at[pl.ds(peer * rows, rows)] for peer in range(peers)],
+        lambda peer: returned.at[peer],
+        out_send,
+        out_recv,
+        out_local,
+    )
+    loads = [
+        pltpu.make_async_copy(
+            att_in.at[:, pl.ds(block * bq, bq)], att_ref.at[block % 2], att_sem.at[block]
+        )
+        for block in range(blocks)
+    ]
+    for load in loads[:2]:
+        load.start()
+    start_together(True)
+    for start, _, _ in incoming:
+        start()
+    work, last = scatter_work(plan, arrays, spacing, (sources, outs, scatter_refs))
+    dk_ref[...] = jnp.zeros_like(dk_ref)
+    dv_ref[...] = jnp.zeros_like(dv_ref)
+    dtab_ref[...] = jnp.zeros_like(dtab_ref)
+    bias_ref[...] = jnp.zeros_like(bias_ref)
+    for turn in range(turns_of(work, spacing)):
+        run_turn(work, spacing, turn, last)
+        for block in range(blocks):
+            if block_turns[block] != turn:
+                continue
+            if block == 0:
+                for _, arrive, _ in incoming:
+                    arrive()
+            loads[block].wait()
+            attend_back(
+                length,
+                bq,
+                hp,
+                vd,
+                block,
+                x_ref,
+                tab_ref,
+                att_ref.at[block % 2],
+                gm_ref,
+                ret_ref,
+                (dk_ref, dv_ref, dtab_ref, bias_ref),
             )
-        lone = (1,) * bits if all(lasts) else cube
-        from_chips.append(pltpu.VMEM((slots, 2 * (chips - 1)) + lone + (rows, width), bfloat))
-    kinds = 2 * (chips - 1) + 2 * bits + 1
+            if block + 2 < blocks:
+                loads[block + 2].start()
+            if block == blocks - 1:
+                ret_ref[:, hk : 2 * hk] = dk_ref[...].T.astype(bfloat)
+                ret_ref[:, 2 * hk :] = dv_ref[...].T.astype(bfloat)
+                for start, _, _ in leaving:
+                    start()
+    for _, arrive, _ in leaving:
+        arrive()
+    for _, _, finish in incoming + leaving:
+        finish()
+    finish_sends(work)
+
+
+def scatter_and_attend_back(
+    grads, widths, lines_last, spacing, block_turns, leaving, x, tab, attention, dims
+):
+    hp, vd, bq = dims
+    peers, rows, _ = leaving.shape
+    length = peers * rows
+    hk = hp * KD
+    back = 2 * hk + hp * vd
+    plan, arrays = scatter_plan(grads, widths, lines_last)
+    flat, specs = flat_sources(grads)
+    anywhere = pl.BlockSpec(memory_space=pl.ANY)
+    vmem = pl.BlockSpec(memory_space=pltpu.VMEM)
+    dma = pltpu.SemaphoreType.DMA
     return pl.pallas_call(
-        functools.partial(scatter_kernel, tuple(plan), tuple(arrays), spacing),
-        in_specs=[pl.BlockSpec(memory_space=pl.ANY)] * len(grads),
-        out_specs=[pl.BlockSpec(memory_space=pltpu.VMEM)] * len(grads),
-        out_shape=[jax.ShapeDtypeStruct(g.shape[-2:], single) for g in grads],
-        scratch_shapes=kept
-        + from_core
-        + from_bits
-        + from_chips
+        functools.partial(attend_back_kernel, plan, arrays, spacing, block_turns, dims),
+        in_specs=specs + [anywhere, vmem, vmem, anywhere],
+        out_specs=[vmem] * len(grads) + [anywhere, vmem, vmem],
+        out_shape=[jax.ShapeDtypeStruct((a[0], a[1] * a[2]), single) for a in arrays]
         + [
-            pltpu.SemaphoreType.DMA((len(plan), kinds)),
-            pltpu.SemaphoreType.DMA((len(plan), kinds)),
-            pltpu.SemaphoreType.DMA((len(plan),)),
+            jax.ShapeDtypeStruct((peers, rows, back), bfloat),
+            jax.ShapeDtypeStruct(tab.shape, single),
+            jax.ShapeDtypeStruct((8, hk), single),
         ],
+        scratch_shapes=[
+            pltpu.VMEM((length, hp * vd), bfloat),
+            pltpu.VMEM((length, back), bfloat),
+            pltpu.VMEM((2, hp, bq, length), bfloat),
+            pltpu.VMEM((hk, length), single),
+            pltpu.VMEM((hp * vd, length), single),
+        ]
+        + scatter_scratch(plan, arrays, spacing)
+        + [dma((peers,))] * 6
+        + [dma((length // bq,))],
         compiler_params=pltpu.CompilerParams(
-            collective_id=collective_id, has_side_effects=True, vmem_limit_bytes=60 * 2**20
+            collective_id=2, has_side_effects=True, vmem_limit_bytes=VMEM_LIMIT
         ),
-    )(*grads)
-
-
-def exchange(blocks):
-    size = lax.axis_size("seq")
-    here = lax.axis_index("seq")
-    out = place(jnp.zeros(blocks.shape, blocks.dtype), pick(blocks, here, 0), here, 0)
-    for distance in range(1, size):
-        peer = here ^ distance
-        out = place(out, swap_seq(pick(blocks, peer, 0), distance), peer, 0)
-    return out
+    )(*flat, leaving, x, tab, attention)
 
 
 def shards(
@@ -825,6 +938,8 @@
     grid = (win_size // CORES, CORES) + (2,) * (seq_size.bit_length() - 1)
 
     def weight_grad(left, right):
+        if left.shape[1] // devices % 16 == 0:
+            return left, right
         grad = jnp.einsum("td,te->de", left, right, preferred_element_type=single).astype(bfloat)
         rows, cols = grad.shape
         return grad.reshape(grid + (rows // devices, cols))
@@ -835,9 +950,6 @@
     grad_act = jnp.einsum("td,fd->tf", cot_rows, whole_mlp, preferred_element_type=single)
     grad_pre = gelu_back(grad_act)[0].astype(bfloat)
     grad_in = weight_grad(normed_two, grad_pre)
-    grad_mlp, grad_in = scatter_all(
-        (grad_mlp, grad_in), (256, 512), lambda number: number % 4 != 0, 2, 2
-    )
     grad_bias_in = jnp.sum(grad_pre.astype(single), axis=0)
     grad_normed_two = jnp.einsum("tf,df->td", grad_pre, whole_in, preferred_element_type=single)
     hidden_term, grad_ln2_gain, grad_ln2_shift = norm_two_back(grad_normed_two)
@@ -849,14 +961,19 @@
         "te,de->td", grad_branch, whole_out, preferred_element_type=single
     ).astype(bfloat)
     grad_mixed = jnp.transpose(grad_mixed.reshape(tokens, seq_size, hp * vd), (1, 0, 2))
-    grad_heads = exchange(grad_mixed).reshape(seq_size * tokens, hp * vd)
-    grad_q, grad_kv, grad_table, grad_bias = attention_backward(
-        heads_in, table, attention, grad_heads, hp, vd, BLOCK_Q
+    grad_mlp, grad_in, returned, grad_table, grad_bias = scatter_and_attend_back(
+        (grad_mlp, grad_in),
+        (256, 512),
+        lambda number: number % 4 != 0,
+        2,
+        BLOCK_TURNS,
+        grad_mixed,
+        heads_in,
+        table,
+        attention,
+        (hp, vd, BLOCK_Q),
     )
     own = hp * KD
-    returned = exchange(
-        jnp.concatenate([grad_q, grad_kv], axis=1).reshape(seq_size, tokens, 2 * own + hp * vd)
-    )
     returned = jnp.transpose(returned, (1, 0, 2))
     grad_qk_rows = jnp.concatenate(
         [

time: 572 us -> 489 us (0.85)
  local copies, waits for them, and re-layouts: 71.8 us -> 33.8 us
  matrix products: 88.9 us -> 60 us
  waiting for transfers between devices: 11.1 us -> 0 us
  Pallas kernels: 359 us -> 367 us
  starting transfers between devices: 7.04 us -> 0 us
    dot_general x5 -> x0, matrix products: 31.7 us -> none  [weight_grad(): jnp.einsum('td,te->de', left, right, preferred_element_type=single)]
    ppermute x6 -> x0, waiting for transfers between devices: 11.1 us -> none  [swap_seq(): return lax.ppermute(value, 'seq', [(i, i ^ distance) for i in range(size)])]
    pallas_call x3 -> x2, Pallas kernels: 176 us -> 185 us  [the longest x1 119 us: scatter_and_attend_back(): pl.pallas_call(functools.partial(attend_back_kernel, plan, arrays, spacin...]
    unnamed x145 -> x150, local copies, waits for them, and re-layouts: 20.4 us -> 12.7 us
    ppermute x6 -> x0, starting transfers between devices: 7.04 us -> none  [swap_seq(): return lax.ppermute(value, 'seq', [(i, i ^ distance) for i in range(size)])]
    another operation x3 -> x2, local copies, waits for them, and re-layouts: 6.03 us -> 0.01 us
    concatenate x1, local copies, waits for them, and re-layouts: 6.09 us -> 0.09 us  [shards(): packed = jnp.concatenate(vectors + (w_rel.T.reshape(-1),))]
  transfers between devices with their start and end apart: 6 -> 0, of which waited for: 2 -> 0; matrix products, arithmetic and copies ran while one was open for 9% -> 0% of each run, Pallas kernels for 15% -> 0%
where the time goes in v4:
time: 489 us; the launch traced here: 482 us
  Pallas kernels  367 us (75%)
  matrix products  60 us (12%)
  local copies, waits for them, and re-layouts  33.8 us (7%)
  other arithmetic  18.8 us (4%)
    pallas_call x1, Pallas kernels, gather_and_attend(): pl.pallas_call(functools.partial(attend_kernel, plan, count, spacing, fir...  135 us
    pallas_call x1, Pallas kernels, scatter_and_attend_back(): pl.pallas_call(functools.partial(attend_back_kernel, plan, arrays, spacin...  119 us
    pallas_call x1, Pallas kernels, scatter_all(): pl.pallas_call(functools.partial(scatter_kernel, plan, arrays, spacing),...  66.2 us
    pallas_call x1, Pallas kernels, gather_all(): pl.pallas_call(functools.partial(gather_kernel, plan, len(shards), spacin...  47.9 us
    unnamed x150, local copies, waits for them, and re-layouts  12.7 us
    dot_general x1, matrix products, shards(): jnp.dot(normed_two, whole_in, preferred_element_type=single) + bias_in  10.5 us

profile of v4, /device:TPU:0, one launch (start us, length us, event | category | flops | bytes accessed | tf_op | source)
XLA Modules:
  0.0 481.7 jit_solution(1328912754391252184)
XLA Ops:
  3.4 47.9 %shard_map.313 = (bf16[4,2,2,2,16,256]{5,4,3,2,1,0:T(8,128)(2,1)}, bf16[4,2,2,2,48,1024]{5,4,3,2,1,0:T(8,128)(2,1)}, bf16[4,2,2,2,48,1536]{5,4,3,2,1,0:T(8,128)(2,1)}) custom-call(bf16[16,256]{1,0:T(8,128)(2,1)} %reshape.378.refs_0_, bf16[48,1024]{1,0:T(8,128)(2,1)} %pad_maximum_fusion.refs_1_, bf16[48,1536]{1,0:T(8,128)(2,1)} %refs_2_.2), custom_call_target="tpu_custom_call" | custom-call | tf_op jit(solution)/shard_map/pallas_call | solution.py:317
  51.3 1.0 copy.76
  52.7 1.3 convolution_convert_fusion.refs_4_.refs_6_
  56.2 4.5 fusion.54
  60.9 1.3 add_convert_fusion.2
  62.4 0.9 copy.60
  63.6 0.9 copy.61
  64.5 1.2 slice.173
  65.9 0.9 copy.62
  66.8 4.4 convolution_convert_fusion.2
  72.8 2.9 maximum_bitcast_fusion.refs_3_
  75.6 134.6 %shard_map.314 = (bf16[4,2,2,2,48,1536]{5,4,3,2,1,0:T(8,128)(2,1)}, bf16[4,2,2,2,48,3072]{5,4,3,2,1,0:T(8,128)(2,1)}, bf16[4,2,2,2,96,1536]{5,4,3,2,1,0:T(8,128)...) custom-call(bf16[48,1536]{1,0:T(8,128)(2,1)} %refs_0_.1, ...), custom_call_target="tpu_custom_call" | custom-call | tf_op jit(solution)/shard_map/pallas_call | solution.py:434
  210.3 2.4 copy.72
  212.8 4.8 fusion.68
  218.5 1.5 add_convert_fusion.refs_2_
  221.5 10.5 %multiply_convert_fusion = (bf16[384,3072]{1,0:T(8,128)(2,1)}, f32[384,3072]{1,0:T(8,128)S(1)}) fusion(f32[3072]{0:T(1024)} %reshape.418, bf16[384,1536]{1,0:T(8,128)(2,1)} %add_convert_fusion.refs_2_, bf16[1536,3072]{1,0:T(8,128)(2,1)} %bitcast.155), kind=kOutput, calls=%fused_computation.14 | convolution fusion | flops 3635675136 | bytes 17707008 | tf_op jit(solution)/shard_map/dot_general | solution.py:932
  232.0 9.5 %fusion.69 = (bf16[3072]{0:T(1024)(128)(2,1)}, bf16[384,3072]{1,0:T(8,128)(2,1)S(1)}) fusion(f32[384,3072]{1,0:T(8,128)S(1)} %get-tuple-element.105, bf16[3072,1536]{1,0:T(8,128)(2,1)} %bitcast.153, bf16[1,384,1536]{2,1,0:T(8,128)(2,1)S(1)} %copy-done.3), kind=kOutput, calls=%fused_computation.134 | convolution fusion | flops 3648648192 | bytes 17700864 | tf_op jit(solution)/shard_map/td,fd->tf/dot_general | solution.py:950
  241.6 4.9 %multiply_reduce_fusion = (bf16[1536]{0:T(1024)(128)(2,1)}, f32[384]{0:T(512)S(1)}, bf16[1536]{0:T(1024)(128)(2,1)}, f32[384,1536]{1,0:T(8,128)S(1)}) fusion(f32[384,1536]{1,0:T(8,128)S(1)} %get-tuple-element.103, f32[384]{0:T(512)S(1)} %copy-done.40, f32[384]{0:T(512)S(1)} %copy-done.32, f32[1536]{0:T(1024)S(1)} %reshape.416, ...), kind=kOutput, calls=%fused_computation.53 | convolution fusion | flops 3628593664 | bytes 16531968 | tf_op jit(solution)/shard_map/tf,df->td/dot_general | solution.py:954
  248.6 1.0 copy-done.8
  249.6 4.4 convolution_convert_fusion.1
  254.8 1.4 copy.66
  256.2 118.7 %shard_map.315 = (f32[96,1536]{1,0:T(8,128)}, f32[48,3072]{1,0:T(8,128)}, bf16[4,384,640]{2,1,0:T(8,128)(2,1)}, f32[128,3072]{1,0:T(8,128)}, f32[8,128]{1,0:T(8,128)}) custom-call(bf16[384,3072]{1,0:T(8,128)(2,1)} %get-tuple-element.104.refs_0_, bf16[384,1536]{1,0:T(8,128)(2,1)} %bitcast.125, bf16[384,1536]{1,0:T(8,128)(2,1)} %add_convert_fusion.refs_2_, ...), custom_call_target="tpu_custom_call" | custom-call | tf_op jit(solution)/shard_map/pallas_call | solution.py:794
  374.9 1.3 slice_bitcast_fusion.1
  377.0 1.4 fusion.70
  379.4 1.2 copy-done.6
  380.6 2.3 fusion.59
  383.0 2.2 fusion.23
  385.5 2.8 convolution_dynamic-update-slice_fusion
  392.0 66.2 %shard_map.316 = (f32[48,1536]{1,0:T(8,128)}, f32[48,1024]{1,0:T(8,128)}, f32[48,1536]{1,0:T(8,128)}, f32[16,256]{1,0:T(8,128)}) custom-call(bf16[384,1536]{1,0:T(8,128)(2,1)} %bitcast.130, bf16[384,1536]{1,0:T(8,128)(2,1)} %copy-done.8, bf16[384,1536]{1,0:T(8,128)(2,1)} %get-tuple-element.74.refs_2_.refs_4_, bf16[384,1024]{1,0:T(8,128)(2,1)} %copy-done.12, ...), custom_call_target="tpu_custom_call" | custom-call | tf_op jit(solution)/shard_map/pallas_call | solution.py:691
  458.2 1.6 fusion.65
  463.0 5.3 %add_bitcast_fusion = f32[1,384,1536]{2,1,0:T(8,128)} fusion(f32[384,1536]{1,0:T(8,128)} %copy-done.2, f32[384]{0:T(512)S(1)} %negate_multiply_fusion, f32[384]{0:T(512)S(1)} %copy-done.46, bf16[1,384,1536]{2,1,0:T(8,128)(2,1)S(1)} %copy-done.4, f32[384]{0:T(512)} %copy-done.47, f32[384]{0:T(512)S(1)} %copy-done.38, bf16[1,384,1536]{2,1,0:T(8,128)(2,1)} %param.22, ...), kind=kLoop, calls=%fused_computation.54 | loop fusion | flops 7077888 | bytes 9451008 | tf_op jit(solution)/shard_map/reshape | solution.py:992
  469.2 9.3 %fusion.20 = bf16[1,384,1536]{2,1,0:T(8,128)(2,1)} fusion(f32[384,1536]{1,0:T(8,128)S(1)} %copy-done.1, bf16[384,3072]{1,0:T(8,128)(2,1)} %get-tuple-element.104.refs_0_, bf16[3072,1536]{1,0:T(8,128)(2,1)} %bitcast.154, f32[1536]{0:T(1024)S(1)} %reshape.419), kind=kOutput, calls=%fused_computation.37 | convolution fusion | flops 3625648128 | bytes 15341568 | tf_op jit(solution)/shard_map/dot_general | solution.py:935
  (223 shorter events, 25.3 us)
Async XLA Ops:
  1.5 52.6 %copy-start.22 = (bf16[3071,32]{0,1:T(8,128)(2,1)}, bf16[3071,32]{0,1:T(8,128)(2,1)S(1)}, u32[]{:S(2)}) copy-start(bf16[3071,32]{0,1:T(8,128)(2,1)S(1)} %get-tuple-element.95) | copy-start | bytes 589636
  1.5 52.5 %copy-start.24 = (bf16[3071,32]{0,1:T(8,128)(2,1)}, bf16[3071,32]{0,1:T(8,128)(2,1)S(1)}, u32[]{:S(2)}) copy-start(bf16[3071,32]{0,1:T(8,128)(2,1)S(1)} %get-tuple-element.100) | copy-start | bytes 589636
  1.6 52.4 %copy-start.20 = (bf16[3071,32]{0,1:T(8,128)(2,1)}, bf16[3071,32]{0,1:T(8,128)(2,1)S(1)}, u32[]{:S(2)}) copy-start(bf16[3071,32]{0,1:T(8,128)(2,1)S(1)} %get-tuple-element.97) | copy-start | bytes 589636
  1.7 52.3 %copy-start.14 = (bf16[3071,96]{0,1:T(8,128)(2,1)}, bf16[3071,96]{0,1:T(8,128)(2,1)S(1)}, u32[]{:S(2)}) copy-start(bf16[3071,96]{0,1:T(8,128)(2,1)S(1)} %fusion.39) | copy-start | bytes 1768900
  52.3 8.4 %copy-start.13 = (bf16[4,8,16,256]{3,1,2,0:T(8,128)(2,1)}, bf16[4,8,16,256]{3,1,2,0:T(8,128)(2,1)S(1)}, u32[]{:S(2)}) copy-start(bf16[4,8,16,256]{3,1,2,0:T(8,128)(2,1)S(1)} %copy.76) | copy-start | bytes 786436
  54.9 12.0 %copy-start.33 = (f32[1536]{0:T(1024)}, f32[1536]{0:T(1024)S(1)}, u32[]{:S(2)}) copy-start(f32[1536]{0:T(1024)S(1)} %reshape.412) | copy-start | bytes 18436
  62.4 4.4 copy-start.36
  62.4 4.4 copy-start.49
  75.6 137.1 %copy-start.28 = (f32[32,48]{1,0:T(8,128)S(1)}, f32[32,48]{1,0:T(8,128)}, u32[]{:S(2)}) copy-start(f32[32,48]{1,0:T(8,128)} %get-tuple-element.78) | copy-start | bytes 18436
  217.6 28.9 %copy-start = (f32[384,1536]{1,0:T(8,128)}, f32[384,1536]{1,0:T(8,128)S(1)}, u32[]{:S(2)}) copy-start(f32[384,1536]{1,0:T(8,128)S(1)} %get-tuple-element.103) | copy-start | bytes 7077892
  218.0 2.8 copy-start.43
  218.0 2.8 copy-start.39
  221.5 10.5 %copy-start.3 = (bf16[1,384,1536]{2,1,0:T(8,128)(2,1)S(1)}, bf16[1,384,1536]{2,1,0:T(8,128)(2,1)}, u32[]{:S(2)}) copy-start(bf16[1,384,1536]{2,1,0:T(8,128)(2,1)} %param.23) | copy-start | bytes 3538948
  221.5 20.1 %slice-start = ((s8[9437184]{0:T(1024)(128)(4,1)}), s8[4194304]{0:T(1024)(128)(4,1)S(1)}, s32[]{:S(2)}) async-start(s8[9437184]{0:T(1024)(128)(4,1)} %bitcast.156), calls=%async_computation | async-start | bytes 8388608
  221.5 20.1 %slice-start.1 = ((s8[9437184]{0:T(1024)(128)(4,1)}), s8[4194304]{0:T(1024)(128)(4,1)S(1)}, s32[]{:S(2)}) async-start(s8[9437184]{0:T(1024)(128)(4,1)} %bitcast.156), calls=%async_computation.1 | async-start | bytes 8388608
  232.0 9.5 %copy-start.32 = (f32[384]{0:T(512)S(1)}, f32[384]{0:T(512)}, u32[]{:S(2)}) copy-start(f32[384]{0:T(512)} %copy-done.31) | copy-start | bytes 4612
  232.0 9.5 %copy-start.40 = (f32[384]{0:T(512)S(1)}, f32[384]{0:T(512)}, u32[]{:S(2)}) copy-start(f32[384]{0:T(512)} %copy-done.39) | copy-start | bytes 4612
  232.0 9.5 %slice-start.2 = ((s8[9437184]{0:T(1024)(128)(4,1)}), s8[1048576]{0:T(1024)(128)(4,1)S(1)}, s32[]{:S(2)}) async-start(s8[9437184]{0:T(1024)(128)(4,1)} %bitcast.156), calls=%async_computation.2 | async-start | bytes 2097152
  241.5 4.9 %copy-start.10 = (bf16[384,3072]{1,0:T(8,128)(2,1)}, bf16[384,3072]{1,0:T(8,128)(2,1)S(1)}, u32[]{:S(2)}) copy-start(bf16[384,3072]{1,0:T(8,128)(2,1)S(1)} %get-tuple-element.109.refs_3_) | copy-start | bytes 7077892
  241.6 4.9 %copy-start.44 = (f32[384]{0:T(512)S(1)}, f32[384]{0:T(512)}, u32[]{:S(2)}) copy-start(f32[384]{0:T(512)} %copy-done.43) | copy-start | bytes 4612
  374.9 4.5 slice-start.3
  379.4 3.5 copy-start.9
  385.5 4.9 %copy-start.54 = (bf16[1536]{0:T(1024)(128)(2,1)S(1)}, bf16[1536]{0:T(1024)(128)(2,1)}, u32[]{:S(2)}) copy-start(bf16[1536]{0:T(1024)(128)(2,1)} %get-tuple-element.56) | copy-start | bytes 9220
  385.5 5.0 %copy-start.53 = (bf16[1536]{0:T(1024)(128)(2,1)S(1)}, bf16[1536]{0:T(1024)(128)(2,1)}, u32[]{:S(2)}) copy-start(bf16[1536]{0:T(1024)(128)(2,1)} %get-tuple-element.60) | copy-start | bytes 9220
  385.5 5.1 %copy-start.52 = (bf16[3072]{0:T(1024)(128)(2,1)S(1)}, bf16[3072]{0:T(1024)(128)(2,1)}, u32[]{:S(2)}) copy-start(bf16[3072]{0:T(1024)(128)(2,1)} %get-tuple-element.108) | copy-start | bytes 18436
  385.5 5.2 %copy-start.4 = (bf16[1,384,1536]{2,1,0:T(8,128)(2,1)S(1)}, bf16[1,384,1536]{2,1,0:T(8,128)(2,1)}, u32[]{:S(2)}) copy-start(bf16[1,384,1536]{2,1,0:T(8,128)(2,1)} %param.23) | copy-start | bytes 3538948
  392.0 71.1 %copy-start.38 = (f32[384]{0:T(512)S(1)}, f32[384]{0:T(512)}, u32[]{:S(2)}) copy-start(f32[384]{0:T(512)} %copy-done.35) | copy-start | bytes 4612
  392.0 71.1 %copy-start.46 = (f32[384]{0:T(512)S(1)}, f32[384]{0:T(512)}, u32[]{:S(2)}) copy-start(f32[384]{0:T(512)} %copy-done.45) | copy-start | bytes 4612
  463.0 6.1 %copy-start.1 = (f32[384,1536]{1,0:T(8,128)S(1)}, f32[384,1536]{1,0:T(8,128)}, u32[]{:S(2)}) copy-start(f32[384,1536]{1,0:T(8,128)} %copy-done) | copy-start | bytes 7077892
  469.1 9.3 %copy-start.19 = (f32[48,1536]{1,0:T(8,128)S(1)}, f32[48,1536]{1,0:T(8,128)}, u32[]{:S(2)}) copy-start(f32[48,1536]{1,0:T(8,128)} %get-tuple-element.137) | copy-start | bytes 884740
  469.2 10.1 %copy-start.18 = (f32[48,1536]{1,0:T(8,128)S(1)}, f32[48,1536]{1,0:T(8,128)}, u32[]{:S(2)}) copy-start(f32[48,1536]{1,0:T(8,128)} %get-tuple-element.141) | copy-start | bytes 884740
  469.2 10.8 %copy-start.17 = (f32[48,3072]{1,0:T(8,128)S(1)}, f32[48,3072]{1,0:T(8,128)}, u32[]{:S(2)}) copy-start(f32[48,3072]{1,0:T(8,128)} %get-tuple-element.145) | copy-start | bytes 1769476
  (38 other events, 67.3 us)

commit v5 on v4

--- a/solution.py
+++ b/solution.py
@@ -15,7 +15,7 @@
 CORES = 2
 BLOCK_Q = 256
 FIRST_BLOCK_TURN = 8
-BLOCK_TURNS = (4, 6, 8, 10, 12, 13)
+BLOCK_TURNS = (6, 8, 10, 12, 14, 16)
 VMEM_LIMIT = 62 * 2**20
 bfloat = jnp.bfloat16
 single = jnp.float32
@@ -361,15 +361,97 @@
     return items
 
 
+def gelu_parts(v):
+    root = math.sqrt(2.0 / math.pi)
+    t = jnp.tanh(root * (v + 0.044715 * (v * v * v)))
+    cdf = 0.5 * (1.0 + t)
+    slope = cdf + 0.5 * v * (1.0 - t * t) * (root * (1.0 + 3 * 0.044715 * (v * v)))
+    return v * cdf, slope
+
+
+def ffn_tasks(plan, gathered, received, ins, outs, scratch):
+    source, cot, vectors, bias_in = ins
+    attended, hidden_in, normed_two, activation, grad_pre, layer_out = outs
+    slope, grad_act, rings, load_sem = scratch
+    peers = received.shape[0]
+    tokens, width = source.shape
+    last = {chunk[0]: number for number, chunk in enumerate(plan)}
+    first = {}
+    for number, chunk in enumerate(plan):
+        first.setdefault(chunk[0], number)
+
+    def task(number, chunk):
+        which, col, cols, _ = chunk
+        ring = rings[which]
+        held = ring.at[number % 2]
+        columns = pl.ds(col, cols)
+        lead = (slice(None),) * (len(ring.shape) - 2)
+        load = pltpu.make_async_copy(
+            gathered[which].at[lead + (columns,)], held, load_sem.at[number]
+        )
+
+        def weight():
+            return held[...].reshape(math.prod(ring.shape[1:-1]), cols)
+
+        def project():
+            if number == first[which]:
+                attended[...] = jnp.concatenate([received[peer] for peer in range(peers)], axis=1)
+            branch = jnp.dot(attended[...], weight(), preferred_element_type=single)
+            hidden_in[:, columns] = (
+                source[:, columns].astype(single) + branch + vectors[0:1, columns]
+            )
+            if number == last[which]:
+                normed = layer_norm(hidden_in[...], vectors[1:2, :], vectors[2:3, :])
+                normed_two[...] = normed.astype(bfloat)
+
+        def widen():
+            pre = jnp.dot(normed_two[...], weight(), preferred_element_type=single)
+            value, derivative = gelu_parts(pre + bias_in[0:1, columns])
+            activation[:, columns] = value.astype(bfloat)
+            slope[:, columns] = derivative
+
+        def narrow():
+            w = weight()
+            out = jnp.dot(activation[...], w, preferred_element_type=single)
+            out = hidden_in[:, columns] + out + vectors[3:4, columns]
+            layer_out[:, columns] = out.astype(bfloat)
+            back = lax.dot_general(
+                cot[:, columns], w, (((1,), (1,)), ((), ())), preferred_element_type=single
+            )
+            if number != first[which]:
+                back = grad_act[...] + back
+            if number == last[which]:
+                grad_pre[...] = (back * slope[...]).astype(bfloat)
+            else:
+                grad_act[...] = back
+
+        return load, (project, widen, narrow)[which]
+
+    return [task(number, chunk) for number, chunk in enumerate(plan)]
+
+
 def attend_kernel(plan, count, spacing, first_turn, dims, *refs):
-    hp, vd, bq = dims
+    hp, vd, bq, ffn = dims
     shards, (outgoing, tab_ref), refs = refs[:count], refs[count : count + 2], refs[count + 2 :]
-    outs, (x_ref, att_out, attended), refs = refs[:count], refs[count : count + 3], refs[count + 3 :]
+    if ffn:
+        ffn_ins, refs = refs[:4], refs[4:]
+    outs, (x_ref, att_out), refs = refs[:count], refs[count : count + 2], refs[count + 2 :]
+    if not ffn:
+        received, refs = refs[0], refs[1:]
+    else:
+        ffn_outs, refs = refs[:6], refs[6:]
+        (slope, grad_act, *rings, load_sem), refs = refs[: 3 + count], refs[3 + count :]
+        received, refs = refs[0], refs[1:]
     att_ref, mixed_ref, *gather_refs = refs[:-7]
     in_send, in_recv, in_local, out_send, out_recv, out_local, att_sem = refs[-7:]
     length = x_ref.shape[0]
     peers, rows = outgoing.shape[0], outgoing.shape[1]
     own, work = gather_work(plan, shards, outs, *gather_refs)
+    tasks = []
+    if ffn:
+        tasks = ffn_tasks(
+            plan, outs, received, ffn_ins, ffn_outs, (slope, grad_act, rings, load_sem)
+        )
     incoming = exchange_work(
         [outgoing.at[peer] for peer in range(peers)],
         lambda peer: x_ref.at[pl.ds(peer * rows, rows)],
@@ -379,7 +461,7 @@
     )
     leaving = exchange_work(
         [mixed_ref.at[pl.ds(peer * rows, rows)] for peer in range(peers)],
-        lambda peer: attended.at[peer],
+        lambda peer: received.at[peer],
         out_send,
         out_recv,
         out_local,
@@ -398,9 +480,10 @@
         )
         for block in range(blocks)
     ]
-    sent = 0
+    sent = loaded = done = 0
+    arrived = set()
     for turn in range(turns_of(work, spacing)):
-        run_turn(work, spacing, turn)
+        run_turn(work, spacing, turn, arrived.add)
         block = turn - first_turn
         if block == 0:
             for _, arrive, _ in incoming:
@@ -413,8 +496,26 @@
             while sent < peers and (sent + 1) * rows <= (block + 1) * bq:
                 leaving[sent][0]()
                 sent += 1
-    for _, arrive, _ in leaving:
-        arrive()
+        if block >= blocks and done < loaded:
+            if done == 0:
+                for _, arrive, _ in leaving:
+                    arrive()
+            tasks[done][0].wait()
+            tasks[done][1]()
+            done += 1
+        while loaded < len(tasks) and loaded in arrived and loaded < done + 2:
+            tasks[loaded][0].start()
+            loaded += 1
+    if done == 0:
+        for _, arrive, _ in leaving:
+            arrive()
+    while done < len(tasks):
+        while loaded < len(tasks) and loaded < done + 2:
+            tasks[loaded][0].start()
+            loaded += 1
+        tasks[done][0].wait()
+        tasks[done][1]()
+        done += 1
     for _, _, finish in incoming + leaving:
         finish()
     for item in kept[-2:]:
@@ -422,8 +523,8 @@
     finish_sends(work)
 
 
-def gather_and_attend(shards, widths, lines_first, spacing, first_turn, outgoing, tab, dims):
-    hp, vd, bq = dims
+def gather_and_attend(shards, widths, lines_first, spacing, first_turn, outgoing, tab, ffn_ins, dims):
+    hp, vd, bq, ffn = dims
     peers, rows, cols = outgoing.shape
     length = peers * rows
     plan = gather_plan(shards, widths, lines_first)
@@ -431,17 +532,37 @@
     anywhere = pl.BlockSpec(memory_space=pl.ANY)
     vmem = pl.BlockSpec(memory_space=pltpu.VMEM)
     dma = pltpu.SemaphoreType.DMA
-    return pl.pallas_call(
+    gathered = gathered_shapes(shards)
+    extra_out, extra_scratch = [], []
+    if ffn:
+        width, hidden = ffn_ins[0].shape[1], ffn_ins[3].shape[1]
+        extra_out = [
+            jax.ShapeDtypeStruct((rows, width), bfloat),
+            jax.ShapeDtypeStruct((rows, width), single),
+            jax.ShapeDtypeStruct((rows, width), bfloat),
+            jax.ShapeDtypeStruct((rows, hidden), bfloat),
+            jax.ShapeDtypeStruct((rows, hidden), bfloat),
+            jax.ShapeDtypeStruct((rows, width), bfloat),
+        ]
+        extra_scratch = [pltpu.VMEM((rows, hidden), single)] * 2
+        for shape, cut in zip(gathered, widths):
+            extra_scratch.append(pltpu.VMEM((2,) + shape.shape[:-1] + (cut,), bfloat))
+        extra_scratch += [dma((len(plan),)), pltpu.VMEM((peers, rows, hp * vd), bfloat)]
+    else:
+        ffn_ins = ()
+        extra_out = [jax.ShapeDtypeStruct((peers, rows, hp * vd), bfloat)]
+    result = pl.pallas_call(
         functools.partial(attend_kernel, plan, count, spacing, first_turn, dims),
-        in_specs=[vmem] * count + [anywhere, vmem],
-        out_specs=[anywhere] * count + [vmem, anywhere, anywhere],
-        out_shape=gathered_shapes(shards)
+        in_specs=[vmem] * count + [anywhere, vmem] + [vmem] * len(ffn_ins),
+        out_specs=[anywhere] * count + [vmem, anywhere] + [vmem if ffn else anywhere] * len(extra_out),
+        out_shape=gathered
         + [
             jax.ShapeDtypeStruct((length, cols), bfloat),
             jax.ShapeDtypeStruct((hp, length, length), bfloat),
-            jax.ShapeDtypeStruct((peers, rows, hp * vd), bfloat),
-        ],
-        scratch_shapes=[
+        ]
+        + extra_out,
+        scratch_shapes=extra_scratch
+        + [
             pltpu.VMEM((2, hp, bq, length), bfloat),
             pltpu.VMEM((length, hp * vd), bfloat),
         ]
@@ -451,7 +572,8 @@
         compiler_params=pltpu.CompilerParams(
             collective_id=1, has_side_effects=True, vmem_limit_bytes=VMEM_LIMIT
         ),
-    )(*shards, outgoing, tab)
+    )(*shards, outgoing, tab, *ffn_ins)
+    return result[: count + 2], result[count + 2 :]
 
 
 def scatter_work(plan, arrays, spacing, refs):
@@ -848,18 +970,12 @@
     hidden = w_in.shape[1]
     scale_factor = KD ** (-0.5)
 
-    vectors = (
-        ln1_scale,
-        ln1_offset,
-        content_bias,
-        position_bias,
-        b_out,
-        ln2_scale,
-        ln2_offset,
-        b_in,
-        b_mlp_out,
-    )
-    packed = jnp.concatenate(vectors + (w_rel.T.reshape(-1),))
+    wide = (ln1_scale, ln1_offset, b_out, ln2_scale, ln2_offset, b_mlp_out)
+    narrow = (content_bias, position_bias)
+    packed = jnp.concatenate(wide + (b_in,) + narrow + (w_rel.T.reshape(-1),))
+    cuts = [len(wide) * ln1_scale.shape[0]]
+    cuts.append(cuts[0] + b_in.shape[0])
+    cuts.append(cuts[1] + len(narrow) * content_bias.shape[0])
     packed_size = packed.shape[0]
     small_cols = -(-packed_size // 4096) * 256
     small_size = 16 * small_cols
@@ -867,31 +983,23 @@
     packed, whole_qk, whole_v = gather_all(
         (packed, jnp.concatenate([w_query, w_key], axis=1), w_value),
         (256, 512, 512),
-        lambda number: number % 4 != 3,
-        2,
+        lambda number: number % 3 != 2,
+        3,
         0,
     )
     packed = packed.reshape(devices, small_size)
     whole_qk = whole_qk.reshape(width, 2 * hk)
     whole_v = whole_v.reshape(width, width)
-    whole_vectors = []
-    at = 0
-    for vector in vectors:
-        length = vector.shape[0]
-        whole_vectors.append(packed[:, at : at + length].reshape(devices * length).astype(single))
-        at += length
-    whole_rel = packed[:, at:packed_size].reshape(hk, F)
-    (
-        ln1_gain,
-        ln1_shift,
-        bias_content,
-        bias_position,
-        bias_out,
-        ln2_gain,
-        ln2_shift,
-        bias_in,
-        bias_mlp,
-    ) = whole_vectors
+
+    def rows_of(columns, count):
+        rows = columns.reshape(devices, count, -1).transpose(1, 0, 2)
+        return rows.reshape(count, -1).astype(single)
+
+    wide_rows = rows_of(packed[:, : cuts[0]], len(wide))
+    ln1_gain, ln1_shift, bias_out, ln2_gain, ln2_shift, bias_mlp = wide_rows
+    bias_in = packed[:, cuts[0] : cuts[1]].reshape(-1).astype(single)
+    bias_content, bias_position = rows_of(packed[:, cuts[1] : cuts[2]], len(narrow))
+    whole_rel = packed[:, cuts[2] : packed_size].reshape(hk, F)
 
     features = jnp.pad(rel_features(WLEN, F).astype(bfloat), ((0, 1), (0, 0)))
     own_rel = lax.dynamic_slice_in_dim(whole_rel, seq * hp * KD, hp * KD, 0)
@@ -911,29 +1019,39 @@
     )
     outgoing = jnp.concatenate([part.reshape(tokens, seq_size, -1) for part in parts], axis=2)
     outgoing = jnp.transpose(outgoing, (1, 0, 2))
-    whole_out, whole_in, whole_mlp, heads_in, attention, attended = gather_and_attend(
+    in_kernel = w_out.shape[0] % 16 == 0 and hp * vd % 128 == 0
+    row_vectors = wide_rows[2:]
+    cot_rows = cotangent.reshape(tokens, width)
+    first_results, ffn_results = gather_and_attend(
         (w_out, w_in, w_mlp_out),
         (512, 512, 256),
-        lambda number: number % 4 != 3,
+        lambda number: number % 3 != 1,
         3,
         FIRST_BLOCK_TURN,
         outgoing,
         table,
-        (hp, vd, BLOCK_Q),
-    )
+        (inputs.reshape(tokens, width), cot_rows, row_vectors, bias_in[None, :]),
+        (hp, vd, BLOCK_Q, in_kernel),
+    )
+    whole_out, whole_in, whole_mlp, heads_in, attention = first_results
     whole_out = whole_out.reshape(width, width)
     whole_in = whole_in.reshape(width, hidden)
     whole_mlp = whole_mlp.reshape(hidden, width)
-    attended = jnp.transpose(attended, (1, 0, 2)).reshape(tokens, width)
-
-    hidden_in = source + jnp.dot(attended, whole_out, preferred_element_type=single) + bias_out
-    normed_two_f, norm_two_back = jax.vjp(layer_norm, hidden_in, ln2_gain, ln2_shift)
-    normed_two = normed_two_f.astype(bfloat)
-    pre_act = jnp.dot(normed_two, whole_in, preferred_element_type=single) + bias_in
-    gelu_out, gelu_back = jax.vjp(jax.nn.gelu, pre_act)
-    activation = gelu_out.astype(bfloat)
-    result = hidden_in + jnp.dot(activation, whole_mlp, preferred_element_type=single) + bias_mlp
-    layer_out = result.astype(bfloat).reshape(inputs.shape)
+    if in_kernel:
+        attended, hidden_in, normed_two, activation, grad_pre, result = ffn_results
+    else:
+        attended = jnp.transpose(ffn_results[0], (1, 0, 2)).reshape(tokens, width)
+        branch = jnp.dot(attended, whole_out, preferred_element_type=single)
+        hidden_in = source + branch + bias_out
+        normed_two = layer_norm(hidden_in, ln2_gain, ln2_shift).astype(bfloat)
+        pre_act = jnp.dot(normed_two, whole_in, preferred_element_type=single) + bias_in
+        gelu_out, gelu_back = jax.vjp(jax.nn.gelu, pre_act)
+        activation = gelu_out.astype(bfloat)
+        result = hidden_in + jnp.dot(activation, whole_mlp, preferred_element_type=single)
+        result = (result + bias_mlp).astype(bfloat)
+        grad_act = jnp.einsum("td,fd->tf", cot_rows, whole_mlp, preferred_element_type=single)
+        grad_pre = gelu_back(grad_act)[0].astype(bfloat)
+    layer_out = result.reshape(inputs.shape)
 
     grid = (win_size // CORES, CORES) + (2,) * (seq_size.bit_length() - 1)
 
@@ -944,14 +1062,12 @@
         rows, cols = grad.shape
         return grad.reshape(grid + (rows // devices, cols))
 
-    cot_rows = cotangent.reshape(tokens, width)
     grad_mlp = weight_grad(activation, cot_rows)
     grad_bias_mlp = jnp.sum(cot_rows.astype(single), axis=0)
-    grad_act = jnp.einsum("td,fd->tf", cot_rows, whole_mlp, preferred_element_type=single)
-    grad_pre = gelu_back(grad_act)[0].astype(bfloat)
     grad_in = weight_grad(normed_two, grad_pre)
     grad_bias_in = jnp.sum(grad_pre.astype(single), axis=0)
     grad_normed_two = jnp.einsum("tf,df->td", grad_pre, whole_in, preferred_element_type=single)
+    _, norm_two_back = jax.vjp(layer_norm, hidden_in, ln2_gain, ln2_shift)
     hidden_term, grad_ln2_gain, grad_ln2_shift = norm_two_back(grad_normed_two)
     grad_hidden = cot_rows.astype(single) + hidden_term
     grad_branch = grad_hidden.astype(bfloat)
@@ -996,22 +1112,32 @@
         jnp.zeros((hk, F), single), grad_rel, seq * own, 0
     )
 
-    def spread(own_heads):
-        return lax.dynamic_update_slice_in_dim(jnp.zeros((hk,), single), own_heads, seq * own, 0)
-
-    vector_grads = (
-        grad_ln1_gain,
-        grad_ln1_shift,
-        spread(grad_bias[0]),
-        spread(grad_bias[1]),
-        grad_bias_out,
-        grad_ln2_gain,
-        grad_ln2_shift,
-        grad_bias_in,
-        grad_bias_mlp,
-    )
+    wide_grads = jnp.stack(
+        [
+            grad_ln1_gain,
+            grad_ln1_shift,
+            grad_bias_out,
+            grad_ln2_gain,
+            grad_ln2_shift,
+            grad_bias_mlp,
+        ]
+    )
+    narrow_grads = lax.dynamic_update_slice_in_dim(
+        jnp.zeros((len(narrow), hk), single), grad_bias[: len(narrow)], seq * own, 1
+    )
+
+    def by_owner(rows):
+        count = rows.shape[0]
+        return rows.reshape(count, devices, -1).transpose(1, 0, 2).reshape(devices, -1)
+
     small = jnp.concatenate(
-        [v.reshape(devices, -1) for v in vector_grads + (whole_grad_rel,)], axis=1
+        [
+            by_owner(wide_grads),
+            grad_bias_in.reshape(devices, -1),
+            by_owner(narrow_grads),
+            whole_grad_rel.reshape(devices, -1),
+        ],
+        axis=1,
     )
     small = jnp.pad(small, ((0, 0), (0, small_size - packed_size))).astype(bfloat)
     grad_out, grad_qk, grad_v, small = scatter_all(
@@ -1022,33 +1148,28 @@
         3,
     )
     small = small.reshape(-1)[:packed_size]
-    small_grads = []
-    at = 0
-    for vector in vectors:
-        length = vector.shape[0]
-        small_grads.append(small[at : at + length])
-        at += length
-    g = small_grads
-    own_grad_rel = small[at:].reshape(-1, F).T
+    wide_own = small[: cuts[0]].reshape(len(wide), -1)
+    narrow_own = small[cuts[1] : cuts[2]].reshape(len(narrow), -1)
+    own_grad_rel = small[cuts[2] :].reshape(-1, F).T
     return (
         layer_out,
         grad_inputs,
-        g[0],
-        g[1],
+        wide_own[0],
+        wide_own[1],
         grad_qk[:, :hk],
         grad_qk[:, hk:],
         grad_v,
         own_grad_rel,
-        g[2],
-        g[3],
+        narrow_own[0],
+        narrow_own[1],
         grad_out,
-        g[4],
-        g[5],
-        g[6],
+        wide_own[2],
+        wide_own[3],
+        wide_own[4],
         grad_in,
-        g[7],
+        small[cuts[0] : cuts[1]],
         grad_mlp,
-        g[8],
+        wide_own[5],
     )
 
 

time: 489 us -> 465 us (0.951)
  matrix products: 60 us -> 28.7 us
  Pallas kernels: 367 us -> 377 us
    dot_general x4 -> x0, matrix products: 34.1 us -> none  [the longest x1 10.5 us: shards(): jnp.dot(normed_two, whole_in, preferred_element_type=single) + bias_in]
    pallas_call x1, Pallas kernels: 135 us -> 151 us  [gather_and_attend(): pl.pallas_call(functools.partial(attend_kernel, plan, count, spacing, fir...]
    pallas_call x1, Pallas kernels: 119 us -> 111 us  [scatter_and_attend_back(): pl.pallas_call(functools.partial(attend_back_kernel, plan, arrays, spacin...]
    unnamed x150 -> x115, local copies, waits for them, and re-layouts: 12.7 us -> 13.8 us
where the time goes in v5:
time: 465 us; the launch traced here: 458 us
  Pallas kernels  377 us (81%)
  local copies, waits for them, and re-layouts  30.5 us (7%)
  matrix products  28.7 us (6%)
  other arithmetic  19.3 us (4%)
    pallas_call x1, Pallas kernels, gather_and_attend(): pl.pallas_call(functools.partial(attend_kernel, plan, count, spacing, fir...  151 us
    pallas_call x1, Pallas kernels, scatter_and_attend_back(): pl.pallas_call(functools.partial(attend_back_kernel, plan, arrays, spacin...  111 us
    pallas_call x1, Pallas kernels, scatter_all(): pl.pallas_call(functools.partial(scatter_kernel, plan, arrays, spacing),...  67.8 us
    pallas_call x1, Pallas kernels, gather_all(): pl.pallas_call(functools.partial(gather_kernel, plan, len(shards), spacin...  47 us
    unnamed x115, local copies, waits for them, and re-layouts  13.8 us

profile of v5, /device:TPU:0, one launch (start us, length us, event | category | flops | bytes accessed | tf_op | source)
XLA Modules:
  0.0 457.6 jit_solution(12251301054279314411)
XLA Ops:
  3.4 47.0 %shard_map.313 = (bf16[4,2,2,2,16,256]{5,4,3,2,1,0:T(8,128)(2,1)}, bf16[4,2,2,2,48,1024]{5,4,3,2,1,0:T(8,128)(2,1)}, bf16[4,2,2,2,48,1536]{5,4,3,2,1,0:T(8,128)(2,1)}) custom-call(bf16[16,256]{1,0:T(8,128)(2,1)} %reshape.350.refs_0_, bf16[48,1024]{1,0:T(8,128)(2,1)} %pad_maximum_fusion.refs_1_, bf16[48,1536]{1,0:T(8,128)(2,1)} %refs_2_.2), custom_call_target="tpu_custom_call" | custom-call | tf_op jit(solution)/shard_map/pallas_call | solution.py:317
  50.4 1.0 copy.88
  51.9 1.3 convolution_convert_fusion.refs_4_.refs_6_
  55.4 4.5 fusion.34
  60.3 1.3 add_convert_fusion.2
  62.5 1.2 slice.157
  64.1 4.4 convolution_convert_fusion.2
  68.5 0.7 copy.68
  69.2 0.8 copy.72
  70.0 1.6 maximum_bitcast_fusion.refs_3_
  72.4 0.8 slice_convert_fusion.2
  73.9 151.2 %shard_map.314 = (bf16[4,2,2,2,48,1536]{5,4,3,2,1,0:T(8,128)(2,1)}, bf16[4,2,2,2,48,3072]{5,4,3,2,1,0:T(8,128)(2,1)}, bf16[4,2,2,2,96,1536]{5,4,3,2,1,0:T(8,128)...) custom-call(bf16[48,1536]{1,0:T(8,128)(2,1)} %refs_0_.1, ...), custom_call_target="tpu_custom_call" | custom-call | tf_op jit(solution)/shard_map/pallas_call | solution.py:554
  225.1 2.0 reduce_sum.134
  227.9 7.7 %multiply_reduce_fusion = (bf16[1536]{0:T(1024)(128)(2,1)S(1)}, f32[384]{0:T(512)S(1)}, bf16[1536]{0:T(1024)(128)(2,1)S(1)}, f32[384,1536]{1,0:T(8,128)S(1)}) fusion(f32[384,1536]{1,0:T(8,128)S(1)} %copy-done.5, f32[384]{0:T(512)S(1)} %fusion.27, f32[384]{0:T(512)S(1)} %broadcast_multiply_fusion, f32[1536]{0:T(1024)S(1)} %mul.222, ...), kind=kOutput, calls=%fused_computation.25 | convolution fusion | flops 3628593664 | bytes 16531968 | tf_op jit(solution)/shard_map/tf,df->td/dot_general | solution.py:1069
  237.8 1.0 copy-done.7
  238.8 4.4 convolution_convert_fusion.1
  244.0 1.5 copy.75
  245.4 111.4 %shard_map.315 = (f32[96,1536]{1,0:T(8,128)}, f32[48,3072]{1,0:T(8,128)}, bf16[4,384,640]{2,1,0:T(8,128)(2,1)}, f32[128,3072]{1,0:T(8,128)}, f32[8,128]{1,0:T(8,128)}) custom-call(bf16[384,3072]{1,0:T(8,128)(2,1)} %get-tuple-element.49.refs_0_, bf16[384,1536]{1,0:T(8,128)(2,1)} %bitcast.78, bf16[384,1536]{1,0:T(8,128)(2,1)} %get-tuple-element.50.refs_2_, ...), custom_call_target="tpu_custom_call" | custom-call | tf_op jit(solution)/shard_map/pallas_call | solution.py:916
  356.8 1.3 slice_bitcast_fusion.1
  359.0 1.4 fusion.49
  361.3 1.2 copy-done.3
  362.6 2.3 fusion.39
  365.0 2.2 fusion.8
  368.2 2.7 convolution_dynamic-update-slice_fusion
  372.1 2.1 reduce.2
  374.5 0.8 copy.89
  375.3 67.8 %shard_map.316 = (f32[48,1536]{1,0:T(8,128)}, f32[48,1024]{1,0:T(8,128)}, f32[48,1536]{1,0:T(8,128)}, f32[16,256]{1,0:T(8,128)}) custom-call(bf16[384,1536]{1,0:T(8,128)(2,1)} %get-tuple-element.55.refs_0_, bf16[384,1536]{1,0:T(8,128)(2,1)} %copy-done.7, bf16[384,1536]{1,0:T(8,128)(2,1)} %get-tuple-element.85.refs_2_.refs_4_, bf16[384,1024]{1,0:T(8,128)(2,1)} %copy-done.10, ...), custom_call_target="tpu_custom_call" | custom-call | tf_op jit(solution)/shard_map/pallas_call | solution.py:813
  443.1 1.6 fusion.45
  448.0 5.2 %add_bitcast_fusion = f32[1,384,1536]{2,1,0:T(8,128)} fusion(f32[384,1536]{1,0:T(8,128)} %copy-done.4, f32[384]{0:T(512)S(1)} %negate_multiply_fusion, f32[384]{0:T(512)S(1)} %negate_multiply_fusion.1, bf16[1,384,1536]{2,1,0:T(8,128)(2,1)S(1)} %copy-done.1, f32[384]{0:T(512)S(1)} %multiply_multiply_fusion, f32[384]{0:T(512)S(1)} %copy-done.31, ...), kind=kLoop, calls=%fused_computation.26 | loop fusion | flops 7077888 | bytes 9451008 | tf_op jit(solution)/shard_map/reshape | solution.py:1108
  453.2 1.0 copy.106
  455.7 0.8 copy.109
  456.5 0.8 copy.110
  (189 shorter events, 20.8 us)
Async XLA Ops:
  0.7 1.9 copy-start.37
  0.7 1.9 copy-start.38
  0.7 1.9 copy-start.44
  0.7 1.9 copy-start.45
  0.7 1.9 copy-start.39
  0.7 1.9 copy-start.40
  1.5 51.7 %copy-start.23 = (bf16[3071,32]{0,1:T(8,128)(2,1)}, bf16[3071,32]{0,1:T(8,128)(2,1)S(1)}, u32[]{:S(2)}) copy-start(bf16[3071,32]{0,1:T(8,128)(2,1)S(1)} %get-tuple-element.100) | copy-start | bytes 589636
  1.5 51.7 %copy-start.25 = (bf16[3071,32]{0,1:T(8,128)(2,1)}, bf16[3071,32]{0,1:T(8,128)(2,1)S(1)}, u32[]{:S(2)}) copy-start(bf16[3071,32]{0,1:T(8,128)(2,1)S(1)} %get-tuple-element.105) | copy-start | bytes 589636
  1.6 51.5 %copy-start.21 = (bf16[3071,32]{0,1:T(8,128)(2,1)}, bf16[3071,32]{0,1:T(8,128)(2,1)S(1)}, u32[]{:S(2)}) copy-start(bf16[3071,32]{0,1:T(8,128)(2,1)S(1)} %get-tuple-element.102) | copy-start | bytes 589636
  1.7 51.4 %copy-start.13 = (bf16[3071,96]{0,1:T(8,128)(2,1)}, bf16[3071,96]{0,1:T(8,128)(2,1)S(1)}, u32[]{:S(2)}) copy-start(bf16[3071,96]{0,1:T(8,128)(2,1)S(1)} %fusion.20) | copy-start | bytes 1768900
  51.4 8.4 %copy-start.12 = (bf16[4,8,16,256]{3,1,2,0:T(8,128)(2,1)}, bf16[4,8,16,256]{3,1,2,0:T(8,128)(2,1)S(1)}, u32[]{:S(2)}) copy-start(bf16[4,8,16,256]{3,1,2,0:T(8,128)(2,1)S(1)} %copy.88) | copy-start | bytes 786436
  51.8 2.3 copy-start.2
  53.3 6.6 %copy-start.17 = (f32[32,6,48]{2,1,0:T(8,128)}, f32[32,6,48]{2,1,0:T(8,128)S(1)}, u32[]{:S(2)}) copy-start(f32[32,6,48]{2,1,0:T(8,128)S(1)} %reshape.377) | copy-start | bytes 110596
  54.8 5.0 %copy-start.34 = (f32[384]{0:T(512)}, f32[384]{0:T(512)S(1)}, u32[]{:S(2)}) copy-start(f32[384]{0:T(512)S(1)} %fusion.26) | copy-start | bytes 4612
  225.1 2.4 copy-start.5
  225.1 2.7 copy-start.27
  356.8 2.2 copy-start.46
  356.8 4.5 slice-start
  359.0 2.1 copy-start.9
  359.0 2.4 slice-start.1
  361.3 3.5 copy-start.8
  362.5 2.3 copy-start.33
  362.6 2.3 copy-start.35
  364.8 2.3 copy-start.6
  364.9 2.8 copy-start.1
  364.9 3.2 copy-start.14
  364.9 3.2 copy-start.22
  364.9 3.2 copy-start.24
  364.9 3.2 copy-start.26
  448.0 5.2 %copy-start.11 = (bf16[384,1536]{1,0:T(8,128)(2,1)S(1)}, bf16[384,1536]{1,0:T(8,128)(2,1)}, u32[]{:S(2)}) copy-start(bf16[384,1536]{1,0:T(8,128)(2,1)} %get-tuple-element.45) | copy-start | bytes 3538948
  453.2 2.5 copy-start.16
  453.2 3.3 copy-start.15
  (17 other events, 23.4 us)

commit v6 on v5

--- a/solution.py
+++ b/solution.py
@@ -371,10 +371,9 @@
 
 def ffn_tasks(plan, gathered, received, ins, outs, scratch):
     source, cot, vectors, bias_in = ins
-    attended, hidden_in, normed_two, activation, grad_pre, layer_out = outs
-    slope, grad_act, rings, load_sem = scratch
+    attended, hidden_in, normed_two, activation, grad_pre = outs
+    grad_act, rings, load_sem = scratch
     peers = received.shape[0]
-    tokens, width = source.shape
     last = {chunk[0]: number for number, chunk in enumerate(plan)}
     first = {}
     for number, chunk in enumerate(plan):
@@ -404,28 +403,19 @@
                 normed = layer_norm(hidden_in[...], vectors[1:2, :], vectors[2:3, :])
                 normed_two[...] = normed.astype(bfloat)
 
+        def fold():
+            term = lax.dot_general(
+                cot[:, columns], weight(), (((1,), (1,)), ((), ())), preferred_element_type=single
+            )
+            grad_act[...] = term if number == first[which] else grad_act[...] + term
+
         def widen():
             pre = jnp.dot(normed_two[...], weight(), preferred_element_type=single)
             value, derivative = gelu_parts(pre + bias_in[0:1, columns])
             activation[:, columns] = value.astype(bfloat)
-            slope[:, columns] = derivative
-
-        def narrow():
-            w = weight()
-            out = jnp.dot(activation[...], w, preferred_element_type=single)
-            out = hidden_in[:, columns] + out + vectors[3:4, columns]
-            layer_out[:, columns] = out.astype(bfloat)
-            back = lax.dot_general(
-                cot[:, columns], w, (((1,), (1,)), ((), ())), preferred_element_type=single
-            )
-            if number != first[which]:
-                back = grad_act[...] + back
-            if number == last[which]:
-                grad_pre[...] = (back * slope[...]).astype(bfloat)
-            else:
-                grad_act[...] = back
-
-        return load, (project, widen, narrow)[which]
+            grad_pre[:, columns] = (grad_act[:, columns] * derivative).astype(bfloat)
+
+        return load, (project, fold, widen)[which]
 
     return [task(number, chunk) for number, chunk in enumerate(plan)]
 
@@ -439,8 +429,8 @@
     if not ffn:
         received, refs = refs[0], refs[1:]
     else:
-        ffn_outs, refs = refs[:6], refs[6:]
-        (slope, grad_act, *rings, load_sem), refs = refs[: 3 + count], refs[3 + count :]
+        ffn_outs, refs = refs[:5], refs[5:]
+        (grad_act, *rings, load_sem), refs = refs[: 2 + count], refs[2 + count :]
         received, refs = refs[0], refs[1:]
     att_ref, mixed_ref, *gather_refs = refs[:-7]
     in_send, in_recv, in_local, out_send, out_recv, out_local, att_sem = refs[-7:]
@@ -449,9 +439,7 @@
     own, work = gather_work(plan, shards, outs, *gather_refs)
     tasks = []
     if ffn:
-        tasks = ffn_tasks(
-            plan, outs, received, ffn_ins, ffn_outs, (slope, grad_act, rings, load_sem)
-        )
+        tasks = ffn_tasks(plan, outs, received, ffn_ins, ffn_outs, (grad_act, rings, load_sem))
     incoming = exchange_work(
         [outgoing.at[peer] for peer in range(peers)],
         lambda peer: x_ref.at[pl.ds(peer * rows, rows)],
@@ -542,9 +530,8 @@
             jax.ShapeDtypeStruct((rows, width), bfloat),
             jax.ShapeDtypeStruct((rows, hidden), bfloat),
             jax.ShapeDtypeStruct((rows, hidden), bfloat),
-            jax.ShapeDtypeStruct((rows, width), bfloat),
         ]
-        extra_scratch = [pltpu.VMEM((rows, hidden), single)] * 2
+        extra_scratch = [pltpu.VMEM((rows, hidden), single)]
         for shape, cut in zip(gathered, widths):
             extra_scratch.append(pltpu.VMEM((2,) + shape.shape[:-1] + (cut,), bfloat))
         extra_scratch += [dma((len(plan),)), pltpu.VMEM((peers, rows, hp * vd), bfloat)]
@@ -820,6 +807,61 @@
             collective_id=collective_id, has_side_effects=True, vmem_limit_bytes=VMEM_LIMIT
         ),
     )(*flat)
+
+
+def scatter_and_widen_kernel(plan, arrays, spacing, first_turn, cols, *refs):
+    count = len(arrays)
+    sources, refs = group_sources(arrays, refs)
+    (weights, activation, hidden_in, bias), refs = refs[:4], refs[4:]
+    outs, layer_out, ring, load_sem, *refs = refs[:count], *refs[count:]
+    pieces = layer_out.shape[1] // cols
+    lead = (slice(None),) * (len(ring.shape) - 2)
+    loads = [
+        pltpu.make_async_copy(
+            weights.at[lead + (pl.ds(piece * cols, cols),)], ring.at[piece % 2], load_sem.at[piece]
+        )
+        for piece in range(pieces)
+    ]
+    for load in loads[:2]:
+        load.start()
+    start_together()
+    work, last = scatter_work(plan, arrays, spacing, (sources, outs, refs))
+    for turn in range(turns_of(work, spacing)):
+        run_turn(work, spacing, turn, last)
+        piece = turn - first_turn
+        if 0 <= piece < pieces:
+            loads[piece].wait()
+            columns = pl.ds(piece * cols, cols)
+            w = ring[piece % 2].reshape(activation.shape[1], cols)
+            out = jnp.dot(activation[...], w, preferred_element_type=single)
+            out = hidden_in[:, columns] + out + bias[:, columns]
+            layer_out[:, columns] = out.astype(bfloat)
+            if piece + 2 < pieces:
+                loads[piece + 2].start()
+    finish_sends(work)
+
+
+def scatter_and_widen(grads, widths, lines_last, spacing, first_turn, layer_ins, collective_id):
+    weights, activation, hidden_in, _ = layer_ins
+    cols = 256
+    plan, arrays = scatter_plan(grads, widths, lines_last)
+    flat, specs = flat_sources(grads)
+    vmem = pl.BlockSpec(memory_space=pltpu.VMEM)
+    return pl.pallas_call(
+        functools.partial(scatter_and_widen_kernel, plan, arrays, spacing, first_turn, cols),
+        in_specs=specs + [pl.BlockSpec(memory_space=pl.ANY), vmem, vmem, vmem],
+        out_specs=[vmem] * (len(arrays) + 1),
+        out_shape=[jax.ShapeDtypeStruct((a[0], a[1] * a[2]), single) for a in arrays]
+        + [jax.ShapeDtypeStruct(hidden_in.shape, bfloat)],
+        scratch_shapes=[
+            pltpu.VMEM((2,) + weights.shape[:-1] + (cols,), bfloat),
+            pltpu.SemaphoreType.DMA((hidden_in.shape[1] // cols,)),
+        ]
+        + scatter_scratch(plan, arrays, spacing),
+        compiler_params=pltpu.CompilerParams(
+            collective_id=collective_id, has_side_effects=True, vmem_limit_bytes=VMEM_LIMIT
+        ),
+    )(*flat, *layer_ins)
 
 
 def attend_back_kernel(plan, arrays, spacing, block_turns, dims, *refs):
@@ -1023,8 +1065,8 @@
     row_vectors = wide_rows[2:]
     cot_rows = cotangent.reshape(tokens, width)
     first_results, ffn_results = gather_and_attend(
-        (w_out, w_in, w_mlp_out),
-        (512, 512, 256),
+        (w_out, w_mlp_out, w_in),
+        (512, 256, 512),
         lambda number: number % 3 != 1,
         3,
         FIRST_BLOCK_TURN,
@@ -1033,12 +1075,12 @@
         (inputs.reshape(tokens, width), cot_rows, row_vectors, bias_in[None, :]),
         (hp, vd, BLOCK_Q, in_kernel),
     )
-    whole_out, whole_in, whole_mlp, heads_in, attention = first_results
+    whole_out, gathered_mlp, whole_in, heads_in, attention = first_results
     whole_out = whole_out.reshape(width, width)
     whole_in = whole_in.reshape(width, hidden)
-    whole_mlp = whole_mlp.reshape(hidden, width)
+    whole_mlp = gathered_mlp.reshape(hidden, width)
     if in_kernel:
-        attended, hidden_in, normed_two, activation, grad_pre, result = ffn_results
+        attended, hidden_in, normed_two, activation, grad_pre = ffn_results
     else:
         attended = jnp.transpose(ffn_results[0], (1, 0, 2)).reshape(tokens, width)
         branch = jnp.dot(attended, whole_out, preferred_element_type=single)
@@ -1051,7 +1093,6 @@
         result = (result + bias_mlp).astype(bfloat)
         grad_act = jnp.einsum("td,fd->tf", cot_rows, whole_mlp, preferred_element_type=single)
         grad_pre = gelu_back(grad_act)[0].astype(bfloat)
-    layer_out = result.reshape(inputs.shape)
 
     grid = (win_size // CORES, CORES) + (2,) * (seq_size.bit_length() - 1)
 
@@ -1140,13 +1181,18 @@
         axis=1,
     )
     small = jnp.pad(small, ((0, 0), (0, small_size - packed_size))).astype(bfloat)
-    grad_out, grad_qk, grad_v, small = scatter_all(
-        (grad_out, grad_qk, grad_v, small.reshape(grid + (16, small_cols))),
-        (512, 512, 512, 256),
-        lambda number: number % 4 != 0,
-        2,
-        3,
-    )
+    final = (grad_out, grad_qk, grad_v, small.reshape(grid + (16, small_cols)))
+    cuts_of = (512, 512, 512, 256)
+    if in_kernel:
+        layer_ins = (gathered_mlp, activation, hidden_in, row_vectors[3:4])
+        grad_out, grad_qk, grad_v, small, result = scatter_and_widen(
+            final, cuts_of, lambda number: number % 4 != 0, 2, 3, layer_ins, 3
+        )
+    else:
+        grad_out, grad_qk, grad_v, small = scatter_all(
+            final, cuts_of, lambda number: number % 4 != 0, 2, 3
+        )
+    layer_out = result.reshape(inputs.shape)
     small = small.reshape(-1)[:packed_size]
     wide_own = small[: cuts[0]].reshape(len(wide), -1)
     narrow_own = small[cuts[1] : cuts[2]].reshape(len(narrow), -1)

time: 465 us -> 464 us (level)
    pallas_call x1, Pallas kernels: 151 us -> 146 us  [gather_and_attend(): pl.pallas_call(functools.partial(attend_kernel, plan, count, spacing, fir...]
    unnamed x115 -> x117, local copies, waits for them, and re-layouts: 13.8 us -> 15.1 us
where the time goes in v6:
time: 464 us; the launch traced here: 456 us
  Pallas kernels  374 us (81%)
  local copies, waits for them, and re-layouts  32.6 us (7%)
  matrix products  29.7 us (6%)
  other arithmetic  17.9 us (4%)
    pallas_call x1, Pallas kernels, gather_and_attend(): pl.pallas_call(functools.partial(attend_kernel, plan, count, spacing, fir...  146 us
    pallas_call x1, Pallas kernels, scatter_and_attend_back(): pl.pallas_call(functools.partial(attend_back_kernel, plan, arrays, spacin...  111 us
    pallas_call x1, Pallas kernels, scatter_and_widen(): pl.pallas_call(functools.partial(scatter_and_widen_kernel, plan, arrays,...  69.5 us
    pallas_call x1, Pallas kernels, gather_all(): pl.pallas_call(functools.partial(gather_kernel, plan, len(shards), spacin...  47 us
    unnamed x117, local copies, waits for them, and re-layouts  15.1 us

profile of v6, /device:TPU:0, one launch (start us, length us, event | category | flops | bytes accessed | tf_op | source)
XLA Modules:
  0.0 456.3 jit_solution(5500932120298431690)
XLA Ops:
  3.4 47.0 %shard_map.313 = (bf16[4,2,2,2,16,256]{5,4,3,2,1,0:T(8,128)(2,1)}, bf16[4,2,2,2,48,1024]{5,4,3,2,1,0:T(8,128)(2,1)}, bf16[4,2,2,2,48,1536]{5,4,3,2,1,0:T(8,128)(2,1)}) custom-call(bf16[16,256]{1,0:T(8,128)(2,1)} %reshape.351.refs_0_, bf16[48,1024]{1,0:T(8,128)(2,1)} %pad_maximum_fusion.refs_1_, bf16[48,1536]{1,0:T(8,128)(2,1)} %refs_2_.2), custom_call_target="tpu_custom_call" | custom-call | tf_op jit(solution)/shard_map/pallas_call | solution.py:317
  50.4 1.0 copy.87
  51.9 1.2 convolution_convert_fusion.refs_4_.refs_6_
  55.4 4.5 fusion.34
  60.3 1.3 add_convert_fusion.2
  62.5 1.2 slice.168
  64.1 4.4 convolution_convert_fusion.2
  69.3 0.8 copy.71
  70.1 1.6 maximum_bitcast_fusion.refs_3_
  72.5 0.8 slice_convert_fusion.2
  74.0 146.4 %shard_map.314 = (bf16[4,2,2,2,48,1536]{5,4,3,2,1,0:T(8,128)(2,1)}, bf16[4,2,2,2,96,1536]{5,4,3,2,1,0:T(8,128)(2,1)}, bf16[4,2,2,2,48,3072]{5,4,3,2,1,0:T(8,128)...) custom-call(bf16[48,1536]{1,0:T(8,128)(2,1)} %refs_0_.1, ...), custom_call_target="tpu_custom_call" | custom-call | tf_op jit(solution)/shard_map/pallas_call | solution.py:541
  220.4 2.0 reduce_sum.134
  223.2 8.3 %multiply_reduce_fusion = (bf16[1536]{0:T(1024)(128)(2,1)}, f32[384]{0:T(512)S(1)}, bf16[1536]{0:T(1024)(128)(2,1)}, f32[384,1536]{1,0:T(8,128)S(1)}) fusion(f32[384,1536]{1,0:T(8,128)S(1)} %copy-done, f32[384]{0:T(512)S(1)} %fusion.27, f32[384]{0:T(512)S(1)} %broadcast_multiply_fusion, f32[1536]{0:T(1024)S(1)} %mul.222, ...), kind=kOutput, calls=%fused_computation.26 | convolution fusion | flops 3628593664 | bytes 16531968 | tf_op jit(solution)/shard_map/tf,df->td/dot_general | solution.py:1110
  232.8 1.0 fusion.39
  233.9 4.8 %convolution_convert_fusion.1 = bf16[384,1536]{1,0:T(8,128)(2,1)S(1)} fusion(bf16[384,1536]{1,0:T(8,128)(2,1)S(1)} %get-tuple-element.77.refs_1_, bf16[1536,1536]{1,0:T(8,128)(2,1)} %bitcast.116), kind=kOutput, calls=%fused_computation.10 | convolution fusion | flops 1812529152 | bytes 7077888 | tf_op jit(solution)/shard_map/te,de->td/dot_general | solution.py:1117
  239.4 1.5 copy.74
  240.9 111.3 %shard_map.315 = (f32[96,1536]{1,0:T(8,128)}, f32[48,3072]{1,0:T(8,128)}, bf16[4,384,640]{2,1,0:T(8,128)(2,1)}, f32[128,3072]{1,0:T(8,128)}, f32[8,128]{1,0:T(8,128)}) custom-call(bf16[384,3072]{1,0:T(8,128)(2,1)} %get-tuple-element.50.refs_0_.refs_8_, bf16[384,1536]{1,0:T(8,128)(2,1)} %bitcast.78, bf16[384,1536]{1,0:T(8,128)(2,1)} %get-tuple-element.51.refs_2_, ...), custom_call_target="tpu_custom_call" | custom-call | tf_op jit(solution)/shard_map/pallas_call | solution.py:958
  352.2 1.3 slice_bitcast_fusion.1
  354.3 1.4 fusion.48
  356.6 1.2 copy-done.4
  357.9 2.3 fusion.10
  360.3 1.3 copy-done.6
  361.6 1.1 fusion.36
  363.7 2.8 convolution_dynamic-update-slice_fusion
  367.7 2.1 reduce.2
  370.2 0.8 copy.88
  370.9 4.3 add_bitcast_fusion
  375.9 69.5 %shard_map.316 = (f32[48,1536]{1,0:T(8,128)}, f32[48,1024]{1,0:T(8,128)}, f32[48,1536]{1,0:T(8,128)}, f32[16,256]{1,0:T(8,128)}, bf16[384,1536]{1,0:T(8,128)(2,1)}) custom-call(bf16[384,1536]{1,0:T(8,128)(2,1)} %get-tuple-element.46.refs_0_, bf16[384,1536]{1,0:T(8,128)(2,1)} %copy-done.7, bf16[384,1536]{1,0:T(8,128)(2,1)} %get-tuple-element.88.refs_2_.refs_4_, ...), custom_call_target="tpu_custom_call" | custom-call | tf_op jit(solution)/shard_map/pallas_call | solution.py:850
  445.4 1.7 fusion.44
  450.4 2.4 copy.105
  454.2 0.8 copy.108
  455.1 0.8 copy.109
  (192 shorter events, 21.4 us)
Async XLA Ops:
  0.7 1.9 copy-start.38
  0.7 1.9 copy-start.39
  1.5 51.6 %copy-start.22 = (bf16[3071,32]{0,1:T(8,128)(2,1)}, bf16[3071,32]{0,1:T(8,128)(2,1)S(1)}, u32[]{:S(2)}) copy-start(bf16[3071,32]{0,1:T(8,128)(2,1)S(1)} %get-tuple-element.103) | copy-start | bytes 589636
  1.5 51.6 %copy-start.23 = (bf16[3071,32]{0,1:T(8,128)(2,1)}, bf16[3071,32]{0,1:T(8,128)(2,1)S(1)}, u32[]{:S(2)}) copy-start(bf16[3071,32]{0,1:T(8,128)(2,1)S(1)} %get-tuple-element.108) | copy-start | bytes 589636
  1.6 51.5 %copy-start.20 = (bf16[3071,32]{0,1:T(8,128)(2,1)}, bf16[3071,32]{0,1:T(8,128)(2,1)S(1)}, u32[]{:S(2)}) copy-start(bf16[3071,32]{0,1:T(8,128)(2,1)S(1)} %get-tuple-element.105) | copy-start | bytes 589636
  1.7 51.4 %copy-start.12 = (bf16[3071,96]{0,1:T(8,128)(2,1)}, bf16[3071,96]{0,1:T(8,128)(2,1)S(1)}, u32[]{:S(2)}) copy-start(bf16[3071,96]{0,1:T(8,128)(2,1)S(1)} %fusion.20) | copy-start | bytes 1768900
  51.4 8.5 %copy-start.11 = (bf16[4,8,16,256]{3,1,2,0:T(8,128)(2,1)}, bf16[4,8,16,256]{3,1,2,0:T(8,128)(2,1)S(1)}, u32[]{:S(2)}) copy-start(bf16[4,8,16,256]{3,1,2,0:T(8,128)(2,1)S(1)} %copy.87) | copy-start | bytes 786436
  51.9 2.3 copy-start.3
  53.2 6.6 %copy-start.16 = (f32[32,6,48]{2,1,0:T(8,128)}, f32[32,6,48]{2,1,0:T(8,128)S(1)}, u32[]{:S(2)}) copy-start(f32[32,6,48]{2,1,0:T(8,128)S(1)} %reshape.378) | copy-start | bytes 110596
  54.1 5.7 %copy-start.28 = (f32[1536]{0:T(1024)}, f32[1536]{0:T(1024)S(1)}, u32[]{:S(2)}) copy-start(f32[1536]{0:T(1024)S(1)} %add.133) | copy-start | bytes 18436
  220.4 2.4 copy-start
  220.4 2.7 copy-start.25
  233.9 4.8 %copy-start.7 = (bf16[384,1536]{1,0:T(8,128)(2,1)}, bf16[384,1536]{1,0:T(8,128)(2,1)S(1)}, u32[]{:S(2)}) copy-start(bf16[384,1536]{1,0:T(8,128)(2,1)S(1)} %get-tuple-element.77.refs_1_) | copy-start | bytes 3538948
  352.1 2.2 copy-start.47
  352.1 4.5 slice-start
  354.3 2.1 copy-start.9
  354.3 2.4 slice-start.1
  356.6 3.6 copy-start.8
  357.9 2.3 copy-start.33
  360.2 3.0 copy-start.2
  360.2 2.7 copy-start.34
  360.2 2.8 copy-start.37
  360.3 2.9 copy-start.36
  361.6 2.1 copy-start.13
  361.6 2.1 copy-start.21
  366.5 4.4 copy-start.29
  366.5 4.4 copy-start.31
  370.9 4.3 copy-start.24
  445.4 7.4 %copy-start.19 = (f32[48,1536]{1,0:T(8,128)S(1)}, f32[48,1536]{1,0:T(8,128)}, u32[]{:S(2)}) copy-start(f32[48,1536]{1,0:T(8,128)} %get-tuple-element.140) | copy-start | bytes 884740
  445.4 8.1 %copy-start.18 = (f32[48,1536]{1,0:T(8,128)S(1)}, f32[48,1536]{1,0:T(8,128)}, u32[]{:S(2)}) copy-start(f32[48,1536]{1,0:T(8,128)} %get-tuple-element.144) | copy-start | bytes 884740
  445.4 8.8 %copy-start.15 = (f32[48,3072]{1,0:T(8,128)S(1)}, f32[48,3072]{1,0:T(8,128)}, u32[]{:S(2)}) copy-start(f32[48,3072]{1,0:T(8,128)} %get-tuple-element.148) | copy-start | bytes 1769476
  450.4 4.7 %copy-start.14 = (f32[96,1536]{1,0:T(8,128)S(1)}, f32[96,1536]{1,0:T(8,128)}, u32[]{:S(2)}) copy-start(f32[96,1536]{1,0:T(8,128)} %get-tuple-element.150) | copy-start | bytes 1769476
  (18 other events, 28.3 us)

commit v7 on v6

--- a/solution.py
+++ b/solution.py
@@ -575,7 +575,7 @@
     own_seq = {bit: (seq >> bit) & 1 for bit in range(bits)}
 
     def add(target, source):
-        target[...] = (target[...].astype(single) + source[...].astype(single)).astype(bfloat)
+        target[...] = target[...] + source[...]
 
     def slabs(chunk, chip, bit_index, lead=0, span=None):
         which, slot, _ = chunk

time: 464 us -> 464 us (level)
  no operation moved by 1% of the time
where the time goes in v7:
time: 464 us; the launch traced here: 457 us
  Pallas kernels  374 us (81%)
  local copies, waits for them, and re-layouts  32.6 us (7%)
  matrix products  29.7 us (6%)
  other arithmetic  17.9 us (4%)
    pallas_call x1, Pallas kernels, gather_and_attend(): pl.pallas_call(functools.partial(attend_kernel, plan, count, spacing, fir...  146 us
    pallas_call x1, Pallas kernels, scatter_and_attend_back(): pl.pallas_call(functools.partial(attend_back_kernel, plan, arrays, spacin...  111 us
    pallas_call x1, Pallas kernels, scatter_and_widen(): pl.pallas_call(functools.partial(scatter_and_widen_kernel, plan, arrays,...  69.7 us
    pallas_call x1, Pallas kernels, gather_all(): pl.pallas_call(functools.partial(gather_kernel, plan, len(shards), spacin...  47 us
    unnamed x117, local copies, waits for them, and re-layouts  15.1 us

profile of v7, /device:TPU:0, one launch (start us, length us, event | category | flops | bytes accessed | tf_op | source)
XLA Modules:
  0.0 456.7 jit_solution(17566695044177847627)
XLA Ops:
  3.4 47.0 %shard_map.313 = (bf16[4,2,2,2,16,256]{5,4,3,2,1,0:T(8,128)(2,1)}, bf16[4,2,2,2,48,1024]{5,4,3,2,1,0:T(8,128)(2,1)}, bf16[4,2,2,2,48,1536]{5,4,3,2,1,0:T(8,128)(2,1)}) custom-call(bf16[16,256]{1,0:T(8,128)(2,1)} %reshape.351.refs_0_, bf16[48,1024]{1,0:T(8,128)(2,1)} %pad_maximum_fusion.refs_1_, bf16[48,1536]{1,0:T(8,128)(2,1)} %refs_2_.2), custom_call_target="tpu_custom_call" | custom-call | tf_op jit(solution)/shard_map/pallas_call | solution.py:317
  50.4 1.0 copy.87
  51.9 1.2 convolution_convert_fusion.refs_4_.refs_6_
  55.4 4.5 fusion.34
  60.3 1.3 add_convert_fusion.2
  62.5 1.2 slice.168
  64.1 4.4 convolution_convert_fusion.2
  69.3 0.8 copy.71
  70.1 1.6 maximum_bitcast_fusion.refs_3_
  72.5 0.8 slice_convert_fusion.2
  74.0 146.4 %shard_map.314 = (bf16[4,2,2,2,48,1536]{5,4,3,2,1,0:T(8,128)(2,1)}, bf16[4,2,2,2,96,1536]{5,4,3,2,1,0:T(8,128)(2,1)}, bf16[4,2,2,2,48,3072]{5,4,3,2,1,0:T(8,128)...) custom-call(bf16[48,1536]{1,0:T(8,128)(2,1)} %refs_0_.1, ...), custom_call_target="tpu_custom_call" | custom-call | tf_op jit(solution)/shard_map/pallas_call | solution.py:541
  220.4 2.0 reduce_sum.134
  223.2 8.3 %multiply_reduce_fusion = (bf16[1536]{0:T(1024)(128)(2,1)}, f32[384]{0:T(512)S(1)}, bf16[1536]{0:T(1024)(128)(2,1)}, f32[384,1536]{1,0:T(8,128)S(1)}) fusion(f32[384,1536]{1,0:T(8,128)S(1)} %copy-done, f32[384]{0:T(512)S(1)} %fusion.27, f32[384]{0:T(512)S(1)} %broadcast_multiply_fusion, f32[1536]{0:T(1024)S(1)} %mul.222, ...), kind=kOutput, calls=%fused_computation.26 | convolution fusion | flops 3628593664 | bytes 16531968 | tf_op jit(solution)/shard_map/tf,df->td/dot_general | solution.py:1110
  232.8 1.0 fusion.39
  233.9 4.8 %convolution_convert_fusion.1 = bf16[384,1536]{1,0:T(8,128)(2,1)S(1)} fusion(bf16[384,1536]{1,0:T(8,128)(2,1)S(1)} %get-tuple-element.77.refs_1_, bf16[1536,1536]{1,0:T(8,128)(2,1)} %bitcast.116), kind=kOutput, calls=%fused_computation.10 | convolution fusion | flops 1812529152 | bytes 7077888 | tf_op jit(solution)/shard_map/te,de->td/dot_general | solution.py:1117
  239.4 1.5 copy.74
  240.9 111.3 %shard_map.315 = (f32[96,1536]{1,0:T(8,128)}, f32[48,3072]{1,0:T(8,128)}, bf16[4,384,640]{2,1,0:T(8,128)(2,1)}, f32[128,3072]{1,0:T(8,128)}, f32[8,128]{1,0:T(8,128)}) custom-call(bf16[384,3072]{1,0:T(8,128)(2,1)} %get-tuple-element.50.refs_0_.refs_8_, bf16[384,1536]{1,0:T(8,128)(2,1)} %bitcast.78, bf16[384,1536]{1,0:T(8,128)(2,1)} %get-tuple-element.51.refs_2_, ...), custom_call_target="tpu_custom_call" | custom-call | tf_op jit(solution)/shard_map/pallas_call | solution.py:958
  352.3 1.3 slice_bitcast_fusion.1
  354.4 1.4 fusion.48
  356.7 1.2 copy-done.4
  358.0 2.3 fusion.10
  360.4 1.3 copy-done.6
  361.7 1.1 fusion.36
  363.8 2.8 convolution_dynamic-update-slice_fusion
  367.8 2.1 reduce.2
  370.3 0.8 copy.88
  371.0 4.3 add_bitcast_fusion
  376.0 69.7 %shard_map.316 = (f32[48,1536]{1,0:T(8,128)}, f32[48,1024]{1,0:T(8,128)}, f32[48,1536]{1,0:T(8,128)}, f32[16,256]{1,0:T(8,128)}, bf16[384,1536]{1,0:T(8,128)(2,1)}) custom-call(bf16[384,1536]{1,0:T(8,128)(2,1)} %get-tuple-element.46.refs_0_, bf16[384,1536]{1,0:T(8,128)(2,1)} %copy-done.7, bf16[384,1536]{1,0:T(8,128)(2,1)} %get-tuple-element.88.refs_2_.refs_4_, ...), custom_call_target="tpu_custom_call" | custom-call | tf_op jit(solution)/shard_map/pallas_call | solution.py:850
  445.7 1.7 fusion.44
  450.7 2.4 copy.105
  454.5 0.8 copy.108
  455.3 0.8 copy.109
  (192 shorter events, 21.4 us)
Async XLA Ops:
  0.7 1.9 copy-start.38
  0.7 1.9 copy-start.39
  1.5 51.6 %copy-start.22 = (bf16[3071,32]{0,1:T(8,128)(2,1)}, bf16[3071,32]{0,1:T(8,128)(2,1)S(1)}, u32[]{:S(2)}) copy-start(bf16[3071,32]{0,1:T(8,128)(2,1)S(1)} %get-tuple-element.103) | copy-start | bytes 589636
  1.5 51.6 %copy-start.23 = (bf16[3071,32]{0,1:T(8,128)(2,1)}, bf16[3071,32]{0,1:T(8,128)(2,1)S(1)}, u32[]{:S(2)}) copy-start(bf16[3071,32]{0,1:T(8,128)(2,1)S(1)} %get-tuple-element.108) | copy-start | bytes 589636
  1.6 51.5 %copy-start.20 = (bf16[3071,32]{0,1:T(8,128)(2,1)}, bf16[3071,32]{0,1:T(8,128)(2,1)S(1)}, u32[]{:S(2)}) copy-start(bf16[3071,32]{0,1:T(8,128)(2,1)S(1)} %get-tuple-element.105) | copy-start | bytes 589636
  1.7 51.4 %copy-start.12 = (bf16[3071,96]{0,1:T(8,128)(2,1)}, bf16[3071,96]{0,1:T(8,128)(2,1)S(1)}, u32[]{:S(2)}) copy-start(bf16[3071,96]{0,1:T(8,128)(2,1)S(1)} %fusion.20) | copy-start | bytes 1768900
  51.4 8.5 %copy-start.11 = (bf16[4,8,16,256]{3,1,2,0:T(8,128)(2,1)}, bf16[4,8,16,256]{3,1,2,0:T(8,128)(2,1)S(1)}, u32[]{:S(2)}) copy-start(bf16[4,8,16,256]{3,1,2,0:T(8,128)(2,1)S(1)} %copy.87) | copy-start | bytes 786436
  51.9 2.3 copy-start.3
  53.2 6.6 %copy-start.16 = (f32[32,6,48]{2,1,0:T(8,128)}, f32[32,6,48]{2,1,0:T(8,128)S(1)}, u32[]{:S(2)}) copy-start(f32[32,6,48]{2,1,0:T(8,128)S(1)} %reshape.378) | copy-start | bytes 110596
  54.1 5.7 %copy-start.28 = (f32[1536]{0:T(1024)}, f32[1536]{0:T(1024)S(1)}, u32[]{:S(2)}) copy-start(f32[1536]{0:T(1024)S(1)} %add.133) | copy-start | bytes 18436
  220.4 2.4 copy-start
  220.4 2.7 copy-start.25
  233.9 4.8 %copy-start.7 = (bf16[384,1536]{1,0:T(8,128)(2,1)}, bf16[384,1536]{1,0:T(8,128)(2,1)S(1)}, u32[]{:S(2)}) copy-start(bf16[384,1536]{1,0:T(8,128)(2,1)S(1)} %get-tuple-element.77.refs_1_) | copy-start | bytes 3538948
  352.2 2.2 copy-start.47
  352.2 4.5 slice-start
  354.4 2.1 copy-start.9
  354.4 2.4 slice-start.1
  356.7 3.6 copy-start.8
  358.0 2.3 copy-start.33
  360.3 3.0 copy-start.2
  360.3 2.7 copy-start.34
  360.3 2.8 copy-start.37
  360.4 2.9 copy-start.36
  361.7 2.1 copy-start.13
  361.7 2.1 copy-start.21
  366.6 4.4 copy-start.29
  366.6 4.4 copy-start.31
  371.0 4.3 copy-start.24
  445.7 7.4 %copy-start.19 = (f32[48,1536]{1,0:T(8,128)S(1)}, f32[48,1536]{1,0:T(8,128)}, u32[]{:S(2)}) copy-start(f32[48,1536]{1,0:T(8,128)} %get-tuple-element.140) | copy-start | bytes 884740
  445.7 8.1 %copy-start.18 = (f32[48,1536]{1,0:T(8,128)S(1)}, f32[48,1536]{1,0:T(8,128)}, u32[]{:S(2)}) copy-start(f32[48,1536]{1,0:T(8,128)} %get-tuple-element.144) | copy-start | bytes 884740
  445.7 8.8 %copy-start.15 = (f32[48,3072]{1,0:T(8,128)S(1)}, f32[48,3072]{1,0:T(8,128)}, u32[]{:S(2)}) copy-start(f32[48,3072]{1,0:T(8,128)} %get-tuple-element.148) | copy-start | bytes 1769476
  450.7 4.7 %copy-start.14 = (f32[96,1536]{1,0:T(8,128)S(1)}, f32[96,1536]{1,0:T(8,128)}, u32[]{:S(2)}) copy-start(f32[96,1536]{1,0:T(8,128)} %get-tuple-element.150) | copy-start | bytes 1769476
  (18 other events, 28.3 us)
